TPU v7x, 128 devices: a whole 4x4x4 slice. The times are simulated.
128 devices in a mesh: tm: 4 (over y_lo, core), space: 32 (over y_hi, z, x).
Axes of the slice: x: 4, y: 4 (y_hi: 2, y_lo: 2; y = y_hi * 2 + y_lo), z: 4, core: 2. Of those that a mesh axis runs over, the one named last changes fastest.
Arguments:
- space_query: bfloat16 [1, 16, 1024, 4096], P(None, 'tm', 'space'), may hold values from -28 to 28
- space_key: bfloat16 [1, 16, 1024, 4096], P(None, 'tm', 'space'), may hold values from -28 to 28
- space_value: bfloat16 [1, 16, 1024, 4096], P(None, 'tm', 'space'), may hold values from -6 to 6
- space_grad: bfloat16 [1, 16, 1024, 4096], P(None, 'tm', 'space'), may hold values from -6 to 6
- time_query: bfloat16 [1, 16, 1024, 4096], P(None, 'tm', 'space'), may hold values from -28 to 28
- time_key: bfloat16 [1, 16, 1024, 4096], P(None, 'tm', 'space'), may hold values from -28 to 28
- time_value: bfloat16 [1, 16, 1024, 4096], P(None, 'tm', 'space'), may hold values from -6 to 6
- time_grad: bfloat16 [1, 16, 1024, 4096], P(None, 'tm', 'space'), may hold values from -6 to 6
Outputs:
- space_dquery: bfloat16 [1, 16, 1024, 4096], P(None, 'tm', 'space')
- space_dkey: bfloat16 [1, 16, 1024, 4096], P(None, 'tm', 'space')
- space_dvalue: bfloat16 [1, 16, 1024, 4096], P(None, 'tm', 'space')
- time_dquery: bfloat16 [1, 16, 1024, 4096], P(None, 'tm', 'space')
- time_dkey: bfloat16 [1, 16, 1024, 4096], P(None, 'tm', 'space')
- time_dvalue: bfloat16 [1, 16, 1024, 4096], P(None, 'tm', 'space')
All inputs are finite; a program needn't handle non-finite values.
Results may differ from a plain program's by a relative error of at most 0.02.
Values may be sent and summed in bfloat16 or wider, within the bound.
No kernel may reach another device: no remote copies, remote signals or barrier semaphores. Data moves between devices by JAX's collectives and lax.ppermute only.
A program may use at most 128 MiB of HBM per device.

v0:
```python
import math

import jax
import jax.numpy as jnp
from jax import lax
from jax.sharding import PartitionSpec as P

HEAD_DIM = 128


def spatial_grads(query_rows, key_rows, value_rows, grad_rows):
    clip_count, frame_count, positions, width = query_rows.shape
    head_count = width // HEAD_DIM
    shape_heads = (clip_count * frame_count, positions, head_count, HEAD_DIM)
    queries = query_rows.reshape(shape_heads)
    keyset = key_rows.reshape(shape_heads)
    valueset = value_rows.reshape(shape_heads)
    gradset = grad_rows.reshape(shape_heads)
    score_scale = 1.0 / math.sqrt(HEAD_DIM)
    block_rows = min(512, positions)
    block_count = positions // block_rows

    def spatial_step(block_index, running):
        dquery_all, dkey_sum, dvalue_sum = running
        row_start = block_index * block_rows
        query_block = lax.dynamic_slice_in_dim(queries, row_start, block_rows, 1)
        grad_block = lax.dynamic_slice_in_dim(gradset, row_start, block_rows, 1)
        scores = (
            jnp.einsum("bqhd,bkhd->bhqk", query_block, keyset, preferred_element_type=jnp.float32)
            * score_scale
        )
        row_peak = jnp.max(scores, axis=-1, keepdims=True)
        exponent = jnp.exp(scores - row_peak)
        probs = exponent / jnp.sum(exponent, axis=-1, keepdims=True)
        weights_low = probs.astype(jnp.bfloat16)
        output = jnp.einsum(
            "bhqk,bkhd->bqhd", weights_low, valueset, preferred_element_type=jnp.float32
        )
        row_delta = jnp.sum(grad_block.astype(jnp.float32) * output, axis=-1)
        prob_grad = jnp.einsum(
            "bqhd,bkhd->bhqk", grad_block, valueset, preferred_element_type=jnp.float32
        )
        score_grad = (probs * (prob_grad - jnp.transpose(row_delta, (0, 2, 1))[..., None])).astype(
            jnp.bfloat16
        )
        dquery_block = (
            jnp.einsum("bhqk,bkhd->bqhd", score_grad, keyset, preferred_element_type=jnp.float32)
            * score_scale
        )
        dkey_sum = dkey_sum + jnp.einsum(
            "bhqk,bqhd->bkhd", score_grad, query_block, preferred_element_type=jnp.float32
        )
        dvalue_sum = dvalue_sum + jnp.einsum(
            "bhqk,bqhd->bkhd", weights_low, grad_block, preferred_element_type=jnp.float32
        )
        dquery_all = lax.dynamic_update_slice_in_dim(dquery_all, dquery_block, row_start, 1)
        return (dquery_all, dkey_sum, dvalue_sum)

    zeros_full = jnp.zeros(shape_heads, jnp.float32)
    dquery_all, dkey_sum, dvalue_sum = lax.fori_loop(
        0, block_count, spatial_step, (zeros_full, zeros_full, zeros_full)
    )
    out_shape = (clip_count, frame_count, positions, width)
    return (
        dquery_all.reshape(out_shape),
        (dkey_sum * score_scale).reshape(out_shape),
        dvalue_sum.reshape(out_shape),
    )


def temporal_grads(query_rows, key_rows, value_rows, grad_rows, offset):
    clip_count, query_frames, positions, width = query_rows.shape
    key_frames = key_rows.shape[1]
    row_count = positions * (width // HEAD_DIM)
    queries = query_rows.reshape(clip_count, query_frames, row_count, HEAD_DIM).astype(jnp.float32)
    keyset = key_rows.reshape(clip_count, key_frames, row_count, HEAD_DIM).astype(jnp.float32)
    valueset = value_rows.reshape(clip_count, key_frames, row_count, HEAD_DIM).astype(jnp.float32)
    gradset = grad_rows.reshape(clip_count, query_frames, row_count, HEAD_DIM).astype(jnp.float32)
    score_scale = 1.0 / math.sqrt(HEAD_DIM)
    scores = jnp.sum(queries[:, :, None] * keyset[:, None], axis=-1) * score_scale
    frame_query = lax.broadcasted_iota(jnp.int32, (query_frames, key_frames, 1), 0) + offset
    frame_key = lax.broadcasted_iota(jnp.int32, (query_frames, key_frames, 1), 1)
    allowed = frame_key <= frame_query
    scores = jnp.where(allowed, scores, jnp.float32(-1e30))
    row_peak = jnp.max(scores, axis=2, keepdims=True)
    exponent = jnp.where(allowed, jnp.exp(scores - row_peak), jnp.float32(0.0))
    probs = exponent / jnp.sum(exponent, axis=2, keepdims=True)
    weights_low = probs.astype(jnp.bfloat16).astype(jnp.float32)
    output = jnp.sum(weights_low[..., None] * valueset[:, None], axis=2)
    row_delta = jnp.sum(gradset * output, axis=-1)
    prob_grad = jnp.sum(gradset[:, :, None] * valueset[:, None], axis=-1)
    score_grad = (
        (probs * (prob_grad - row_delta[:, :, None])).astype(jnp.bfloat16).astype(jnp.float32)
    )
    dquery = jnp.sum(score_grad[..., None] * keyset[:, None], axis=2) * score_scale
    dkey = jnp.sum(score_grad[..., None] * queries[:, :, None], axis=1) * score_scale
    dvalue = jnp.sum(weights_low[..., None] * gradset[:, :, None], axis=1)
    query_shape = (clip_count, query_frames, positions, width)
    key_shape = (clip_count, key_frames, positions, width)
    return (dquery.reshape(query_shape), dkey.reshape(key_shape), dvalue.reshape(key_shape))


def local(
    space_query, space_key, space_value, space_grad, time_query, time_key, time_value, time_grad
):
    dquery, dkey, dvalue = spatial_grads(
        lax.all_to_all(space_query, "space", split_axis=3, concat_axis=2, tiled=True),
        lax.all_to_all(space_key, "space", split_axis=3, concat_axis=2, tiled=True),
        lax.all_to_all(space_value, "space", split_axis=3, concat_axis=2, tiled=True),
        lax.all_to_all(space_grad, "space", split_axis=3, concat_axis=2, tiled=True),
    )
    space_dquery = lax.all_to_all(
        dquery.astype(jnp.bfloat16), "space", split_axis=2, concat_axis=3, tiled=True
    )
    space_dkey = lax.all_to_all(
        dkey.astype(jnp.bfloat16), "space", split_axis=2, concat_axis=3, tiled=True
    )
    space_dvalue = lax.all_to_all(
        dvalue.astype(jnp.bfloat16), "space", split_axis=2, concat_axis=3, tiled=True
    )
    keys_whole, values_whole = (
        lax.all_gather(time_key, "tm", axis=1, tiled=True),
        lax.all_gather(time_value, "tm", axis=1, tiled=True),
    )
    offset = lax.axis_index("tm") * time_query.shape[1]
    dquery, dkey_terms, dvalue_terms = temporal_grads(
        time_query, keys_whole, values_whole, time_grad, offset
    )
    dkey_own, dvalue_own = (
        lax.psum_scatter(
            dkey_terms.astype(jnp.bfloat16), "tm", scatter_dimension=1, tiled=True
        ).astype(jnp.float32),
        lax.psum_scatter(
            dvalue_terms.astype(jnp.bfloat16), "tm", scatter_dimension=1, tiled=True
        ).astype(jnp.float32),
    )
    time_dquery = dquery.astype(jnp.bfloat16)
    time_dkey = dkey_own.astype(jnp.bfloat16)
    time_dvalue = dvalue_own.astype(jnp.bfloat16)
    return (space_dquery, space_dkey, space_dvalue, time_dquery, time_dkey, time_dvalue)


def solution(mesh):
    return jax.shard_map(
        local,
        mesh=mesh,
        in_specs=(
            P(None, "tm", "space", None),
            P(None, "tm", "space", None),
            P(None, "tm", "space", None),
            P(None, "tm", "space", None),
            P(None, "tm", "space", None),
            P(None, "tm", "space", None),
            P(None, "tm", "space", None),
            P(None, "tm", "space", None),
        ),
        out_specs=(
            P(None, "tm", "space", None),
            P(None, "tm", "space", None),
            P(None, "tm", "space", None),
            P(None, "tm", "space", None),
            P(None, "tm", "space", None),
            P(None, "tm", "space", None),
        ),
        check_vma=False,
    )
```

profile of v0, /device:TPU:0, one launch (start us, length us, event | category | flops | bytes accessed | tf_op | source)
XLA Modules:
  0.0 469.9 jit_solution(6721976901847294972)
XLA Ops:
  11.8 46.3 %all-gather.3.cloned.1.call-done = bf16[1,16,32,4096]{3,2,0,1:T(8,128)(2,1)} async-done(((bf16[1,4,32,4096]{3,2,0,1:T(8,128)(2,1)}), bf16[1,16,32,4096]{3,2,0,1:T(8,128)(2,1)}) %all-gather.3.cloned.1.call-update) | async-done | bytes 4194320 | tf_op jit(solution)/shard_map/all_gather | solution.py:122
  58.2 7.8 %reshape.384 = f32[16,1024,128]{2,1,0:T(8,128)} reshape(bf16[1,16,32,4096]{3,2,0,1:T(8,128)(2,1)} %all-gather.3.cloned.1.call-done) | data formatting | bytes 12582912 | tf_op jit(solution)/shard_map/convert_element_type | solution.py:76
  66.0 11.3 %multiply_reduce_fusion.6 = f32[4,16,1024]{2,1,0:T(8,128)S(1)} fusion(f32[16,1024,128]{2,1,0:T(8,128)} %reshape.384, f32[4,1024,128]{2,1,0:T(8,128)} %reshape.383), kind=kLoop, calls=%fused_computation.38 | loop fusion | flops 16711680 | bytes 10747904 | tf_op jit(solution)/shard_map/reduce_sum | solution.py:80
  77.5 29.8 %all-gather.5.cloned.1.call-done = bf16[1,16,32,4096]{3,2,0,1:T(8,128)(2,1)} async-done(((bf16[1,4,32,4096]{3,2,0,1:T(8,128)(2,1)}), bf16[1,16,32,4096]{3,2,0,1:T(8,128)(2,1)}) %all-gather.5.cloned.1.call-update) | async-done | bytes 4194320 | tf_op jit(solution)/shard_map/all_gather | solution.py:123
  107.3 7.9 %reshape.386 = f32[16,1024,128]{2,1,0:T(8,128)} reshape(bf16[1,16,32,4096]{3,2,0,1:T(8,128)(2,1)} %all-gather.5.cloned.1.call-done) | data formatting | bytes 12582912 | tf_op jit(solution)/shard_map/convert_element_type | solution.py:77
  115.2 23.6 %multiply_reduce_fusion.4 = (f32[4,1024,128]{2,1,0:T(8,128)}, f32[4,16,1024]{2,1,0:T(8,128)S(1)}, bf16[16,1024,128]{2,1,0:T(8,128)(2,1)}) fusion(f32[4,16,1024]{2,1,0:T(8,128)S(1)} %get-tuple-element.232, f32[16,1024,128]{2,1,0:T(8,128)} %reshape.386, f32[4,1024,128]{2,1,0:T(8,128)S(1)} %reshape.385), kind=kLoop, calls=%fused_computation.36 | loop fusion | flops 47644672 | bytes 17301504 | tf_op jit(solution)/shard_map/reduce_sum | solution.py:89
  141.0 16.3 %multiply_reduce_fusion.2 = (f32[16,1024,128]{2,1,0:T(8,128)}, f32[4,1024,128]{2,1,0:T(8,128)}) fusion(f32[4,16,1024]{2,1,0:T(8,128)S(1)} %fusion.30, f32[4,1024,128]{2,1,0:T(8,128)} %reshape.383, f32[16,1024,128]{2,1,0:T(8,128)} %reshape.384), kind=kLoop, calls=%fused_computation.34 | loop fusion | flops 30932992 | bytes 21233664 | tf_op jit(solution)/shard_map/reduce_sum | solution.py:96
  157.3 6.5 %multiply_convert_fusion.1 = bf16[16,1024,128]{2,1,0:T(8,128)(2,1)} fusion(f32[16,1024,128]{2,1,0:T(8,128)} %get-tuple-element.212), kind=kLoop, calls=%fused_computation.39 | loop fusion | flops 4194304 | bytes 12582912 | tf_op jit(solution)/shard_map/convert_element_type | solution.py:131
  163.8 7.3 %convert_element_type.222 = bf16[1,16,32,4096]{3,2,1,0:T(8,128)(2,1)} reshape(bf16[16,1024,128]{2,1,0:T(8,128)(2,1)} %multiply_convert_fusion.1) | data formatting | bytes 8388608 | tf_op jit(solution)/shard_map/convert_element_type | solution.py:131
  172.3 4.7 copy.88
  177.0 7.9 %reshape.397 = bf16[32,2,8192]{2,1,0:T(2,128)(2,1)} reshape(bf16[4096,1,4,32]{3,2,1,0:T(4,128)(2,1)} %bitcast.150) | data formatting | bytes 2097152
  184.8 9.6 %all-to-all-start.3 = ((bf16[32,2,8192]{2,1,0:T(2,128)(2,1)}), bf16[32,2,8192]{2,1,0:T(2,128)(2,1)S(1)}, u32[]{:S(2)}, u32[]{:S(2)}) async-start(bf16[32,2,8192]{2,1,0:T(2,128)(2,1)} %reshape.397), calls=%async_computation.3 | async-start | bytes 2097152 | tf_op jit(solution)/shard_map/all_to_all | solution.py:109
  194.4 4.7 %copy.81 = bf16[1,4,32,4096]{2,1,0,3:T(4,128)(2,1)} copy(bf16[1,4,32,4096]{3,2,1,0:T(8,128)(2,1)S(1)} %copy-done.14) | data formatting | bytes 2097152 | tf_op args[0]
  199.1 7.7 %reshape.391 = bf16[32,2,8192]{2,1,0:T(2,128)(2,1)} reshape(bf16[4096,1,4,32]{3,2,1,0:T(4,128)(2,1)} %bitcast.151) | data formatting | bytes 2097152
  206.9 7.3 %all-to-all-done.3 = bf16[32,2,8192]{2,1,0:T(2,128)(2,1)S(1)} async-done(((bf16[32,2,8192]{2,1,0:T(2,128)(2,1)}), bf16[32,2,8192]{2,1,0:T(2,128)(2,1)S(1)}, u32[]{:S(2)}, u32[]{:S(2)}) %all-to-all-start.3) | async-done | bytes 1048608 | tf_op jit(solution)/shard_map/all_to_all | solution.py:109
  214.2 6.0 %all-to-all-start = ((bf16[32,2,8192]{2,1,0:T(2,128)(2,1)}), bf16[32,2,8192]{2,1,0:T(2,128)(2,1)S(1)}, u32[]{:S(2)}, u32[]{:S(2)}) async-start(bf16[32,2,8192]{2,1,0:T(2,128)(2,1)} %reshape.391), calls=%async_computation | async-start | bytes 2097152 | tf_op jit(solution)/shard_map/all_to_all | solution.py:107
  220.2 4.7 %copy.83 = bf16[1,4,32,4096]{2,1,0,3:T(4,128)(2,1)} copy(bf16[1,4,32,4096]{3,2,1,0:T(8,128)(2,1)S(1)} %copy-done.15) | data formatting | bytes 2097152 | tf_op args[1]
  224.9 7.7 %reshape.393 = bf16[32,2,8192]{2,1,0:T(2,128)(2,1)} reshape(bf16[4096,1,4,32]{3,2,1,0:T(4,128)(2,1)} %bitcast.152) | data formatting | bytes 2097152
  232.6 7.3 %all-to-all-done = bf16[32,2,8192]{2,1,0:T(2,128)(2,1)S(1)} async-done(((bf16[32,2,8192]{2,1,0:T(2,128)(2,1)}), bf16[32,2,8192]{2,1,0:T(2,128)(2,1)S(1)}, u32[]{:S(2)}, u32[]{:S(2)}) %all-to-all-start) | async-done | bytes 1048608 | tf_op jit(solution)/shard_map/all_to_all | solution.py:107
  239.9 5.5 %all-to-all-start.1 = ((bf16[32,2,8192]{2,1,0:T(2,128)(2,1)}), bf16[32,2,8192]{2,1,0:T(2,128)(2,1)S(1)}, u32[]{:S(2)}, u32[]{:S(2)}) async-start(bf16[32,2,8192]{2,1,0:T(2,128)(2,1)} %reshape.393), calls=%async_computation.1 | async-start | bytes 2097152 | tf_op jit(solution)/shard_map/all_to_all | solution.py:108
  245.4 6.1 %copy.85 = bf16[1,4,32,4096]{2,1,0,3:T(4,128)(2,1)} copy(bf16[1,4,32,4096]{3,2,1,0:T(8,128)(2,1)} %param.13) | data formatting | bytes 2097152 | tf_op args[3]
  251.5 7.7 %reshape.395 = bf16[32,2,8192]{2,1,0:T(2,128)(2,1)} reshape(bf16[4096,1,4,32]{3,2,1,0:T(4,128)(2,1)} %bitcast.153) | data formatting | bytes 2097152
  259.2 4.1 all-to-all-done.1
  263.3 5.9 %all-to-all-start.2 = ((bf16[32,2,8192]{2,1,0:T(2,128)(2,1)}), bf16[32,2,8192]{2,1,0:T(2,128)(2,1)}, u32[]{:S(2)}, u32[]{:S(2)}) async-start(bf16[32,2,8192]{2,1,0:T(2,128)(2,1)} %reshape.395), calls=%async_computation.2 | async-start | bytes 2097152 | tf_op jit(solution)/shard_map/all_to_all | solution.py:110
  269.2 3.5 reshape.398
  272.8 6.4 %copy.109 = bf16[1,4,32,32,128]{4,2,3,1,0:T(8,128)(2,1)} copy(bf16[1,4,32,32,128]{2,1,4,3,0:T(4,128)(2,1)} %bitcast.146) | data formatting | bytes 2097152 | tf_op jit(solution)/shard_map/all_to_all | solution.py:109
  281.5 3.5 reshape.392
  285.0 6.4 %copy.82 = bf16[1,4,32,32,128]{4,3,2,1,0:T(8,128)(2,1)} copy(bf16[1,4,32,32,128]{3,1,4,2,0:T(4,128)(2,1)} %bitcast.147) | data formatting | bytes 2097152 | tf_op jit(solution)/shard_map/all_to_all | solution.py:107
  291.4 3.5 reshape.394
  294.9 6.3 %copy.84 = bf16[1,4,32,32,128]{4,3,2,1,0:T(8,128)(2,1)} copy(bf16[1,4,32,32,128]{3,1,4,2,0:T(4,128)(2,1)} %bitcast.148) | data formatting | bytes 2097152 | tf_op jit(solution)/shard_map/all_to_all | solution.py:108
  301.2 7.4 %reshape.396 = bf16[4096,1,4,32]{3,2,1,0:T(4,128)(2,1)} reshape(bf16[32,2,8192]{2,1,0:T(2,128)(2,1)} %all-to-all-done.2) | data formatting | bytes 2097152
  308.6 6.3 %copy.107 = bf16[1,4,32,32,128]{4,2,3,1,0:T(8,128)(2,1)} copy(bf16[1,4,32,32,128]{2,1,4,3,0:T(4,128)(2,1)} %bitcast.149) | data formatting | bytes 2097152 | tf_op jit(solution)/shard_map/all_to_all | solution.py:110
  314.9 7.3 %convert_element_type.224 = bf16[1,16,32,4096]{3,2,1,0:T(8,128)(2,1)} reshape(bf16[16,1024,128]{2,1,0:T(8,128)(2,1)} %get-tuple-element.211) | data formatting | bytes 8388608 | tf_op jit(solution)/shard_map/convert_element_type | solution.py:134
  323.4 61.4 %while.18 = (s32[]{:T(128)}, bf16[4,1024,1,128]{3,0,1,2:T(4,128)(2,1)}, f32[4,1024,1,128]{1,3,0,2:T(8,128)S(1)}, f32[4,1024,1,128]{1,3,0,2:T(8,128)}, bf16[4,102...) while((s32[]{:T(128)}, ...), condition=%wide.region_4.0_spmd.clone, body=%wide.region_0.0_spmd.clone.sunk | while | flops 3245603840 | bytes 169910672 | solution.py:60
  330.9 2.7 copy-done
  333.9 4.1 fusion.79
  338.0 5.6 %multiply_convert_fusion.6 = bf16[4,512,1024]{2,1,0:T(8,128)(2,1)} fusion(f32[4,512]{1,0:T(4,128)S(1)} %fusion.79, f32[4,512,1024]{2,1,0:T(8,128)} %copy-done, f32[4,512]{1,0:T(4,128)S(1)} %get-tuple-element.286, bf16[4,1024,1,128]{1,3,0,2:T(8,128)(2,1)S(1)} %copy-done.16, bf16[4,512,1,128]{3,1,0,2:T(8,128)(2,1)S(1)} %constant_dynamic-slice_fusion.2), kind=kOutput, calls=%fused_computation.1.clone.1 | convolution fusion | flops 545259520 | bytes 14172160 | tf_op jit(solution)/shard_map/while/body/eval_jaxpr/bqhd,bkhd->bhqk/dot_general | solution.py:40
  343.6 3.7 bitcast_add_fusion.4
  363.5 4.1 fusion.79
  367.6 5.6 %multiply_convert_fusion.6 = bf16[4,512,1024]{2,1,0:T(8,128)(2,1)} fusion(f32[4,512]{1,0:T(4,128)S(1)} %fusion.79, f32[4,512,1024]{2,1,0:T(8,128)} %copy-done, f32[4,512]{1,0:T(4,128)S(1)} %get-tuple-element.286, bf16[4,1024,1,128]{1,3,0,2:T(8,128)(2,1)S(1)} %copy-done.16, bf16[4,512,1,128]{3,1,0,2:T(8,128)(2,1)S(1)} %constant_dynamic-slice_fusion.2), kind=kOutput, calls=%fused_computation.1.clone.1 | convolution fusion | flops 545259520 | bytes 14172160 | tf_op jit(solution)/shard_map/while/body/eval_jaxpr/bqhd,bkhd->bhqk/dot_general | solution.py:40
  373.2 3.7 bitcast_add_fusion.4
  376.9 2.6 fusion.80
  381.0 3.8 bitcast_add_fusion.5
  388.0 9.9 %all-to-all-start.6 = ((bf16[1,4,1024,128]{3,1,0,2:T(4,128)(2,1)}), bf16[1,4,1024,128]{3,1,0,2:T(4,128)(2,1)}, u32[]{:S(2)}, u32[]{:S(2)}) async-start(bf16[1,4,1024,128]{3,1,0,2:T(4,128)(2,1)} %bitcast.158), calls=%async_computation.6 | async-start | bytes 2097152 | tf_op jit(solution)/shard_map/all_to_all | solution.py:118
  398.9 15.9 %all-to-all-done.6 = bf16[1,4,1024,128]{3,1,0,2:T(4,128)(2,1)} async-done(((bf16[1,4,1024,128]{3,1,0,2:T(4,128)(2,1)}), bf16[1,4,1024,128]{3,1,0,2:T(4,128)(2,1)}, u32[]{:S(2)}, u32[]{:S(2)}) %all-to-all-start.6) | async-done | bytes 1048608 | tf_op jit(solution)/shard_map/all_to_all | solution.py:118
  414.9 21.5 %all_to_all.114 = bf16[1,4,1024,128]{3,1,0,2:T(4,128)(2,1)} all-to-all(bf16[1,4,1024,128]{3,1,0,2:T(4,128)(2,1)S(1)} %bitcast.159), channel_id=1, replica_groups=mesh['tm'=4,'space'=32] {'space'}, dimensions={2} | all-to-all | bytes 2097152 | tf_op jit(solution)/shard_map/all_to_all | solution.py:115
  436.3 4.6 all-to-all-start.4
  445.0 12.9 %all-to-all-done.4 = bf16[1,4,1024,128]{3,1,0,2:T(4,128)(2,1)S(1)} async-done(((bf16[1,4,1024,128]{3,1,0,2:T(4,128)(2,1)}), bf16[1,4,1024,128]{3,1,0,2:T(4,128)(2,1)S(1)}, u32[]{:S(2)}, u32[]{:S(2)}) %all-to-all-start.4) | async-done | bytes 1048608 | tf_op jit(solution)/shard_map/all_to_all | solution.py:112
  (95 shorter events, 50.7 us)
Async XLA Ops:
  7.2 4.1 copy-start.12
  7.2 51.0 %all-gather.3.cloned.1.call-start = ((), (), s32[]{:S(2)}) async-start(), calls=%async_computation.9 | async-start | bytes 5242880 | tf_op jit(solution)/shard_map/all_gather | solution.py:122
  7.9 99.4 %all-gather.5.cloned.1.call-start = ((), (), s32[]{:S(2)}) async-start(), calls=%async_computation.10 | async-start | bytes 5242880 | tf_op jit(solution)/shard_map/all_gather | solution.py:123
  8.7 454.7 %reduce-scatter.3.cloned.1.call-start = ((), (), s32[]{:S(2)}) async-start(), calls=%async_computation.11 | async-start | bytes 5242880 | tf_op jit(solution)/shard_map/reduce_scatter | solution.py:130
  171.0 1.2 copy-start.13
  177.0 17.5 %copy-start.14 = (bf16[1,4,32,4096]{3,2,1,0:T(8,128)(2,1)S(1)}, bf16[1,4,32,4096]{3,2,1,0:T(8,128)(2,1)}, u32[]{:S(2)}) copy-start(bf16[1,4,32,4096]{3,2,1,0:T(8,128)(2,1)} %param.10) | copy-start | bytes 3145732
  184.8 29.4 %all-to-all-start.3 = ((bf16[32,2,8192]{2,1,0:T(2,128)(2,1)}), bf16[32,2,8192]{2,1,0:T(2,128)(2,1)S(1)}, u32[]{:S(2)}, u32[]{:S(2)}) async-start(bf16[32,2,8192]{2,1,0:T(2,128)(2,1)} %reshape.397), calls=%async_computation.3 | async-start | bytes 2097152 | tf_op jit(solution)/shard_map/all_to_all | solution.py:109
  199.1 21.1 %copy-start.15 = (bf16[1,4,32,4096]{3,2,1,0:T(8,128)(2,1)S(1)}, bf16[1,4,32,4096]{3,2,1,0:T(8,128)(2,1)}, u32[]{:S(2)}) copy-start(bf16[1,4,32,4096]{3,2,1,0:T(8,128)(2,1)} %param.11) | copy-start | bytes 3145732
  214.2 25.6 %all-to-all-start = ((bf16[32,2,8192]{2,1,0:T(2,128)(2,1)}), bf16[32,2,8192]{2,1,0:T(2,128)(2,1)S(1)}, u32[]{:S(2)}, u32[]{:S(2)}) async-start(bf16[32,2,8192]{2,1,0:T(2,128)(2,1)} %reshape.391), calls=%async_computation | async-start | bytes 2097152 | tf_op jit(solution)/shard_map/all_to_all | solution.py:107
  239.9 19.3 %copy-start.5 = (bf16[32,2,8192]{2,1,0:T(2,128)(2,1)}, bf16[32,2,8192]{2,1,0:T(2,128)(2,1)S(1)}, u32[]{:S(2)}) copy-start(bf16[32,2,8192]{2,1,0:T(2,128)(2,1)S(1)} %all-to-all-done) | copy-start | bytes 3145732
  239.9 23.4 %all-to-all-start.1 = ((bf16[32,2,8192]{2,1,0:T(2,128)(2,1)}), bf16[32,2,8192]{2,1,0:T(2,128)(2,1)S(1)}, u32[]{:S(2)}, u32[]{:S(2)}) async-start(bf16[32,2,8192]{2,1,0:T(2,128)(2,1)} %reshape.393), calls=%async_computation.1 | async-start | bytes 2097152 | tf_op jit(solution)/shard_map/all_to_all | solution.py:108
  263.3 5.9 %copy-start.7 = (bf16[32,2,8192]{2,1,0:T(2,128)(2,1)}, bf16[32,2,8192]{2,1,0:T(2,128)(2,1)S(1)}, u32[]{:S(2)}) copy-start(bf16[32,2,8192]{2,1,0:T(2,128)(2,1)S(1)} %all-to-all-done.1) | copy-start | bytes 3145732
  263.3 37.9 %all-to-all-start.2 = ((bf16[32,2,8192]{2,1,0:T(2,128)(2,1)}), bf16[32,2,8192]{2,1,0:T(2,128)(2,1)}, u32[]{:S(2)}, u32[]{:S(2)}) async-start(bf16[32,2,8192]{2,1,0:T(2,128)(2,1)} %reshape.395), calls=%async_computation.2 | async-start | bytes 2097152 | tf_op jit(solution)/shard_map/all_to_all | solution.py:110
  269.2 194.2 %reduce-scatter.5.cloned.1.call-start = ((), (), s32[]{:S(2)}) async-start(), calls=%async_computation.12 | async-start | bytes 5242880 | tf_op jit(solution)/shard_map/reduce_scatter | solution.py:133
  272.8 8.7 %copy-start.6 = (bf16[32,2,8192]{2,1,0:T(2,128)(2,1)S(1)}, bf16[32,2,8192]{2,1,0:T(2,128)(2,1)}, u32[]{:S(2)}) copy-start(bf16[32,2,8192]{2,1,0:T(2,128)(2,1)} %copy-done.5) | copy-start | bytes 3145732
  285.0 6.4 %copy-start.8 = (bf16[32,2,8192]{2,1,0:T(2,128)(2,1)S(1)}, bf16[32,2,8192]{2,1,0:T(2,128)(2,1)}, u32[]{:S(2)}) copy-start(bf16[32,2,8192]{2,1,0:T(2,128)(2,1)} %copy-done.7) | copy-start | bytes 3145732
  328.4 5.2 %copy-start = (f32[4,512,1024]{2,1,0:T(8,128)}, f32[4,512,1024]{2,1,0:T(8,128)S(1)}, u32[]{:S(2)}) copy-start(f32[4,512,1024]{2,1,0:T(8,128)S(1)} %get-tuple-element.285) | copy-start | bytes 25165828 | tf_op jit(solution)/shard_map/while
  328.4 5.2 %copy-start.3 = (bf16[4,1024,1,128]{3,1,0,2:T(8,128)(2,1)S(1)}, bf16[4,1024,1,128]{3,1,0,2:T(8,128)(2,1)}, u32[]{:S(2)}) copy-start(bf16[4,1024,1,128]{3,1,0,2:T(8,128)(2,1)} %get-tuple-element.317) | copy-start | bytes 3145732 | tf_op jit(solution)/shard_map/while
  333.9 4.1 copy-start.16
  343.6 3.7 copy-start.2
  347.3 2.7 copy-start.10
  347.3 4.1 copy-start.1
  350.4 1.0 copy-start.11
  358.6 4.6 copy-start
  358.6 4.6 copy-start.3
  363.4 4.1 copy-start.16
  373.2 3.7 copy-start.2
  376.9 2.7 copy-start.10
  376.9 4.1 copy-start.1
  380.0 1.0 copy-start.11
  388.0 26.8 %all-to-all-start.6 = ((bf16[1,4,1024,128]{3,1,0,2:T(4,128)(2,1)}), bf16[1,4,1024,128]{3,1,0,2:T(4,128)(2,1)}, u32[]{:S(2)}, u32[]{:S(2)}) async-start(bf16[1,4,1024,128]{3,1,0,2:T(4,128)(2,1)} %bitcast.158), calls=%async_computation.6 | async-start | bytes 2097152 | tf_op jit(solution)/shard_map/all_to_all | solution.py:118
  436.3 21.6 %all-to-all-start.4 = ((bf16[1,4,1024,128]{3,1,0,2:T(4,128)(2,1)}), bf16[1,4,1024,128]{3,1,0,2:T(4,128)(2,1)S(1)}, u32[]{:S(2)}, u32[]{:S(2)}) async-start(bf16[1,4,1024,128]{3,1,0,2:T(4,128)(2,1)} %bitcast.157), calls=%async_computation.4 | async-start | bytes 2097152 | tf_op jit(solution)/shard_map/all_to_all | solution.py:112
  440.9 2.7 copy-start.9
  443.6 18.2 %copy-start.4 = (f32[4,1024,128]{2,1,0:T(8,128)S(1)}, f32[4,1024,128]{2,1,0:T(8,128)}, u32[]{:S(2)}) copy-start(f32[4,1024,128]{2,1,0:T(8,128)} %get-tuple-element.213) | copy-start | bytes 6291460
Sparse Core Ops, SparseCore 0:
  9.7 48.4 all-gather.2
  59.8 47.4 all-gather.4
  171.2 69.1 reduce-scatter.2
  322.3 46.6 reduce-scatter.4
where the time goes:
time: 473 us; the launch traced here: 470 us
  local copies, waits for them, and re-layouts  152 us (32%)
  waiting for transfers between devices  125 us (26%)
  other arithmetic  72 us (15%)
  matrix products  43.4 us (9%)
  starting transfers between devices  41.5 us (9%)
  blocking collectives  21.5 us (5%)
  between operations  14 us (3%)
    unnamed x35, local copies, waits for them, and re-layouts  74.9 us
    all_gather x1, waiting for transfers between devices, local(): lax.all_gather(time_key, 'tm', axis=1, tiled=True)  46.3 us
    all_gather x1, waiting for transfers between devices, local(): lax.all_gather(time_value, 'tm', axis=1, tiled=True)  29.8 us
    reduce_sum x1, other arithmetic, temporal_grads(): output = jnp.sum(weights_low[..., None] * valueset[:, None], axis=2)  23.6 us
    all_to_all x1, blocking collectives, local(): lax.all_to_all(dkey.astype(jnp.bfloat16), 'space', split_axis=2, concat_a...  21.5 us
    reduce_sum x1, other arithmetic, temporal_grads(): jnp.sum(score_grad[..., None] * queries[:, :, None], axis=1) * score_scale  16.3 us
    all_to_all x1, waiting for transfers between devices, local(): lax.all_to_all(dvalue.astype(jnp.bfloat16), 'space', split_axis=2, concat...  15.9 us
    all_to_all x1, waiting for transfers between devices, local(): lax.all_to_all(dquery.astype(jnp.bfloat16), 'space', split_axis=2, concat...  12.9 us
  transfers between devices with their start and end apart: 10, of which 7 were waited for; matrix products, arithmetic and copies ran while one was open for 41% of the time, Pallas kernels for 0%

commit v1 on v0

v1 whole, which is shorter than its diff:
```python
import functools
import math

import jax
import jax.numpy as jnp
from jax import lax
from jax.experimental import pallas as pl
from jax.experimental.pallas import tpu as pltpu
from jax.sharding import PartitionSpec as P

HEAD_DIM = 128
SCALE = 1.0 / math.sqrt(HEAD_DIM)
LOG2E = 1.0 / math.log(2.0)


def dot(a, b, contract):
    return lax.dot_general(a, b, (contract, ((), ())), preferred_element_type=jnp.float32)


def pack_kernel(*refs):
    *ins, out = refs
    heads = out.shape[0]
    for a, ref in enumerate(ins):
        for h in range(heads):
            out[h, 0, a] = ref[0, :, h * HEAD_DIM : (h + 1) * HEAD_DIM]


def pack_heads(*arrays):
    frames, positions, width = arrays[0].shape
    heads = width // HEAD_DIM
    count = len(arrays)
    return pl.pallas_call(
        pack_kernel,
        grid=(frames,),
        in_specs=[pl.BlockSpec((1, positions, width), lambda f: (f, 0, 0))] * count,
        out_specs=pl.BlockSpec(
            (heads, 1, count, positions, HEAD_DIM), lambda f: (0, f, 0, 0, 0)
        ),
        out_shape=jax.ShapeDtypeStruct(
            (heads, frames, count, positions, HEAD_DIM), arrays[0].dtype
        ),
        name="pack_heads",
    )(*arrays)


def unpack_kernel(ref, *outs):
    heads = ref.shape[0]
    for a, out in enumerate(outs):
        for h in range(heads):
            out[0, :, h * HEAD_DIM : (h + 1) * HEAD_DIM] = ref[h, 0, a]


def unpack_heads(array):
    heads, frames, count, positions, _ = array.shape
    width = heads * HEAD_DIM
    return pl.pallas_call(
        unpack_kernel,
        grid=(frames,),
        in_specs=[
            pl.BlockSpec((heads, 1, count, positions, HEAD_DIM), lambda f: (0, f, 0, 0, 0))
        ],
        out_specs=[pl.BlockSpec((1, positions, width), lambda f: (f, 0, 0))] * count,
        out_shape=[jax.ShapeDtypeStruct((frames, positions, width), array.dtype)] * count,
        name="unpack_heads",
    )(array)


def spatial_kernel(block, ref, out):
    parts, _, _, rows, _ = ref.shape
    total = parts * rows
    query, key, value, grad = (ref[:, 0, a].reshape(total, HEAD_DIM) for a in range(4))
    key_t = key.T
    dkey = dvalue = None
    for start in range(0, total, block):
        q = query[start : start + block]
        g = grad[start : start + block]
        scores = dot(key, q, ((1,), (1,)))
        peak = jnp.max(scores, axis=0, keepdims=True)
        e = jnp.exp2((scores - peak) * (SCALE * LOG2E))
        pgrad = dot(value, g, ((1,), (1,)))
        probs = e * (1.0 / jnp.sum(e, axis=0, keepdims=True))
        weights = probs.astype(jnp.bfloat16)
        term = probs * pgrad
        delta = jnp.sum(term, axis=0, keepdims=True)
        sgrad = (term - probs * delta).astype(jnp.bfloat16)
        dq = dot(key_t, sgrad, ((1,), (0,))).T * SCALE
        out[start // rows : (start + block) // rows, 0, 0] = dq.astype(out.dtype).reshape(
            block // rows, rows, HEAD_DIM
        )
        dk = dot(sgrad, q, ((1,), (0,)))
        dv = dot(weights, g, ((1,), (0,)))
        dkey = dk if dkey is None else dkey + dk
        dvalue = dv if dvalue is None else dvalue + dv
    out[:, 0, 1] = (dkey * SCALE).astype(out.dtype).reshape(parts, rows, HEAD_DIM)
    out[:, 0, 2] = dvalue.astype(out.dtype).reshape(parts, rows, HEAD_DIM)


def spatial_grads(array):
    parts, frames, _, rows, _ = array.shape
    return pl.pallas_call(
        functools.partial(spatial_kernel, min(256, parts * rows)),
        grid=(frames,),
        in_specs=[pl.BlockSpec((parts, 1, 4, rows, HEAD_DIM), lambda f: (0, f, 0, 0, 0))],
        out_specs=pl.BlockSpec((parts, 1, 3, rows, HEAD_DIM), lambda f: (0, f, 0, 0, 0)),
        out_shape=jax.ShapeDtypeStruct((parts, frames, 3, rows, HEAD_DIM), array.dtype),
        compiler_params=pltpu.CompilerParams(vmem_limit_bytes=48 * 1024 * 1024),
        name="spatial_grads",
    )(array)


GROUP = 16
NEVER = -1e30


def ship_kernel(query, key, value, grad, same, other, sems):
    member = lax.axis_index("tm")
    chip, core = member // 2, member % 2
    width = same.shape[-1]

    def copy_all(first, second, row):
        copies = []
        for half, out in ((core, same), (1 - core, other)):
            columns = pl.ds(pl.multiple_of(half * width, width), width)
            for a, ref in enumerate((first, second)):
                copies.append(
                    pltpu.make_async_copy(
                        ref.at[:, pl.ds(row, GROUP), columns], out.at[a], sems.at[len(copies)]
                    )
                )
        for copy in copies:
            copy.start()
        for copy in copies:
            copy.wait()

    @pl.when(chip == 0)
    def _():
        copy_all(key, value, 0)

    @pl.when(chip == 1)
    def _():
        copy_all(query, grad, GROUP)


def ship_pack(query, key, value, grad):
    frames, _, width = query.shape
    shape = jax.ShapeDtypeStruct((2, frames, GROUP, width // 2), query.dtype)
    return pl.pallas_call(
        ship_kernel,
        in_specs=[pl.BlockSpec(memory_space=pl.ANY)] * 4,
        out_specs=[pl.BlockSpec(memory_space=pl.ANY)] * 2,
        out_shape=[shape, shape],
        scratch_shapes=[pltpu.SemaphoreType.DMA((4,))],
        name="ship_pack",
    )(query, key, value, grad)


def swap_kernel(*refs):
    *ins, out, sems = refs
    core = lax.axis_index("tm") % 2
    width = out.shape[-1]
    columns = pl.ds(pl.multiple_of((1 - core) * width, width), width)
    copies = [
        pltpu.make_async_copy(ref.at[:, :, columns], out.at[a], sems.at[a])
        for a, ref in enumerate(ins)
    ]
    for copy in copies:
        copy.start()
    for copy in copies:
        copy.wait()


def swap_pack(*arrays):
    frames, positions, width = arrays[0].shape
    count = len(arrays)
    return pl.pallas_call(
        swap_kernel,
        in_specs=[pl.BlockSpec(memory_space=pl.ANY)] * count,
        out_specs=pl.BlockSpec(memory_space=pl.ANY),
        out_shape=jax.ShapeDtypeStruct((count, frames, positions, width // 2), arrays[0].dtype),
        scratch_shapes=[pltpu.SemaphoreType.DMA((count,))],
        name="swap_pack",
    )(*arrays)


def frame_mask(core, chip_frames, causal):
    rows = chip_frames * GROUP
    half = chip_frames // 2
    key_row = lax.broadcasted_iota(jnp.int32, (rows, rows), 0)
    query_row = lax.broadcasted_iota(jnp.int32, (rows, rows), 1)
    same = key_row % GROUP == query_row % GROUP
    key_frame = (key_row // GROUP + core * half) % chip_frames
    query_frame = (query_row // GROUP + core * half) % chip_frames
    return same & ((key_frame <= query_frame) | jnp.logical_not(causal))


def gather_rows(own, other, row, columns):
    rows = pl.ds(row, GROUP)
    return jnp.concatenate(
        [
            own[:, rows, columns].reshape(-1, HEAD_DIM),
            other[:, rows, columns].reshape(-1, HEAD_DIM),
        ],
        axis=0,
    )


def block_stats(mask, query, key, value, grad):
    scores = dot(key, query, ((1,), (1,))) * (SCALE * LOG2E)
    scores = jnp.where(mask, scores, NEVER)
    peak = jnp.max(scores, axis=0, keepdims=True)
    e = jnp.exp2(scores - peak)
    pgrad = dot(value, grad, ((1,), (1,)))
    return (
        (scores, pgrad),
        (peak, jnp.sum(e, axis=0, keepdims=True), jnp.sum(e * pgrad, axis=0, keepdims=True)),
    )


def block_grads(products, stats, more, query, key, grad):
    scores, pgrad = products
    peak = jnp.maximum(stats[0], more[0])
    own_scale, more_scale = jnp.exp2(stats[0] - peak), jnp.exp2(more[0] - peak)
    inverse = 1.0 / (stats[1] * own_scale + more[1] * more_scale)
    delta = (stats[2] * own_scale + more[2] * more_scale) * inverse
    probs = jnp.exp2(scores - peak) * inverse
    weights = probs.astype(jnp.bfloat16)
    sgrad = (probs * (pgrad - delta)).astype(jnp.bfloat16)
    dquery = dot(sgrad, key, ((0,), (0,))) * SCALE
    dkey = dot(sgrad, query, ((1,), (0,))) * SCALE
    dvalue = dot(weights, grad, ((1,), (0,)))
    return dquery, dkey, dvalue


def stats_kernel(place, query, key, value, grad, swapped, same, other, out):
    core, chip = place[0], place[1]
    frames = query.shape[0]
    mask = frame_mask(core, 2 * frames, chip == 1)
    for h in range(query.shape[-1] // HEAD_DIM):
        columns = pl.ds(h * HEAD_DIM, HEAD_DIM)
        own = [
            gather_rows(ref, swapped.at[a], GROUP, columns)
            for a, ref in enumerate((query, key, value, grad))
        ]
        sent = [gather_rows(same.at[a], other.at[a], 0, columns) for a in range(2)]
        q = jnp.where(chip == 0, sent[0], own[0])
        g = jnp.where(chip == 0, sent[1], own[3])
        _, stats = block_stats(mask, q, own[1], own[2], g)
        out[h] = jnp.concatenate(stats + (jnp.zeros((5, stats[0].shape[1]), jnp.float32),), axis=0)


def grads_kernel(
    place, query, key, value, grad, swapped, same, other, far, mine, theirs, back, back_other
):
    core, chip = place[0], place[1]
    frames = query.shape[0]
    causal = frame_mask(core, 2 * frames, True)
    cross = frame_mask(core, 2 * frames, False)
    first = chip == 0
    for h in range(query.shape[-1] // HEAD_DIM):
        columns = pl.ds(h * HEAD_DIM, HEAD_DIM)
        early, late = (
            [
                gather_rows(ref, swapped.at[a], row, columns)
                for a, ref in enumerate((query, key, value, grad))
            ]
            for row in (0, GROUP)
        )
        sent = [gather_rows(same.at[a], other.at[a], 0, columns) for a in range(2)]
        crossed = [
            jnp.where(first, sent[0], early[0]),
            jnp.where(first, late[1], sent[0]),
            jnp.where(first, late[2], sent[1]),
            jnp.where(first, sent[1], early[3]),
        ]
        received = tuple(far[h, i : i + 1] for i in range(3))
        none = (
            jnp.full_like(received[0], NEVER),
            jnp.zeros_like(received[1]),
            jnp.zeros_like(received[2]),
        )
        early_products, early_stats = block_stats(causal, *early)
        late_products, late_stats = block_stats(causal, *late)
        cross_products, cross_stats = block_stats(cross, *crossed)

        def choose(when_first, when_second):
            return tuple(jnp.where(first, a, b) for a, b in zip(when_first, when_second))

        early_out = block_grads(
            early_products, early_stats, choose(none, cross_stats), early[0], early[1], early[3]
        )
        late_out = block_grads(
            late_products, late_stats, choose(none, received), late[0], late[1], late[3]
        )
        cross_out = block_grads(
            cross_products,
            cross_stats,
            choose(received, early_stats),
            crossed[0],
            crossed[1],
            crossed[3],
        )
        zero = jnp.zeros_like(cross_out[0])
        early_out = (early_out[0] + jnp.where(first, zero, cross_out[0]),) + early_out[1:]
        late_out = (late_out[0],) + tuple(
            a + jnp.where(first, b, zero) for a, b in zip(late_out[1:], cross_out[1:])
        )
        back_out = (
            jnp.where(first, cross_out[0], cross_out[1]),
            jnp.where(first, zero, cross_out[2]),
        )

        def place_rows(own, others, a, row, values):
            values = values.astype(jnp.bfloat16).reshape(2, frames, GROUP, HEAD_DIM)
            own[a, :, pl.ds(row, GROUP), columns] = values[0]
            others[a, :, pl.ds(row, GROUP), columns] = values[1]

        for a in range(3):
            place_rows(mine, theirs, a, 0, early_out[a])
            place_rows(mine, theirs, a, GROUP, late_out[a])
        for a in range(2):
            place_rows(back, back_other, a, 0, back_out[a])


def finish_kernel(place, mine, swapped, back, back_swapped, dquery, dkey, dvalue):
    first = place[1] == 0

    def write(ref, far):
        early, late = pl.ds(0, GROUP), pl.ds(GROUP, GROUP)
        zero = jnp.zeros(far.shape[1:], jnp.float32)
        far_first, far_second = far[0].astype(jnp.float32), far[1].astype(jnp.float32)

        def added(a, rows, more):
            return (ref[a, :, rows].astype(jnp.float32) + more).astype(jnp.bfloat16)

        dquery[:, early] = ref[0, :, early]
        dquery[:, late] = added(0, late, jnp.where(first, zero, far_first))
        dkey[:, early] = added(1, early, jnp.where(first, far_first, zero))
        dkey[:, late] = ref[1, :, late]
        dvalue[:, early] = added(2, early, jnp.where(first, far_second, zero))
        dvalue[:, late] = ref[2, :, late]

    @pl.when(pl.program_id(0) == 0)
    def _():
        write(mine, back)

    @pl.when(pl.program_id(0) == 1)
    def _():
        write(swapped, back_swapped)


STEPS = 4


def temporal_grads(query, key, value, grad):
    frames, positions, width = query.shape
    half = width // 2
    block = half // STEPS
    heads = half // HEAD_DIM
    step_heads = heads // STEPS
    member = lax.axis_index("tm")
    place = jnp.stack([member % 2, member // 2])
    chips = [(t, t ^ 2) for t in range(4)]
    cores = [(t, t ^ 1) for t in range(4)]
    arrays = (query, key, value, grad)

    ship_same, ship_other = ship_pack(*arrays)
    ship_other = lax.ppermute(ship_other, "tm", chips)
    ship_same = lax.ppermute(ship_same, "tm", chips)
    swapped = lax.ppermute(swap_pack(*arrays), "tm", cores)
    ship_other = lax.ppermute(ship_other, "tm", cores)

    own_spec = pl.BlockSpec((frames, positions, block), lambda j, p: (0, 0, p[0] * STEPS + j))

    def half_spec(count, rows):
        return pl.BlockSpec((count, frames, rows, block), lambda j, p: (0, 0, 0, j))

    stats_spec = pl.BlockSpec((step_heads, 8, 2 * frames * GROUP), lambda j, p: (j, 0, 0))
    inputs = [own_spec] * 4 + [half_spec(4, positions), half_spec(2, GROUP), half_spec(2, GROUP)]
    operands = arrays + (swapped, ship_same, ship_other)
    stats = pl.pallas_call(
        stats_kernel,
        grid_spec=pltpu.PrefetchScalarGridSpec(
            num_scalar_prefetch=1, grid=(STEPS,), in_specs=inputs, out_specs=stats_spec
        ),
        out_shape=jax.ShapeDtypeStruct((heads, 8, 2 * frames * GROUP), jnp.float32),
        name="temporal_stats",
    )(place, *operands)
    far = lax.ppermute(stats, "tm", chips)

    def half_shape(count, rows):
        return jax.ShapeDtypeStruct((count, frames, rows, half), query.dtype)

    mine, theirs, back, back_other = pl.pallas_call(
        grads_kernel,
        grid_spec=pltpu.PrefetchScalarGridSpec(
            num_scalar_prefetch=1,
            grid=(STEPS,),
            in_specs=inputs + [stats_spec],
            out_specs=[half_spec(3, positions)] * 2 + [half_spec(2, GROUP)] * 2,
        ),
        out_shape=[half_shape(3, positions)] * 2 + [half_shape(2, GROUP)] * 2,
        name="temporal_grads",
    )(place, *operands, far)
    return place, mine, theirs, back, back_other


def temporal_finish(place, mine, theirs, back, back_other):
    _, frames, positions, half = mine.shape
    block = half // STEPS
    chips = [(t, t ^ 2) for t in range(4)]
    cores = [(t, t ^ 1) for t in range(4)]
    back_other = lax.ppermute(back_other, "tm", chips)
    back = lax.ppermute(back, "tm", chips)
    swapped = lax.ppermute(theirs, "tm", cores)
    back_other = lax.ppermute(back_other, "tm", cores)

    def spec(which, count, rows):
        return pl.BlockSpec(
            (count, frames, rows, block),
            (lambda i, j, p: (0, 0, 0, jnp.where(i == 0, j, STEPS - 1)))
            if which == 0
            else (lambda i, j, p: (0, 0, 0, jnp.where(i == 0, 0, j))),
        )

    out_spec = pl.BlockSpec(
        (frames, positions, block),
        lambda i, j, p: (0, 0, jnp.where(i == 0, p[0], 1 - p[0]) * STEPS + j),
    )
    out_shape = jax.ShapeDtypeStruct((frames, positions, 2 * half), mine.dtype)
    return pl.pallas_call(
        finish_kernel,
        grid_spec=pltpu.PrefetchScalarGridSpec(
            num_scalar_prefetch=1,
            grid=(2, STEPS),
            in_specs=[spec(0, 3, positions), spec(1, 3, positions), spec(0, 2, GROUP), spec(1, 2, GROUP)],
            out_specs=[out_spec] * 3,
        ),
        out_shape=[out_shape] * 3,
        name="temporal_finish",
    )(place, mine, swapped, back, back_other)


def local(
    space_query, space_key, space_value, space_grad, time_query, time_key, time_value, time_grad
):
    def flat(array):
        return array.reshape(array.shape[1:])

    packed = pack_heads(*map(flat, (space_query, space_key, space_value, space_grad)))
    packed = lax.all_to_all(packed, "space", 0, 0, tiled=True)
    pieces = temporal_grads(*map(flat, (time_query, time_key, time_value, time_grad)))
    packed, pieces = lax.optimization_barrier((packed, pieces))
    packed = lax.all_to_all(spatial_grads(packed), "space", 0, 0, tiled=True)
    outs = tuple(unpack_heads(packed)) + tuple(temporal_finish(*pieces))
    return tuple(out.reshape(space_query.shape) for out in outs)


def solution(mesh):
    spec = P(None, "tm", "space", None)
    return jax.shard_map(
        local, mesh=mesh, in_specs=(spec,) * 8, out_specs=(spec,) * 6, check_vma=False
    )
```

time: 473 us -> 268 us (0.57)
  Pallas kernels: 0 us -> 150 us
  local copies, waits for them, and re-layouts: 152 us -> 4.62 us
  other arithmetic: 72 us -> 0.59 us
  waiting for transfers between devices: 125 us -> 80.8 us
  matrix products: 43.4 us -> 0 us
  blocking collectives: 21.5 us -> 0 us
  starting transfers between devices: 41.5 us -> 25.8 us
  between operations: 14 us -> 0.71 us
    pallas_call x0 -> x8, Pallas kernels: none -> 150 us  [the longest x1 64.7 us: swap_pack(): pl.pallas_call(swap_kernel, in_specs=[pl.BlockSpec(memory_space=pl.ANY)]...]
    ppermute x0 -> x9, waiting for transfers between devices: none -> 80.8 us  [the longest x1 45 us: temporal_finish(): back_other = lax.ppermute(back_other, 'tm', chips)]
    all_gather x2 -> x0, waiting for transfers between devices: 76.1 us -> none  [the longest x1 46.3 us: local(): lax.all_gather(time_key, 'tm', axis=1, tiled=True)]
    unnamed x35 -> x10, local copies, waits for them, and re-layouts: 74.9 us -> 4.62 us
    reduce_sum x4 -> x0, other arithmetic: 53.4 us -> none  [the longest x1 23.6 us: temporal_grads(): output = jnp.sum(weights_low[..., None] * valueset[:, None], axis=2)]
    all_to_all x6 -> x2, waiting for transfers between devices: 47.6 us -> 0.01 us  [the longest x1 0.01 us: local(): packed = lax.all_to_all(packed, 'space', 0, 0, tiled=True)]
    dot_general x12 -> x0, matrix products: 43.4 us -> none  [the longest x2 11.2 us: spatial_step(): jnp.einsum('bqhd,bkhd->bhqk', grad_block, valueset, preferred_element_typ...]
    convert_element_type x7 -> x0, local copies, waits for them, and re-layouts: 34.6 us -> none  [the longest x1 7.88 us: temporal_grads(): value_rows.reshape(clip_count, key_frames, row_count, HEAD_DIM)]
  transfers between devices with their start and end apart: 10 -> 11, of which waited for: 7 -> 5; matrix products, arithmetic and copies ran while one was open for 41% -> 0% of each run, Pallas kernels for 0% -> 46%
where the time goes in v1:
time: 268 us; the launch traced here: 263 us
  Pallas kernels  150 us (56%)
  waiting for transfers between devices  80.8 us (30%)
  starting transfers between devices  25.8 us (10%)
  local copies, waits for them, and re-layouts  4.62 us (2%)
    pallas_call x1, Pallas kernels, swap_pack(): pl.pallas_call(swap_kernel, in_specs=[pl.BlockSpec(memory_space=pl.ANY)]...  64.7 us
    ppermute x1, waiting for transfers between devices, temporal_finish(): back_other = lax.ppermute(back_other, 'tm', chips)  45 us
    pallas_call x1, Pallas kernels, ship_pack(): pl.pallas_call(ship_kernel, in_specs=[pl.BlockSpec(memory_space=pl.ANY)]...  32.9 us
    pallas_call x1, Pallas kernels, spatial_grads(): pl.pallas_call(functools.partial(spatial_kernel, min(256, parts * rows)),...  20.1 us
    ppermute x1, waiting for transfers between devices, temporal_grads(): ship_other = lax.ppermute(ship_other, 'tm', chips)  13 us
    all_to_all x1, starting transfers between devices, local(): packed = lax.all_to_all(packed, 'space', 0, 0, tiled=True)  11 us
    pallas_call x1, Pallas kernels, temporal_grads(): pl.pallas_call(grads_kernel, grid_spec=pltpu.PrefetchScalarGridSpec(num_s...  10.4 us
    ppermute x1, waiting for transfers between devices, temporal_grads(): ship_same = lax.ppermute(ship_same, 'tm', chips)  10.1 us
  transfers between devices with their start and end apart: 11, of which 5 were waited for; matrix products, arithmetic and copies ran while one was open for 0% of the time, Pallas kernels for 46%

profile of v1, /device:TPU:0, one launch (start us, length us, event | category | flops | bytes accessed | tf_op | source)
XLA Modules:
  0.0 262.6 jit_solution(804949085633843485)
XLA Ops:
  0.6 4.9 %pack_heads.1 = bf16[32,4,4,32,128]{4,3,2,1,0:T(8,128)(2,1)} custom-call(bf16[4,32,4096]{2,1,0:T(8,128)(2,1)} %bitcast.32, bf16[4,32,4096]{2,1,0:T(8,128)(2,1)} %bitcast.33, bf16[4,32,4096]{2,1,0:T(8,128)(2,1)} %bitcast.34, bf16[4,32,4096]{2,1,0:T(8,128)(2,1)} %bitcast.35), custom_call_target="tpu_custom_call" | custom-call | tf_op jit(solution)/shard_map/pack_heads/pallas_call | solution.py:32
  5.5 11.0 %all-to-all-start = ((bf16[32,4,4,32,128]{4,3,2,1,0:T(8,128)(2,1)}), bf16[32,4,4,32,128]{4,3,2,1,0:T(8,128)(2,1)}, u32[]{:S(2)}, u32[]{:S(2)}) async-start(bf16[32,4,4,32,128]{4,3,2,1,0:T(8,128)(2,1)} %pack_heads.1), calls=%async_computation | async-start | bytes 8388608 | tf_op jit(solution)/shard_map/all_to_all | solution.py:450
  16.6 64.7 %swap_pack.1 = bf16[4,4,32,2048]{3,2,1,0:T(8,128)(2,1)} custom-call(bf16[4,32,4096]{2,1,0:T(8,128)(2,1)} %bitcast.16, bf16[4,32,4096]{2,1,0:T(8,128)(2,1)} %bitcast.20, bf16[4,32,4096]{2,1,0:T(8,128)(2,1)} %bitcast.24, bf16[4,32,4096]{2,1,0:T(8,128)(2,1)} %bitcast.28), custom_call_target="tpu_custom_call" | custom-call | tf_op jit(solution)/shard_map/swap_pack/pallas_call | solution.py:175
  81.2 0.1 collective-permute-start
  81.3 32.9 %ship_pack.1 = (bf16[2,4,16,2048]{3,2,1,0:T(8,128)(2,1)}, bf16[2,4,16,2048]{3,2,1,0:T(8,128)(2,1)}) custom-call(bf16[4,32,4096]{2,1,0:T(8,128)(2,1)} %bitcast.17, bf16[4,32,4096]{2,1,0:T(8,128)(2,1)} %bitcast.21, bf16[4,32,4096]{2,1,0:T(8,128)(2,1)} %bitcast.25, bf16[4,32,4096]{2,1,0:T(8,128)(2,1)} %bitcast.29), custom_call_target="tpu_custom_call" | custom-call | tf_op jit(solution)/shard_map/ship_pack/pallas_call | solution.py:147
  114.3 0.8 collective-permute-start.2
  115.0 1.3 collective-permute-start.1
  116.4 13.0 %collective-permute-done.2 = bf16[2,4,16,2048]{3,2,1,0:T(8,128)(2,1)} collective-permute-done((bf16[2,4,16,2048]{3,2,1,0:T(8,128)(2,1)}, bf16[2,4,16,2048]{3,2,1,0:T(8,128)(2,1)}, u32[]{:S(2)}, u32[]{:S(2)}) %collective-permute-start.2) | collective-permute-done | bytes 524320 | tf_op jit(solution)/shard_map/ppermute | solution.py:367
  129.4 0.0 collective-permute-start.3
  129.4 0.6 pad_add_fusion.place
  130.0 10.1 %collective-permute-done.1.same = bf16[2,4,16,2048]{3,2,1,0:T(8,128)(2,1)S(1)} collective-permute-done((bf16[2,4,16,2048]{3,2,1,0:T(8,128)(2,1)}, bf16[2,4,16,2048]{3,2,1,0:T(8,128)(2,1)S(1)}, u32[]{:S(2)}, u32[]{:S(2)}) %collective-permute-start.1) | collective-permute-done | bytes 524320 | tf_op jit(solution)/shard_map/ppermute | solution.py:368
  140.1 0.0 copy-start.2
  140.1 0.0 collective-permute-done.3.other
  140.1 0.0 copy-start.3
  140.1 0.0 collective-permute-done.swapped
  140.1 0.8 copy-done.2
  140.9 0.2 copy-done.3
  141.1 0.0 copy-start.1
  141.1 1.4 copy-done.1
  142.5 5.4 %temporal_stats.1 = f32[16,8,128]{2,1,0:T(8,128)} custom-call(s32[2]{0:T(128)} %pad_add_fusion.place, bf16[4,32,4096]{2,1,0:T(8,128)(2,1)} %bitcast.18, bf16[4,32,4096]{2,1,0:T(8,128)(2,1)} %bitcast.22, bf16[4,32,4096]{2,1,0:T(8,128)(2,1)} %bitcast.26, bf16[4,32,4096]{2,1,0:T(8,128)(2,1)} %bitcast.30, bf16[4,4,32,2048]{3,2,1,0:T(8,128)(2,1)} %copy-done.1, ...), custom_call_target="tpu_custom_call" | custom-call | tf_op jit(solution)/shard_map/temporal_stats/pallas_call | solution.py:380
  147.8 0.7 collective-permute-start.4
  148.5 3.8 %collective-permute-done.4.far = f32[16,8,128]{2,1,0:T(8,128)S(1)} collective-permute-done((f32[16,8,128]{2,1,0:T(8,128)}, f32[16,8,128]{2,1,0:T(8,128)S(1)}, u32[]{:S(2)}, u32[]{:S(2)}) %collective-permute-start.4) | collective-permute-done | bytes 65568 | tf_op jit(solution)/shard_map/ppermute | solution.py:388
  152.3 0.0 copy-start.4
  152.3 0.6 copy-done.4
  152.9 10.4 %temporal_grads.1 = (bf16[3,4,32,2048]{3,2,1,0:T(8,128)(2,1)}, bf16[3,4,32,2048]{3,2,1,0:T(8,128)(2,1)}, bf16[2,4,16,2048]{3,2,1,0:T(8,128)(2,1)}, bf16[2,4,16,2048]{3,2,1,0:T(8,128)(2,1)}) custom-call(s32[2]{0:T(128)} %pad_add_fusion.place, bf16[4,32,4096]{2,1,0:T(8,128)(2,1)} %bitcast.19, bf16[4,32,4096]{2,1,0:T(8,128)(2,1)} %bitcast.23, ...), custom_call_target="tpu_custom_call" | custom-call | tf_op jit(solution)/shard_map/temporal_grads/pallas_call | solution.py:393
  163.3 0.0 all-to-all-done.ref
  163.3 20.1 %spatial_grads.1 = bf16[32,4,3,32,128]{4,3,2,1,0:T(8,128)(2,1)} custom-call(bf16[32,4,4,32,128]{4,3,2,1,0:T(8,128)(2,1)} %all-to-all-done.ref), custom_call_target="tpu_custom_call" | custom-call | tf_op jit(solution)/shard_map/spatial_grads/pallas_call | solution.py:100
  183.4 9.7 %all-to-all-start.1 = ((bf16[32,4,3,32,128]{4,3,2,1,0:T(8,128)(2,1)}), bf16[32,4,3,32,128]{4,3,2,1,0:T(8,128)(2,1)S(1)}, u32[]{:S(2)}, u32[]{:S(2)}) async-start(bf16[32,4,3,32,128]{4,3,2,1,0:T(8,128)(2,1)} %spatial_grads.1), calls=%async_computation.1 | async-start | bytes 6291456 | tf_op jit(solution)/shard_map/all_to_all | solution.py:453
  193.2 0.1 collective-permute-start.5
  193.3 0.8 collective-permute-start.7
  194.0 1.3 collective-permute-start.6
  195.4 45.0 %collective-permute-done.7 = bf16[2,4,16,2048]{3,2,1,0:T(8,128)(2,1)S(1)} collective-permute-done((bf16[2,4,16,2048]{3,2,1,0:T(8,128)(2,1)}, bf16[2,4,16,2048]{3,2,1,0:T(8,128)(2,1)S(1)}, u32[]{:S(2)}, u32[]{:S(2)}) %collective-permute-start.7) | collective-permute-done | bytes 524320 | tf_op jit(solution)/shard_map/ppermute | solution.py:412
  240.4 0.0 collective-permute-start.8
  240.4 8.8 %collective-permute-done.6.back = bf16[2,4,16,2048]{3,2,1,0:T(8,128)(2,1)} collective-permute-done((bf16[2,4,16,2048]{3,2,1,0:T(8,128)(2,1)}, bf16[2,4,16,2048]{3,2,1,0:T(8,128)(2,1)}, u32[]{:S(2)}, u32[]{:S(2)}) %collective-permute-start.6) | collective-permute-done | bytes 524320 | tf_op jit(solution)/shard_map/ppermute | solution.py:413
  249.2 0.0 collective-permute-done.8.back_swapped
  249.2 0.0 collective-permute-done.5.swapped
  249.2 7.4 %temporal_finish.1 = (bf16[4,32,4096]{2,1,0:T(8,128)(2,1)}, bf16[4,32,4096]{2,1,0:T(8,128)(2,1)}, bf16[4,32,4096]{2,1,0:T(8,128)(2,1)}) custom-call(s32[2]{0:T(128)} %pad_add_fusion.place, bf16[3,4,32,2048]{3,2,1,0:T(8,128)(2,1)} %get-tuple-element.35.mine, bf16[3,4,32,2048]{3,2,1,0:T(8,128)(2,1)} %collective-permute-done.5.swapped, ...), custom_call_target="tpu_custom_call" | custom-call | tf_op jit(solution)/shard_map/temporal_finish/pallas_call | solution.py:430
  256.6 0.0 all-to-all-done.1.ref
  256.6 0.0 copy-start
  256.6 1.6 copy-done
  258.2 4.4 %unpack_heads.1 = (bf16[4,32,4096]{2,1,0:T(8,128)(2,1)}, bf16[4,32,4096]{2,1,0:T(8,128)(2,1)}, bf16[4,32,4096]{2,1,0:T(8,128)(2,1)}) custom-call(bf16[32,4,3,32,128]{4,3,2,1,0:T(8,128)(2,1)} %copy-done), custom_call_target="tpu_custom_call" | custom-call | tf_op jit(solution)/shard_map/unpack_heads/pallas_call | solution.py:56
Async XLA Ops:
  5.5 157.8 %all-to-all-start = ((bf16[32,4,4,32,128]{4,3,2,1,0:T(8,128)(2,1)}), bf16[32,4,4,32,128]{4,3,2,1,0:T(8,128)(2,1)}, u32[]{:S(2)}, u32[]{:S(2)}) async-start(bf16[32,4,4,32,128]{4,3,2,1,0:T(8,128)(2,1)} %pack_heads.1), calls=%async_computation | async-start | bytes 8388608 | tf_op jit(solution)/shard_map/all_to_all | solution.py:450
  81.2 58.9 %collective-permute-start = (bf16[4,4,32,2048]{3,2,1,0:T(8,128)(2,1)}, bf16[4,4,32,2048]{3,2,1,0:T(8,128)(2,1)S(1)}, u32[]{:S(2)}, u32[]{:S(2)}) collective-permute-start(bf16[4,4,32,2048]{3,2,1,0:T(8,128)(2,1)} %swap_pack.1), channel_id=1, source_target_pairs={{0,32},{32,0},{64,96},{96,64},{1,33},{33,1},{65,97},{97,65},{2,34}... | collective-permute-start | bytes 6291464 | tf_op jit(solution)/shard_map/ppermute | solution.py:369
  114.3 15.1 %collective-permute-start.2 = (bf16[2,4,16,2048]{3,2,1,0:T(8,128)(2,1)}, bf16[2,4,16,2048]{3,2,1,0:T(8,128)(2,1)}, u32[]{:S(2)}, u32[]{:S(2)}) collective-permute-start(bf16[2,4,16,2048]{3,2,1,0:T(8,128)(2,1)} %get-tuple-element.25), channel_id=1, source_target_pairs={{0,64},{32,96},{64,0},{96,32},{1,65},{33,97},{65,1},{97,33},{2,66}... | collective-permute-start | bytes 1572872 | tf_op jit(solution)/shard_map/ppermute | solution.py:367
  115.0 25.1 %collective-permute-start.1 = (bf16[2,4,16,2048]{3,2,1,0:T(8,128)(2,1)}, bf16[2,4,16,2048]{3,2,1,0:T(8,128)(2,1)S(1)}, u32[]{:S(2)}, u32[]{:S(2)}) collective-permute-start(bf16[2,4,16,2048]{3,2,1,0:T(8,128)(2,1)} %get-tuple-element.24), channel_id=1, source_target_pairs={{0,64},{32,96},{64,0},{96,32},{1,65},{33,97},{65,1},{97,33},{2,66}... | collective-permute-start | bytes 1572872 | tf_op jit(solution)/shard_map/ppermute | solution.py:368
  129.4 10.7 %collective-permute-start.3 = (bf16[2,4,16,2048]{3,2,1,0:T(8,128)(2,1)}, bf16[2,4,16,2048]{3,2,1,0:T(8,128)(2,1)S(1)}, u32[]{:S(2)}, u32[]{:S(2)}) collective-permute-start(bf16[2,4,16,2048]{3,2,1,0:T(8,128)(2,1)} %collective-permute-done.2), channel_id=1, source_target_pairs={{0,32},{32,0},{64,96},{96,64},{1,33},{33,1},{65,97},{97,65},{2,34}... | collective-permute-start | bytes 1572872 | tf_op jit(solution)/shard_map/ppermute | solution.py:370
  140.1 0.8 copy-start.2
  140.1 1.0 copy-start.3
  141.1 1.4 copy-start.1
  147.8 4.5 %collective-permute-start.4 = (f32[16,8,128]{2,1,0:T(8,128)}, f32[16,8,128]{2,1,0:T(8,128)S(1)}, u32[]{:S(2)}, u32[]{:S(2)}) collective-permute-start(f32[16,8,128]{2,1,0:T(8,128)} %temporal_stats.1), channel_id=1, source_target_pairs={{0,64},{32,96},{64,0},{96,32},{1,65},{33,97},{65,1},{97,33},{2,66}... | collective-permute-start | bytes 196616 | tf_op jit(solution)/shard_map/ppermute | solution.py:388
  152.3 0.6 copy-start.4
  183.4 73.1 %all-to-all-start.1 = ((bf16[32,4,3,32,128]{4,3,2,1,0:T(8,128)(2,1)}), bf16[32,4,3,32,128]{4,3,2,1,0:T(8,128)(2,1)S(1)}, u32[]{:S(2)}, u32[]{:S(2)}) async-start(bf16[32,4,3,32,128]{4,3,2,1,0:T(8,128)(2,1)} %spatial_grads.1), calls=%async_computation.1 | async-start | bytes 6291456 | tf_op jit(solution)/shard_map/all_to_all | solution.py:453
  193.2 56.0 %collective-permute-start.5 = (bf16[3,4,32,2048]{3,2,1,0:T(8,128)(2,1)}, bf16[3,4,32,2048]{3,2,1,0:T(8,128)(2,1)}, u32[]{:S(2)}, u32[]{:S(2)}) collective-permute-start(bf16[3,4,32,2048]{3,2,1,0:T(8,128)(2,1)} %get-tuple-element.36), channel_id=1, source_target_pairs={{0,32},{32,0},{64,96},{96,64},{1,33},{33,1},{65,97},{97,65},{2,34}... | collective-permute-start | bytes 4718600 | tf_op jit(solution)/shard_map/ppermute | solution.py:414
  193.3 47.1 %collective-permute-start.7 = (bf16[2,4,16,2048]{3,2,1,0:T(8,128)(2,1)}, bf16[2,4,16,2048]{3,2,1,0:T(8,128)(2,1)S(1)}, u32[]{:S(2)}, u32[]{:S(2)}) collective-permute-start(bf16[2,4,16,2048]{3,2,1,0:T(8,128)(2,1)} %get-tuple-element.38), channel_id=1, source_target_pairs={{0,64},{32,96},{64,0},{96,32},{1,65},{33,97},{65,1},{97,33},{2,66}... | collective-permute-start | bytes 1572872 | tf_op jit(solution)/shard_map/ppermute | solution.py:412
  194.0 55.2 %collective-permute-start.6 = (bf16[2,4,16,2048]{3,2,1,0:T(8,128)(2,1)}, bf16[2,4,16,2048]{3,2,1,0:T(8,128)(2,1)}, u32[]{:S(2)}, u32[]{:S(2)}) collective-permute-start(bf16[2,4,16,2048]{3,2,1,0:T(8,128)(2,1)} %get-tuple-element.37), channel_id=1, source_target_pairs={{0,64},{32,96},{64,0},{96,32},{1,65},{33,97},{65,1},{97,33},{2,66}... | collective-permute-start | bytes 1572872 | tf_op jit(solution)/shard_map/ppermute | solution.py:413
  240.4 8.8 %collective-permute-start.8 = (bf16[2,4,16,2048]{3,2,1,0:T(8,128)(2,1)S(1)}, bf16[2,4,16,2048]{3,2,1,0:T(8,128)(2,1)}, u32[]{:S(2)}, u32[]{:S(2)}) collective-permute-start(bf16[2,4,16,2048]{3,2,1,0:T(8,128)(2,1)S(1)} %collective-permute-done.7), channel_id=1, source_target_pairs={{0,32},{32,0},{64,96},{96,64},{1,33},{33,1},{65,97},{97,65},{2,34}... | collective-permute-start | bytes 1572872 | tf_op jit(solution)/shard_map/ppermute | solution.py:415
  256.6 1.7 copy-start

commit v2 on v1

v2 whole, which is shorter than its diff:
```python
import functools
import math

import jax
import jax.numpy as jnp
from jax import lax
from jax.experimental import pallas as pl
from jax.experimental.pallas import tpu as pltpu
from jax.sharding import PartitionSpec as P

HEAD_DIM = 128
SCALE = 1.0 / math.sqrt(HEAD_DIM)
LOG2E = 1.0 / math.log(2.0)


def cost(micros):
    return pl.CostEstimate(flops=int(micros * 1e9), bytes_accessed=0, transcendentals=0)


def dot(a, b, contract):
    return lax.dot_general(a, b, (contract, ((), ())), preferred_element_type=jnp.float32)


def pack_kernel(*refs):
    *ins, out = refs
    heads = out.shape[0]
    for a, ref in enumerate(ins):
        for h in range(heads):
            out[h, 0, a] = ref[0, :, h * HEAD_DIM : (h + 1) * HEAD_DIM]


def pack_heads(*arrays):
    frames, positions, width = arrays[0].shape
    heads = width // HEAD_DIM
    count = len(arrays)
    return pl.pallas_call(
        pack_kernel,
        grid=(frames,),
        in_specs=[pl.BlockSpec((1, positions, width), lambda f: (f, 0, 0))] * count,
        out_specs=pl.BlockSpec(
            (heads, 1, count, positions, HEAD_DIM), lambda f: (0, f, 0, 0, 0)
        ),
        out_shape=jax.ShapeDtypeStruct(
            (heads, frames, count, positions, HEAD_DIM), arrays[0].dtype
        ),
        cost_estimate=cost(5),
        name="pack_heads",
    )(*arrays)


def unpack_kernel(ref, *outs):
    heads = ref.shape[0]
    for a, out in enumerate(outs):
        for h in range(heads):
            out[0, :, h * HEAD_DIM : (h + 1) * HEAD_DIM] = ref[h, 0, a]


def unpack_heads(array):
    heads, frames, count, positions, _ = array.shape
    width = heads * HEAD_DIM
    return pl.pallas_call(
        unpack_kernel,
        grid=(frames,),
        in_specs=[
            pl.BlockSpec((heads, 1, count, positions, HEAD_DIM), lambda f: (0, f, 0, 0, 0))
        ],
        out_specs=[pl.BlockSpec((1, positions, width), lambda f: (f, 0, 0))] * count,
        out_shape=[jax.ShapeDtypeStruct((frames, positions, width), array.dtype)] * count,
        cost_estimate=cost(4),
        name="unpack_heads",
    )(array)


def spatial_kernel(block, ref, out):
    parts, _, _, rows, _ = ref.shape
    total = parts * rows
    query, key, value, grad = (ref[:, 0, a].reshape(total, HEAD_DIM) for a in range(4))
    key_t = key.T
    dkey = dvalue = None
    for start in range(0, total, block):
        q = query[start : start + block]
        g = grad[start : start + block]
        scores = dot(key, q, ((1,), (1,)))
        peak = jnp.max(scores, axis=0, keepdims=True)
        e = jnp.exp2((scores - peak) * (SCALE * LOG2E))
        pgrad = dot(value, g, ((1,), (1,)))
        probs = e * (1.0 / jnp.sum(e, axis=0, keepdims=True))
        weights = probs.astype(jnp.bfloat16)
        term = probs * pgrad
        delta = jnp.sum(term, axis=0, keepdims=True)
        sgrad = (term - probs * delta).astype(jnp.bfloat16)
        dq = dot(key_t, sgrad, ((1,), (0,))).T * SCALE
        out[start // rows : (start + block) // rows, 0, 0] = dq.astype(out.dtype).reshape(
            block // rows, rows, HEAD_DIM
        )
        dk = dot(sgrad, q, ((1,), (0,)))
        dv = dot(weights, g, ((1,), (0,)))
        dkey = dk if dkey is None else dkey + dk
        dvalue = dv if dvalue is None else dvalue + dv
    out[:, 0, 1] = (dkey * SCALE).astype(out.dtype).reshape(parts, rows, HEAD_DIM)
    out[:, 0, 2] = dvalue.astype(out.dtype).reshape(parts, rows, HEAD_DIM)


def spatial_grads(array):
    parts, frames, _, rows, _ = array.shape
    return pl.pallas_call(
        functools.partial(spatial_kernel, min(256, parts * rows)),
        grid=(frames,),
        in_specs=[pl.BlockSpec((parts, 1, 4, rows, HEAD_DIM), lambda f: (0, f, 0, 0, 0))],
        out_specs=pl.BlockSpec((parts, 1, 3, rows, HEAD_DIM), lambda f: (0, f, 0, 0, 0)),
        out_shape=jax.ShapeDtypeStruct((parts, frames, 3, rows, HEAD_DIM), array.dtype),
        compiler_params=pltpu.CompilerParams(vmem_limit_bytes=48 * 1024 * 1024),
        cost_estimate=cost(20),
        name="spatial_grads",
    )(array)


GROUP = 16
CHIPS = [(t, t ^ 2) for t in range(4)]
CORES = [(t, t ^ 1) for t in range(4)]
NEVER = -1e30


def ship_kernel(query, key, value, grad, same, other, sems):
    member = lax.axis_index("tm")
    chip, core = member // 2, member % 2
    width = same.shape[-1]

    def copy_all(first, second, row):
        copies = []
        for half, out in ((core, same), (1 - core, other)):
            columns = pl.ds(pl.multiple_of(half * width, width), width)
            for a, ref in enumerate((first, second)):
                copies.append(
                    pltpu.make_async_copy(
                        ref.at[:, pl.ds(row, GROUP), columns], out.at[a], sems.at[len(copies)]
                    )
                )
        for copy in copies:
            copy.start()
        for copy in copies:
            copy.wait()

    @pl.when(chip == 0)
    def _():
        copy_all(key, value, 0)

    @pl.when(chip == 1)
    def _():
        copy_all(query, grad, GROUP)


def ship_pack(query, key, value, grad):
    frames, _, width = query.shape
    shape = jax.ShapeDtypeStruct((2, frames, GROUP, width // 2), query.dtype)
    return pl.pallas_call(
        ship_kernel,
        in_specs=[pl.BlockSpec(memory_space=pl.ANY)] * 4,
        out_specs=[pl.BlockSpec(memory_space=pltpu.VMEM)] * 2,
        out_shape=[shape, shape],
        scratch_shapes=[pltpu.SemaphoreType.DMA((4,))],
        cost_estimate=cost(2),
        name="ship_pack",
    )(query, key, value, grad)


def swap_kernel(*refs):
    *ins, out, sems = refs
    core = lax.axis_index("tm") % 2
    width = out.shape[-1]
    columns = pl.ds(pl.multiple_of((1 - core) * width, width), width)
    copies = [
        pltpu.make_async_copy(ref.at[:, :, columns], out.at[a], sems.at[a])
        for a, ref in enumerate(ins)
    ]
    for copy in copies:
        copy.start()
    for copy in copies:
        copy.wait()


def swap_pack(*arrays):
    frames, positions, width = arrays[0].shape
    count = len(arrays)
    return pl.pallas_call(
        swap_kernel,
        in_specs=[pl.BlockSpec(memory_space=pl.ANY)] * count,
        out_specs=pl.BlockSpec(memory_space=pltpu.VMEM),
        out_shape=jax.ShapeDtypeStruct((count, frames, positions, width // 2), arrays[0].dtype),
        scratch_shapes=[pltpu.SemaphoreType.DMA((count,))],
        cost_estimate=cost(3),
        name="swap_pack",
    )(*arrays)


def frame_mask(core, chip_frames, causal):
    rows = chip_frames * GROUP
    half = chip_frames // 2
    key_row = lax.broadcasted_iota(jnp.int32, (rows, rows), 0)
    query_row = lax.broadcasted_iota(jnp.int32, (rows, rows), 1)
    same = key_row % GROUP == query_row % GROUP
    key_frame = (key_row // GROUP + core * half) % chip_frames
    query_frame = (query_row // GROUP + core * half) % chip_frames
    return same & ((key_frame <= query_frame) | jnp.logical_not(causal))


def gather_rows(own, other, row, columns):
    rows = pl.ds(row, GROUP)
    return jnp.concatenate(
        [
            own[:, rows, columns].reshape(-1, HEAD_DIM),
            other[:, rows, columns].reshape(-1, HEAD_DIM),
        ],
        axis=0,
    )


def block_stats(mask, query, key, value, grad):
    scores = dot(key, query, ((1,), (1,))) * (SCALE * LOG2E)
    scores = jnp.where(mask, scores, NEVER)
    peak = jnp.max(scores, axis=0, keepdims=True)
    e = jnp.exp2(scores - peak)
    pgrad = dot(value, grad, ((1,), (1,)))
    return (
        (scores, pgrad),
        (peak, jnp.sum(e, axis=0, keepdims=True), jnp.sum(e * pgrad, axis=0, keepdims=True)),
    )


def block_grads(products, stats, more, query, key, grad):
    scores, pgrad = products
    peak = jnp.maximum(stats[0], more[0])
    own_scale, more_scale = jnp.exp2(stats[0] - peak), jnp.exp2(more[0] - peak)
    inverse = 1.0 / (stats[1] * own_scale + more[1] * more_scale)
    delta = (stats[2] * own_scale + more[2] * more_scale) * inverse
    probs = jnp.exp2(scores - peak) * inverse
    weights = probs.astype(jnp.bfloat16)
    sgrad = (probs * (pgrad - delta)).astype(jnp.bfloat16)
    dquery = dot(sgrad, key, ((0,), (0,))) * SCALE
    dkey = dot(sgrad, query, ((1,), (0,))) * SCALE
    dvalue = dot(weights, grad, ((1,), (0,)))
    return dquery, dkey, dvalue


def stats_kernel(place, query, key, value, grad, swapped, out):
    mask = frame_mask(place[0], 2 * query.shape[0], True)
    for h in range(query.shape[-1] // HEAD_DIM):
        columns = pl.ds(h * HEAD_DIM, HEAD_DIM)
        rows = [
            gather_rows(ref, swapped.at[a], 0, columns)
            for a, ref in enumerate((query, key, value, grad))
        ]
        out[h] = stats_rows(block_stats(mask, *rows)[1])


def stats_rows(stats):
    return jnp.concatenate(stats + (jnp.zeros((5, stats[0].shape[1]), jnp.float32),), axis=0)


def choose(first, when_first, when_second):
    return tuple(jnp.where(first, a, b) for a, b in zip(when_first, when_second))


def no_stats(rows):
    zero = jnp.zeros((1, rows), jnp.float32)
    return (zero + NEVER, zero, zero)


def place_rows(own, others, a, columns, values):
    values = values.astype(jnp.bfloat16).reshape(2, -1, GROUP, HEAD_DIM)
    own[a, :, :, columns] = values[0]
    others[a, :, :, columns] = values[1]


def early_kernel(
    place, query, key, value, grad, swapped, late_key, late_value, late_swapped, same, other, far,
    early, early_other, near, near_other, back, back_other, stats_out,
):
    core, first = place[0], place[1] == 0
    frames = query.shape[0]
    causal = frame_mask(core, 2 * frames, True)
    cross = frame_mask(core, 2 * frames, False)
    for h in range(query.shape[-1] // HEAD_DIM):
        columns = pl.ds(h * HEAD_DIM, HEAD_DIM)
        rows = [
            gather_rows(ref, swapped.at[a], 0, columns)
            for a, ref in enumerate((query, key, value, grad))
        ]
        late = [
            gather_rows(ref, late_swapped.at[a], 0, columns)
            for a, ref in ((1, late_key), (2, late_value))
        ]
        sent = [gather_rows(same.at[a], other.at[a], 0, columns) for a in range(2)]
        crossed = [
            jnp.where(first, sent[0], rows[0]),
            jnp.where(first, late[0], sent[0]),
            jnp.where(first, late[1], sent[1]),
            jnp.where(first, sent[1], rows[3]),
        ]
        received = tuple(far[h, i : i + 1] for i in range(3))
        products, stats = block_stats(causal, *rows)
        cross_products, cross_stats = block_stats(cross, *crossed)
        stats_out[h] = stats_rows(cross_stats)
        none = no_stats(2 * frames * GROUP)
        out = block_grads(
            products, stats, choose(first, none, cross_stats), rows[0], rows[1], rows[3]
        )
        cross_out = block_grads(
            cross_products,
            cross_stats,
            choose(first, received, stats),
            crossed[0],
            crossed[1],
            crossed[3],
        )
        zero = jnp.zeros_like(cross_out[0])
        place_rows(early, early_other, 0, columns, out[0] + jnp.where(first, zero, cross_out[0]))
        place_rows(early, early_other, 1, columns, out[1])
        place_rows(early, early_other, 2, columns, out[2])
        place_rows(near, near_other, 0, columns, cross_out[1])
        place_rows(near, near_other, 1, columns, cross_out[2])
        place_rows(
            back, back_other, 0, columns, jnp.where(first, cross_out[0], cross_out[1])
        )
        place_rows(back, back_other, 1, columns, jnp.where(first, zero, cross_out[2]))


def late_kernel(
    place, query, key, value, grad, swapped, far, early, early_other, near, near_other, back,
    back_other, dquery, dkey, dvalue, theirs,
):
    core, first = place[0], place[1] == 0
    frames = query.shape[0]
    causal = frame_mask(core, 2 * frames, True)
    early_rows, late_rows = pl.ds(0, GROUP), pl.ds(GROUP, GROUP)
    for h in range(query.shape[-1] // HEAD_DIM):
        columns = pl.ds(h * HEAD_DIM, HEAD_DIM)
        rows = [
            gather_rows(ref, swapped.at[a], 0, columns)
            for a, ref in enumerate((query, key, value, grad))
        ]
        received = tuple(far[h, i : i + 1] for i in range(3))
        products, stats = block_stats(causal, *rows)
        none = no_stats(2 * frames * GROUP)
        late = [
            values.reshape(2, frames, GROUP, HEAD_DIM)
            for values in block_grads(
                products, stats, choose(first, none, received), rows[0], rows[1], rows[3]
            )
        ]

        def write(outs, side, near, back, early):
            zero = jnp.zeros((frames, GROUP, HEAD_DIM), jnp.float32)
            back = [back[a, :, :, columns].astype(jnp.float32) for a in range(2)]
            near = [near[a, :, :, columns].astype(jnp.float32) for a in range(2)]
            early = [early[a, :, :, columns].astype(jnp.float32) for a in range(3)]
            early[1] += jnp.where(first, back[0], zero)
            early[2] += jnp.where(first, back[1], zero)
            more = (
                jnp.where(first, zero, back[0]),
                jnp.where(first, near[0], zero),
                jnp.where(first, near[1], zero),
            )
            for a, out in enumerate(outs):
                out[:, early_rows, columns] = early[a].astype(jnp.bfloat16)
                out[:, late_rows, columns] = (late[a][side] + more[a]).astype(jnp.bfloat16)

        write((dquery, dkey, dvalue), 0, near, back, early)
        write([theirs.at[a] for a in range(3)], 1, near_other, back_other, early_other)


def finish_kernel(place, swapped, *refs):
    for a, out in enumerate(refs[3:]):
        out[...] = swapped[a]


STEPS = 4


class Temporal:
    def __init__(self, arrays):
        self.arrays = arrays
        self.frames, self.positions, self.width = arrays[0].shape
        self.half = self.width // 2
        self.block = self.half // STEPS
        self.heads = self.half // HEAD_DIM
        member = lax.axis_index("tm")
        self.place = jnp.stack([member % 2, member // 2])

    def own(self, row):
        return pl.BlockSpec(
            (self.frames, GROUP, self.block), lambda j, p: (0, row, p[0] * STEPS + j)
        )

    def part(self, count, rows, row=0):
        return pl.BlockSpec((count, self.frames, rows, self.block), lambda j, p: (0, 0, row, j))

    def stats(self):
        return pl.BlockSpec(
            (self.heads // STEPS, 8, 2 * self.frames * GROUP), lambda j, p: (j, 0, 0)
        )

    def stats_shape(self):
        return jax.ShapeDtypeStruct((self.heads, 8, 2 * self.frames * GROUP), jnp.float32)

    def shape(self, count, rows):
        return jax.ShapeDtypeStruct((count, self.frames, rows, self.half), jnp.bfloat16)

    def call(self, kernel, name, micros, in_specs, out_specs, out_shape, operands, aliases={}):
        return pl.pallas_call(
            kernel,
            grid_spec=pltpu.PrefetchScalarGridSpec(
                num_scalar_prefetch=1, grid=(STEPS,), in_specs=in_specs, out_specs=out_specs
            ),
            out_shape=out_shape,
            input_output_aliases=aliases,
            cost_estimate=cost(micros),
            name=name,
        )(self.place, *operands)

    def late_stats(self, swapped):
        return self.call(
            stats_kernel,
            "temporal_stats",
            5,
            [self.own(1)] * 4 + [self.part(4, GROUP, 1)],
            self.stats(),
            self.stats_shape(),
            self.arrays + (swapped,),
        )

    def early_grads(self, swapped, same, other, far):
        return self.call(
            early_kernel,
            "temporal_early",
            EARLY_COST,
            [self.own(0)] * 4
            + [self.part(4, GROUP)]
            + [self.own(1)] * 2
            + [self.part(4, GROUP, 1)]
            + [self.part(2, GROUP)] * 2
            + [self.stats()],
            [self.part(3, GROUP)] * 2 + [self.part(2, GROUP)] * 4 + [self.stats()],
            [self.shape(3, GROUP)] * 2 + [self.shape(2, GROUP)] * 4 + [self.stats_shape()],
            self.arrays
            + (swapped, self.arrays[1], self.arrays[2], swapped, same, other, far),
        )

    def late_grads(self, swapped, far, *parts):
        out = pl.BlockSpec(
            (self.frames, self.positions, self.block), lambda j, p: (0, 0, p[0] * STEPS + j)
        )
        out_shape = jax.ShapeDtypeStruct((self.frames, self.positions, self.width), jnp.bfloat16)
        return self.call(
            late_kernel,
            "temporal_late",
            LATE_COST,
            [self.own(1)] * 4
            + [self.part(4, GROUP, 1), self.stats()]
            + [self.part(3, GROUP)] * 2
            + [self.part(2, GROUP)] * 4,
            [out] * 3 + [self.part(3, self.positions)],
            [out_shape] * 3 + [self.shape(3, self.positions)],
            self.arrays + (swapped, far) + parts,
        )

    def finish(self, outs, swapped):
        out = pl.BlockSpec(
            (self.frames, self.positions, self.block),
            lambda j, p: (0, 0, (1 - p[0]) * STEPS + j),
        )
        return self.call(
            finish_kernel,
            "temporal_finish",
            3,
            [self.part(3, self.positions)] + [pl.BlockSpec(memory_space=pl.ANY)] * 3,
            [out] * 3,
            [jax.ShapeDtypeStruct(a.shape, a.dtype) for a in outs],
            (swapped,) + tuple(outs),
            {2: 0, 3: 1, 4: 2},
        )


EARLY_COST = 100
LATE_COST = 100


def local(
    space_query, space_key, space_value, space_grad, time_query, time_key, time_value, time_grad
):
    def flat(array):
        return array.reshape(array.shape[1:])

    def chips(array):
        return lax.ppermute(array, "tm", CHIPS)

    def cores(array):
        return lax.ppermute(array, "tm", CORES)

    spatial = tuple(map(flat, (space_query, space_key, space_value, space_grad)))
    arrays = tuple(map(flat, (time_query, time_key, time_value, time_grad)))

    ships, arrays, spatial = lax.optimization_barrier((ship_pack(*arrays), arrays, spatial))
    same, other = map(chips, ships)
    swapped = cores(swap_pack(*arrays))
    work = Temporal(arrays)
    packed, far, other = lax.optimization_barrier(
        (pack_heads(*spatial), work.late_stats(swapped), other)
    )
    far = chips(far)
    packed = lax.all_to_all(packed, "space", 0, 0, tiled=True)
    early, early_other, near, near_other, back, back_other, far = work.early_grads(
        swapped, same, cores(other), far
    )
    far, back_other, back = chips(far), chips(back_other), chips(back)
    packed, far, back, back_other = lax.optimization_barrier(
        (spatial_grads(packed), far, back, back_other)
    )
    packed = lax.all_to_all(packed, "space", 0, 0, tiled=True)
    *outs, theirs = work.late_grads(
        swapped, far, early, early_other, near, near_other, back, back_other
    )
    outs = work.finish(outs, cores(theirs))
    outs = tuple(unpack_heads(packed)) + tuple(outs)
    return tuple(out.reshape(space_query.shape) for out in outs)


def solution(mesh):
    spec = P(None, "tm", "space", None)
    return jax.shard_map(
        local, mesh=mesh, in_specs=(spec,) * 8, out_specs=(spec,) * 6, check_vma=False
    )
```

time: 268 us -> 170 us (0.63); the launches traced: 263 us -> 169 us
  Pallas kernels: 150 us -> 61.7 us
  waiting for transfers between devices: 80.8 us -> 69.8 us
  starting transfers between devices: 25.8 us -> 30.4 us
    ppermute x9, waiting for transfers between devices: 80.8 us -> 5.05 us  [the longest x3 3.74 us: cores(): return lax.ppermute(array, 'tm', CORES)]
    all_to_all x1 -> x2, waiting for transfers between devices: 0.01 us -> 64.7 us  [local(): packed = lax.all_to_all(packed, 'space', 0, 0, tiled=True)]
    pallas_call x1, Pallas kernels: 64.7 us -> 2.98 us  [swap_pack(): pl.pallas_call(swap_kernel, in_specs=[pl.BlockSpec(memory_space=pl.ANY)]...]
    pallas_call x1, Pallas kernels: 32.9 us -> 2.22 us  [ship_pack(): pl.pallas_call(ship_kernel, in_specs=[pl.BlockSpec(memory_space=pl.ANY)]...]
    all_to_all x1 -> x2, starting transfers between devices: 11 us -> 23.1 us  [local(): packed = lax.all_to_all(packed, 'space', 0, 0, tiled=True)]
    all_to_all x1 -> x0, starting transfers between devices: 9.74 us -> none  [local(): packed = lax.all_to_all(spatial_grads(packed), 'space', 0, 0, tiled=True)]
    pallas_call x3 -> x4, Pallas kernels: 23.1 us -> 27.1 us  [call(): pl.pallas_call(kernel, grid_spec=pltpu.PrefetchScalarGridSpec(num_scalar_...]
    unnamed x10 -> x18, local copies, waits for them, and re-layouts: 4.62 us -> 5.58 us
  transfers between devices with their start and end apart: 11 -> 11, of which waited for: 5 -> 4; matrix products, arithmetic and copies ran while one was open for 0% -> 0% of each run, Pallas kernels for 46% -> 31%
where the time goes in v2:
time: 170 us; the launch traced here: 169 us
  waiting for transfers between devices  69.8 us (41%)
  Pallas kernels  61.7 us (36%)
  starting transfers between devices  30.4 us (18%)
  local copies, waits for them, and re-layouts  5.58 us (3%)
    all_to_all x2, waiting for transfers between devices, local(): packed = lax.all_to_all(packed, 'space', 0, 0, tiled=True)  64.7 us
    pallas_call x4, Pallas kernels, call(): pl.pallas_call(kernel, grid_spec=pltpu.PrefetchScalarGridSpec(num_scalar_...  27.1 us
    all_to_all x2, starting transfers between devices, local(): packed = lax.all_to_all(packed, 'space', 0, 0, tiled=True)  23.1 us
    pallas_call x1, Pallas kernels, spatial_grads(): pl.pallas_call(functools.partial(spatial_kernel, min(256, parts * rows)),...  20.1 us
    ppermute x6, starting transfers between devices, chips(): return lax.ppermute(array, 'tm', CHIPS)  7.13 us
    unnamed x18, local copies, waits for them, and re-layouts  5.58 us
    pallas_call x1, Pallas kernels, pack_heads(): pl.pallas_call(pack_kernel, grid=(frames,), in_specs=[pl.BlockSpec((1, po...  4.9 us
    pallas_call x1, Pallas kernels, unpack_heads(): pl.pallas_call(unpack_kernel, grid=(frames,), in_specs=[pl.BlockSpec((hea...  4.35 us
  transfers between devices with their start and end apart: 11, of which 4 were waited for; matrix products, arithmetic and copies ran while one was open for 0% of the time, Pallas kernels for 31%

profile of v2, /device:TPU:0, one launch (start us, length us, event | category | flops | bytes accessed | tf_op | source)
XLA Modules:
  0.0 168.8 jit_solution(623403363431665936)
XLA Ops:
  0.6 2.2 %ship_pack.1 = (bf16[2,4,16,2048]{3,2,1,0:T(8,128)(2,1)}, bf16[2,4,16,2048]{3,2,1,0:T(8,128)(2,1)}) custom-call(bf16[4,32,4096]{2,1,0:T(8,128)(2,1)} %bitcast.20, bf16[4,32,4096]{2,1,0:T(8,128)(2,1)} %bitcast.25, bf16[4,32,4096]{2,1,0:T(8,128)(2,1)} %bitcast.31, bf16[4,32,4096]{2,1,0:T(8,128)(2,1)} %bitcast.37), custom_call_target="tpu_custom_call" | custom-call | flops 2000000000 | tf_op jit(solution)/shard_map/ship_pack/pallas_call | solution.py:156
  2.9 0.0 copy-start.3
  2.9 3.0 %swap_pack.1 = bf16[4,4,32,2048]{3,2,1,0:T(8,128)(2,1)} custom-call(bf16[4,32,4096]{2,1,0:T(8,128)(2,1)} %bitcast.21, bf16[4,32,4096]{2,1,0:T(8,128)(2,1)} %bitcast.26, bf16[4,32,4096]{2,1,0:T(8,128)(2,1)} %bitcast.32, bf16[4,32,4096]{2,1,0:T(8,128)(2,1)} %bitcast.38), custom_call_target="tpu_custom_call" | custom-call | flops 3000000000 | tf_op jit(solution)/shard_map/swap_pack/pallas_call | solution.py:185
  5.9 0.1 collective-permute-start
  5.9 1.8 %collective-permute-start.1 = (bf16[2,4,16,2048]{3,2,1,0:T(8,128)(2,1)}, bf16[2,4,16,2048]{3,2,1,0:T(8,128)(2,1)}, u32[]{:S(2)}, u32[]{:S(2)}) collective-permute-start(bf16[2,4,16,2048]{3,2,1,0:T(8,128)(2,1)} %get-tuple-element.52), channel_id=1, source_target_pairs={{0,64},{32,96},{64,0},{96,32},{1,65},{33,97},{65,1},{97,33},{2,66}... | collective-permute-start | bytes 1572872 | tf_op jit(solution)/shard_map/ppermute | solution.py:495
  7.7 0.0 copy-done.3
  7.7 0.3 collective-permute-start.2
  8.1 4.9 %pack_heads.1 = bf16[32,4,4,32,128]{4,3,2,1,0:T(8,128)(2,1)} custom-call(bf16[4,32,4096]{2,1,0:T(8,128)(2,1)} %bitcast.16, bf16[4,32,4096]{2,1,0:T(8,128)(2,1)} %bitcast.17, bf16[4,32,4096]{2,1,0:T(8,128)(2,1)} %bitcast.18, bf16[4,32,4096]{2,1,0:T(8,128)(2,1)} %bitcast.19), custom_call_target="tpu_custom_call" | custom-call | flops 5000000000 | tf_op jit(solution)/shard_map/pack_heads/pallas_call | solution.py:36
  13.0 0.6 pad_add_fusion.place
  13.6 0.0 collective-permute-done.swapped.late_swapped
  13.6 0.0 copy-start.1
  13.6 1.4 copy-done.1
  15.0 4.8 %temporal_stats.1 = f32[16,8,128]{2,1,0:T(8,128)} custom-call(s32[2]{0:T(128)} %pad_add_fusion.place, bf16[4,32,4096]{2,1,0:T(8,128)(2,1)} %bitcast.22, bf16[4,32,4096]{2,1,0:T(8,128)(2,1)} %bitcast.27, bf16[4,32,4096]{2,1,0:T(8,128)(2,1)} %bitcast.33, bf16[4,32,4096]{2,1,0:T(8,128)(2,1)} %bitcast.39, bf16[4,4,32,2048]{3,2,1,0:T(8,128)(2,1)} %copy-done.1), custom_call_target="tpu_custom_call" | custom-call | flops 5000000000 | tf_op jit(solution)/shard_map/temporal_stats/pallas_call | solution.py:410
  19.8 1.3 collective-permute-done.1
  21.1 0.0 collective-permute-start.3
  21.1 1.7 collective-permute-start.4
  22.8 10.6 %all-to-all-start = ((bf16[32,4,4,32,128]{4,3,2,1,0:T(8,128)(2,1)}), bf16[32,4,4,32,128]{4,3,2,1,0:T(8,128)(2,1)}, u32[]{:S(2)}, u32[]{:S(2)}) async-start(bf16[32,4,4,32,128]{4,3,2,1,0:T(8,128)(2,1)} %pack_heads.1), calls=%async_computation | async-start | bytes 8388608 | tf_op jit(solution)/shard_map/all_to_all | solution.py:511
  33.4 0.0 collective-permute-done.2.same
  33.4 0.0 copy-start.2
  33.4 0.0 collective-permute-done.4.far
  33.4 0.0 copy-start.8
  33.4 0.0 collective-permute-done.3.other
  33.5 0.8 copy-done.2
  34.2 0.0 copy-done.8
  34.2 0.8 copy-done.6
  35.0 9.7 %temporal_early.1 = (bf16[3,4,16,2048]{3,2,1,0:T(8,128)(2,1)}, bf16[3,4,16,2048]{3,2,1,0:T(8,128)(2,1)}, bf16[2,4,16,2048]{3,2,1,0:T(8,128)(2,1)}, bf16[2,4,16,2...) custom-call(s32[2]{0:T(128)} %pad_add_fusion.place, ...), custom_call_target="tpu_custom_call" | custom-call | flops 99999997952 | tf_op jit(solution)/shard_map/temporal_early/pallas_call | solution.py:410
  44.7 1.3 collective-permute-start.5
  46.0 0.8 collective-permute-start.6
  46.8 1.2 collective-permute-start.7
  48.1 40.6 %all-to-all-done.ref = bf16[32,4,4,32,128]{4,3,2,1,0:T(8,128)(2,1)} async-done(((bf16[32,4,4,32,128]{4,3,2,1,0:T(8,128)(2,1)}), bf16[32,4,4,32,128]{4,3,2,1,0:T(8,128)(2,1)}, u32[]{:S(2)}, u32[]{:S(2)}) %all-to-all-start) | async-done | bytes 4194336 | tf_op jit(solution)/shard_map/all_to_all | solution.py:511
  88.6 20.1 %spatial_grads.1 = bf16[32,4,3,32,128]{4,3,2,1,0:T(8,128)(2,1)} custom-call(bf16[32,4,4,32,128]{4,3,2,1,0:T(8,128)(2,1)} %all-to-all-done.ref), custom_call_target="tpu_custom_call" | custom-call | flops 20000000000 | tf_op jit(solution)/shard_map/spatial_grads/pallas_call | solution.py:106
  108.8 0.0 collective-permute-done.5.far
  108.8 0.0 copy-start.7
  108.8 0.0 collective-permute-done.6.back
  108.8 0.0 copy-start.4
  108.8 0.0 collective-permute-done.7.back_other
  108.8 0.0 copy-start.5
  108.8 0.8 copy-done.4
  109.6 0.2 copy-done.5
  109.8 12.5 %all-to-all-start.1 = ((bf16[32,4,3,32,128]{4,3,2,1,0:T(8,128)(2,1)}), bf16[32,4,3,32,128]{4,3,2,1,0:T(8,128)(2,1)S(1)}, u32[]{:S(2)}, u32[]{:S(2)}) async-start(bf16[32,4,3,32,128]{4,3,2,1,0:T(8,128)(2,1)} %spatial_grads.1), calls=%async_computation.1 | async-start | bytes 6291456 | tf_op jit(solution)/shard_map/all_to_all | solution.py:519
  122.3 0.0 copy-done.7
  122.3 8.4 %temporal_late.1 = (bf16[4,32,4096]{2,1,0:T(8,128)(2,1)}, bf16[4,32,4096]{2,1,0:T(8,128)(2,1)}, bf16[4,32,4096]{2,1,0:T(8,128)(2,1)}, bf16[3,4,32,2048]{3,2,1,0:T(8,128)(2,1)}) custom-call(s32[2]{0:T(128)} %pad_add_fusion.place, bf16[4,32,4096]{2,1,0:T(8,128)(2,1)} %bitcast.24, bf16[4,32,4096]{2,1,0:T(8,128)(2,1)} %bitcast.30, ...), custom_call_target="tpu_custom_call" | custom-call | flops 99999997952 | tf_op jit(solution)/shard_map/temporal_late/pallas_call | solution.py:410
  130.6 0.1 collective-permute-start.8
  130.7 3.7 %collective-permute-done.8.swapped = bf16[3,4,32,2048]{3,2,1,0:T(8,128)(2,1)} collective-permute-done((bf16[3,4,32,2048]{3,2,1,0:T(8,128)(2,1)}, bf16[3,4,32,2048]{3,2,1,0:T(8,128)(2,1)}, u32[]{:S(2)}, u32[]{:S(2)}) %collective-permute-start.8) | collective-permute-done | bytes 1572896 | tf_op jit(solution)/shard_map/ppermute | solution.py:498
  134.5 4.2 %temporal_finish.1 = (bf16[4,32,4096]{2,1,0:T(8,128)(2,1)}, bf16[4,32,4096]{2,1,0:T(8,128)(2,1)}, bf16[4,32,4096]{2,1,0:T(8,128)(2,1)}) custom-call(s32[2]{0:T(128)} %pad_add_fusion.place, bf16[3,4,32,2048]{3,2,1,0:T(8,128)(2,1)} %collective-permute-done.8.swapped, ...), custom_call_target="tpu_custom_call", output_to_operand_aliasing={{0}: (2, {}), {1}: (3, {}), {2}: (4, {})} | custom-call | flops 3000000000 | tf_op jit(solution)/shard_map/temporal_finish/pallas_call | solution.py:410
  138.7 24.1 %all-to-all-done.1.ref = bf16[32,4,3,32,128]{4,3,2,1,0:T(8,128)(2,1)S(1)} async-done(((bf16[32,4,3,32,128]{4,3,2,1,0:T(8,128)(2,1)}), bf16[32,4,3,32,128]{4,3,2,1,0:T(8,128)(2,1)S(1)}, u32[]{:S(2)}, u32[]{:S(2)}) %all-to-all-start.1) | async-done | bytes 3145760 | tf_op jit(solution)/shard_map/all_to_all | solution.py:519
  162.8 1.6 copy-done
  164.5 4.4 %unpack_heads.1 = (bf16[4,32,4096]{2,1,0:T(8,128)(2,1)}, bf16[4,32,4096]{2,1,0:T(8,128)(2,1)}, bf16[4,32,4096]{2,1,0:T(8,128)(2,1)}) custom-call(bf16[32,4,3,32,128]{4,3,2,1,0:T(8,128)(2,1)} %copy-done), custom_call_target="tpu_custom_call" | custom-call | flops 4000000000 | tf_op jit(solution)/shard_map/unpack_heads/pallas_call | solution.py:61
  (2 shorter events, 0.0 us)
Async XLA Ops:
  2.9 4.9 %copy-start.3 = (bf16[2,4,16,2048]{3,2,1,0:T(8,128)(2,1)S(1)}, bf16[2,4,16,2048]{3,2,1,0:T(8,128)(2,1)}, u32[]{:S(2)}) copy-start(bf16[2,4,16,2048]{3,2,1,0:T(8,128)(2,1)} %get-tuple-element.54) | copy-start | bytes 1572868
  5.9 7.7 %collective-permute-start = (bf16[4,4,32,2048]{3,2,1,0:T(8,128)(2,1)}, bf16[4,4,32,2048]{3,2,1,0:T(8,128)(2,1)S(1)}, u32[]{:S(2)}, u32[]{:S(2)}) collective-permute-start(bf16[4,4,32,2048]{3,2,1,0:T(8,128)(2,1)} %swap_pack.1), channel_id=1, source_target_pairs={{0,32},{32,0},{64,96},{96,64},{1,33},{33,1},{65,97},{97,65},{2,34}... | collective-permute-start | bytes 6291464 | tf_op jit(solution)/shard_map/ppermute | solution.py:498
  5.9 15.1 %collective-permute-start.1 = (bf16[2,4,16,2048]{3,2,1,0:T(8,128)(2,1)}, bf16[2,4,16,2048]{3,2,1,0:T(8,128)(2,1)}, u32[]{:S(2)}, u32[]{:S(2)}) collective-permute-start(bf16[2,4,16,2048]{3,2,1,0:T(8,128)(2,1)} %get-tuple-element.52), channel_id=1, source_target_pairs={{0,64},{32,96},{64,0},{96,32},{1,65},{33,97},{65,1},{97,33},{2,66}... | collective-permute-start | bytes 1572872 | tf_op jit(solution)/shard_map/ppermute | solution.py:495
  7.7 25.7 %collective-permute-start.2 = (bf16[2,4,16,2048]{3,2,1,0:T(8,128)(2,1)S(1)}, bf16[2,4,16,2048]{3,2,1,0:T(8,128)(2,1)S(1)}, u32[]{:S(2)}, u32[]{:S(2)}) collective-permute-start(bf16[2,4,16,2048]{3,2,1,0:T(8,128)(2,1)S(1)} %copy-done.3), channel_id=1, source_target_pairs={{0,64},{32,96},{64,0},{96,32},{1,65},{33,97},{65,1},{97,33},{2,66}... | collective-permute-start | bytes 1572872 | tf_op jit(solution)/shard_map/ppermute | solution.py:495
  13.6 1.4 copy-start.1
  21.1 12.4 %collective-permute-start.3 = (bf16[2,4,16,2048]{3,2,1,0:T(8,128)(2,1)}, bf16[2,4,16,2048]{3,2,1,0:T(8,128)(2,1)S(1)}, u32[]{:S(2)}, u32[]{:S(2)}) collective-permute-start(bf16[2,4,16,2048]{3,2,1,0:T(8,128)(2,1)} %collective-permute-done.1), channel_id=1, source_target_pairs={{0,32},{32,0},{64,96},{96,64},{1,33},{33,1},{65,97},{97,65},{2,34}... | collective-permute-start | bytes 1572872 | tf_op jit(solution)/shard_map/ppermute | solution.py:498
  21.1 12.3 %collective-permute-start.4 = (f32[16,8,128]{2,1,0:T(8,128)}, f32[16,8,128]{2,1,0:T(8,128)S(1)}, u32[]{:S(2)}, u32[]{:S(2)}) collective-permute-start(f32[16,8,128]{2,1,0:T(8,128)} %temporal_stats.1), channel_id=1, source_target_pairs={{0,64},{32,96},{64,0},{96,32},{1,65},{33,97},{65,1},{97,33},{2,66}... | collective-permute-start | bytes 196616 | tf_op jit(solution)/shard_map/ppermute | solution.py:495
  22.8 65.9 %all-to-all-start = ((bf16[32,4,4,32,128]{4,3,2,1,0:T(8,128)(2,1)}), bf16[32,4,4,32,128]{4,3,2,1,0:T(8,128)(2,1)}, u32[]{:S(2)}, u32[]{:S(2)}) async-start(bf16[32,4,4,32,128]{4,3,2,1,0:T(8,128)(2,1)} %pack_heads.1), calls=%async_computation | async-start | bytes 8388608 | tf_op jit(solution)/shard_map/all_to_all | solution.py:511
  33.4 0.8 copy-start.2
  33.4 0.8 copy-start.8
  34.2 0.8 copy-start.6
  44.7 64.1 %collective-permute-start.5 = (f32[16,8,128]{2,1,0:T(8,128)}, f32[16,8,128]{2,1,0:T(8,128)S(1)}, u32[]{:S(2)}, u32[]{:S(2)}) collective-permute-start(f32[16,8,128]{2,1,0:T(8,128)} %get-tuple-element.57), channel_id=1, source_target_pairs={{0,64},{32,96},{64,0},{96,32},{1,65},{33,97},{65,1},{97,33},{2,66}... | collective-permute-start | bytes 196616 | tf_op jit(solution)/shard_map/ppermute | solution.py:495
  46.0 62.8 %collective-permute-start.6 = (bf16[2,4,16,2048]{3,2,1,0:T(8,128)(2,1)}, bf16[2,4,16,2048]{3,2,1,0:T(8,128)(2,1)S(1)}, u32[]{:S(2)}, u32[]{:S(2)}) collective-permute-start(bf16[2,4,16,2048]{3,2,1,0:T(8,128)(2,1)} %get-tuple-element.58), channel_id=1, source_target_pairs={{0,64},{32,96},{64,0},{96,32},{1,65},{33,97},{65,1},{97,33},{2,66}... | collective-permute-start | bytes 1572872 | tf_op jit(solution)/shard_map/ppermute | solution.py:495
  46.8 62.0 %collective-permute-start.7 = (bf16[2,4,16,2048]{3,2,1,0:T(8,128)(2,1)}, bf16[2,4,16,2048]{3,2,1,0:T(8,128)(2,1)S(1)}, u32[]{:S(2)}, u32[]{:S(2)}) collective-permute-start(bf16[2,4,16,2048]{3,2,1,0:T(8,128)(2,1)} %get-tuple-element.59), channel_id=1, source_target_pairs={{0,64},{32,96},{64,0},{96,32},{1,65},{33,97},{65,1},{97,33},{2,66}... | collective-permute-start | bytes 1572872 | tf_op jit(solution)/shard_map/ppermute | solution.py:495
  108.8 13.5 %copy-start.7 = (f32[16,8,128]{2,1,0:T(8,128)}, f32[16,8,128]{2,1,0:T(8,128)S(1)}, u32[]{:S(2)}) copy-start(f32[16,8,128]{2,1,0:T(8,128)S(1)} %collective-permute-done.5.far) | copy-start | bytes 196612
  108.8 0.8 copy-start.4
  108.8 1.0 copy-start.5
  109.8 53.0 %all-to-all-start.1 = ((bf16[32,4,3,32,128]{4,3,2,1,0:T(8,128)(2,1)}), bf16[32,4,3,32,128]{4,3,2,1,0:T(8,128)(2,1)S(1)}, u32[]{:S(2)}, u32[]{:S(2)}) async-start(bf16[32,4,3,32,128]{4,3,2,1,0:T(8,128)(2,1)} %spatial_grads.1), calls=%async_computation.1 | async-start | bytes 6291456 | tf_op jit(solution)/shard_map/all_to_all | solution.py:519
  130.6 3.8 %collective-permute-start.8 = (bf16[3,4,32,2048]{3,2,1,0:T(8,128)(2,1)}, bf16[3,4,32,2048]{3,2,1,0:T(8,128)(2,1)}, u32[]{:S(2)}, u32[]{:S(2)}) collective-permute-start(bf16[3,4,32,2048]{3,2,1,0:T(8,128)(2,1)} %get-tuple-element.71), channel_id=1, source_target_pairs={{0,32},{32,0},{64,96},{96,64},{1,33},{33,1},{65,97},{97,65},{2,34}... | collective-permute-start | bytes 4718600 | tf_op jit(solution)/shard_map/ppermute | solution.py:498
  162.8 1.6 copy-start

commit v3 on v2

--- a/solution.py
+++ b/solution.py
@@ -11,6 +11,10 @@
 HEAD_DIM = 128
 SCALE = 1.0 / math.sqrt(HEAD_DIM)
 LOG2E = 1.0 / math.log(2.0)
+MIB = 1024 * 1024
+PARAMS = pltpu.CompilerParams(vmem_limit_bytes=60 * MIB)
+LATE_PARAMS = pltpu.CompilerParams(vmem_limit_bytes=59 * MIB)
+UNPACK_PARAMS = pltpu.CompilerParams(vmem_limit_bytes=16 * MIB)
 
 
 def cost(micros):
@@ -22,27 +26,45 @@
 
 
 def pack_kernel(*refs):
-    *ins, out = refs
-    heads = out.shape[0]
-    for a, ref in enumerate(ins):
-        for h in range(heads):
-            out[h, 0, a] = ref[0, :, h * HEAD_DIM : (h + 1) * HEAD_DIM]
+    *ins, out, rows, heads, row_sems, head_sems = refs
+    count, frames = rows.shape[:2]
+
+    def load(f, a):
+        return pltpu.make_async_copy(ins[a].at[f], rows.at[a, f], row_sems.at[f, a])
+
+    def store(f):
+        return pltpu.make_async_copy(heads.at[:, f], out.at[:, f], head_sems.at[f])
+
+    for f in range(frames):
+        for a in range(count):
+            load(f, a).start()
+    for f in range(frames):
+        for a in range(count):
+            load(f, a).wait()
+            for h in range(heads.shape[0]):
+                heads[h, f, a] = rows[a, f, :, h * HEAD_DIM : (h + 1) * HEAD_DIM]
+        store(f).start()
+    for f in range(frames):
+        store(f).wait()
 
 
 def pack_heads(*arrays):
     frames, positions, width = arrays[0].shape
-    heads = width // HEAD_DIM
-    count = len(arrays)
+    count, heads = len(arrays), width // HEAD_DIM
+    dtype = arrays[0].dtype
+    packed = (heads, frames, count, positions, HEAD_DIM)
     return pl.pallas_call(
         pack_kernel,
-        grid=(frames,),
-        in_specs=[pl.BlockSpec((1, positions, width), lambda f: (f, 0, 0))] * count,
-        out_specs=pl.BlockSpec(
-            (heads, 1, count, positions, HEAD_DIM), lambda f: (0, f, 0, 0, 0)
-        ),
-        out_shape=jax.ShapeDtypeStruct(
-            (heads, frames, count, positions, HEAD_DIM), arrays[0].dtype
-        ),
+        in_specs=[pl.BlockSpec(memory_space=pltpu.HBM)] * count,
+        out_specs=pl.BlockSpec(memory_space=pl.ANY),
+        out_shape=jax.ShapeDtypeStruct(packed, dtype),
+        scratch_shapes=[
+            pltpu.VMEM((count, frames, positions, width), dtype),
+            pltpu.VMEM(packed, dtype),
+            pltpu.SemaphoreType.DMA((frames, count)),
+            pltpu.SemaphoreType.DMA((frames,)),
+        ],
+        compiler_params=PARAMS,
         cost_estimate=cost(5),
         name="pack_heads",
     )(*arrays)
@@ -66,6 +88,7 @@
         ],
         out_specs=[pl.BlockSpec((1, positions, width), lambda f: (f, 0, 0))] * count,
         out_shape=[jax.ShapeDtypeStruct((frames, positions, width), array.dtype)] * count,
+        compiler_params=UNPACK_PARAMS,
         cost_estimate=cost(4),
         name="unpack_heads",
     )(array)
@@ -104,12 +127,12 @@
 def spatial_grads(array):
     parts, frames, _, rows, _ = array.shape
     return pl.pallas_call(
-        functools.partial(spatial_kernel, min(256, parts * rows)),
+        functools.partial(spatial_kernel, min(1024, parts * rows)),
         grid=(frames,),
         in_specs=[pl.BlockSpec((parts, 1, 4, rows, HEAD_DIM), lambda f: (0, f, 0, 0, 0))],
         out_specs=pl.BlockSpec((parts, 1, 3, rows, HEAD_DIM), lambda f: (0, f, 0, 0, 0)),
         out_shape=jax.ShapeDtypeStruct((parts, frames, 3, rows, HEAD_DIM), array.dtype),
-        compiler_params=pltpu.CompilerParams(vmem_limit_bytes=48 * 1024 * 1024),
+        compiler_params=PARAMS,
         cost_estimate=cost(20),
         name="spatial_grads",
     )(array)
@@ -118,24 +141,32 @@
 GROUP = 16
 CHIPS = [(t, t ^ 2) for t in range(4)]
 CORES = [(t, t ^ 1) for t in range(4)]
+CROSSED = [(t, t ^ 3) for t in range(4)]
 NEVER = -1e30
 
 
-def ship_kernel(query, key, value, grad, same, other, sems):
+def ship_kernel(query, key, value, grad, same, other, swap, sems):
     member = lax.axis_index("tm")
     chip, core = member // 2, member % 2
     width = same.shape[-1]
+    own_columns = pl.ds(pl.multiple_of(core * width, width), width)
+    other_columns = pl.ds(pl.multiple_of((1 - core) * width, width), width)
 
     def copy_all(first, second, row):
-        copies = []
-        for half, out in ((core, same), (1 - core, other)):
-            columns = pl.ds(pl.multiple_of(half * width, width), width)
-            for a, ref in enumerate((first, second)):
-                copies.append(
-                    pltpu.make_async_copy(
-                        ref.at[:, pl.ds(row, GROUP), columns], out.at[a], sems.at[len(copies)]
-                    )
-                )
+        rows = pl.ds(row, GROUP)
+        pairs = [
+            (ref.at[:, rows, columns], out.at[a])
+            for columns, out in ((other_columns, other), (own_columns, same))
+            for a, ref in enumerate((first, second))
+        ]
+        pairs += [
+            (ref.at[:, :, other_columns], swap.at[a])
+            for a, ref in enumerate((query, key, value, grad))
+        ]
+        copies = [
+            pltpu.make_async_copy(source, target, sems.at[i])
+            for i, (source, target) in enumerate(pairs)
+        ]
         for copy in copies:
             copy.start()
         for copy in copies:
@@ -151,46 +182,20 @@
 
 
 def ship_pack(query, key, value, grad):
-    frames, _, width = query.shape
-    shape = jax.ShapeDtypeStruct((2, frames, GROUP, width // 2), query.dtype)
+    frames, positions, width = query.shape
+    half = width // 2
+    shape = jax.ShapeDtypeStruct((2, frames, GROUP, half), query.dtype)
+    swap_shape = jax.ShapeDtypeStruct((4, frames, positions, half), query.dtype)
     return pl.pallas_call(
         ship_kernel,
-        in_specs=[pl.BlockSpec(memory_space=pl.ANY)] * 4,
-        out_specs=[pl.BlockSpec(memory_space=pltpu.VMEM)] * 2,
-        out_shape=[shape, shape],
-        scratch_shapes=[pltpu.SemaphoreType.DMA((4,))],
+        in_specs=[pl.BlockSpec(memory_space=pltpu.HBM)] * 4,
+        out_specs=[pl.BlockSpec(memory_space=pltpu.VMEM)] * 3,
+        out_shape=[shape, shape, swap_shape],
+        scratch_shapes=[pltpu.SemaphoreType.DMA((8,))],
+        compiler_params=PARAMS,
         cost_estimate=cost(2),
         name="ship_pack",
     )(query, key, value, grad)
-
-
-def swap_kernel(*refs):
-    *ins, out, sems = refs
-    core = lax.axis_index("tm") % 2
-    width = out.shape[-1]
-    columns = pl.ds(pl.multiple_of((1 - core) * width, width), width)
-    copies = [
-        pltpu.make_async_copy(ref.at[:, :, columns], out.at[a], sems.at[a])
-        for a, ref in enumerate(ins)
-    ]
-    for copy in copies:
-        copy.start()
-    for copy in copies:
-        copy.wait()
-
-
-def swap_pack(*arrays):
-    frames, positions, width = arrays[0].shape
-    count = len(arrays)
-    return pl.pallas_call(
-        swap_kernel,
-        in_specs=[pl.BlockSpec(memory_space=pl.ANY)] * count,
-        out_specs=pl.BlockSpec(memory_space=pltpu.VMEM),
-        out_shape=jax.ShapeDtypeStruct((count, frames, positions, width // 2), arrays[0].dtype),
-        scratch_shapes=[pltpu.SemaphoreType.DMA((count,))],
-        cost_estimate=cost(3),
-        name="swap_pack",
-    )(*arrays)
 
 
 def frame_mask(core, chip_frames, causal):
@@ -243,7 +248,7 @@
 
 
 def stats_kernel(place, query, key, value, grad, swapped, out):
-    mask = frame_mask(place[0], 2 * query.shape[0], True)
+    mask = frame_mask(place[0] % 2, 2 * query.shape[0], True)
     for h in range(query.shape[-1] // HEAD_DIM):
         columns = pl.ds(h * HEAD_DIM, HEAD_DIM)
         rows = [
@@ -276,7 +281,7 @@
     place, query, key, value, grad, swapped, late_key, late_value, late_swapped, same, other, far,
     early, early_other, near, near_other, back, back_other, stats_out,
 ):
-    core, first = place[0], place[1] == 0
+    core, first = place[0] % 2, place[0] < 2
     frames = query.shape[0]
     causal = frame_mask(core, 2 * frames, True)
     cross = frame_mask(core, 2 * frames, False)
@@ -329,7 +334,7 @@
     place, query, key, value, grad, swapped, far, early, early_other, near, near_other, back,
     back_other, dquery, dkey, dvalue, theirs,
 ):
-    core, first = place[0], place[1] == 0
+    core, first = place[0] % 2, place[0] < 2
     frames = query.shape[0]
     causal = frame_mask(core, 2 * frames, True)
     early_rows, late_rows = pl.ds(0, GROUP), pl.ds(GROUP, GROUP)
@@ -374,7 +379,7 @@
         out[...] = swapped[a]
 
 
-STEPS = 4
+STATS_STEPS, EARLY_STEPS, LATE_STEPS, FINISH_STEPS = 2, 4, 4, 4
 
 
 class Temporal:
@@ -382,22 +387,24 @@
         self.arrays = arrays
         self.frames, self.positions, self.width = arrays[0].shape
         self.half = self.width // 2
-        self.block = self.half // STEPS
         self.heads = self.half // HEAD_DIM
         member = lax.axis_index("tm")
-        self.place = jnp.stack([member % 2, member // 2])
-
-    def own(self, row):
+        self.place = member.reshape(1)
+
+    def own(self, steps, row):
         return pl.BlockSpec(
-            (self.frames, GROUP, self.block), lambda j, p: (0, row, p[0] * STEPS + j)
-        )
-
-    def part(self, count, rows, row=0):
-        return pl.BlockSpec((count, self.frames, rows, self.block), lambda j, p: (0, 0, row, j))
-
-    def stats(self):
+            (self.frames, GROUP, self.half // steps),
+            lambda j, p: (0, row, (p[0] % 2) * steps + j),
+        )
+
+    def part(self, steps, count, rows, row=0):
         return pl.BlockSpec(
-            (self.heads // STEPS, 8, 2 * self.frames * GROUP), lambda j, p: (j, 0, 0)
+            (count, self.frames, rows, self.half // steps), lambda j, p: (0, 0, row, j)
+        )
+
+    def stats(self, steps):
+        return pl.BlockSpec(
+            (self.heads // steps, 8, 2 * self.frames * GROUP), lambda j, p: (j, 0, 0)
         )
 
     def stats_shape(self):
@@ -406,41 +413,44 @@
     def shape(self, count, rows):
         return jax.ShapeDtypeStruct((count, self.frames, rows, self.half), jnp.bfloat16)
 
-    def call(self, kernel, name, micros, in_specs, out_specs, out_shape, operands, aliases={}):
+    def call(self, steps, kernel, name, micros, in_specs, out_specs, out_shape, operands, params=PARAMS, aliases={}):
         return pl.pallas_call(
             kernel,
             grid_spec=pltpu.PrefetchScalarGridSpec(
-                num_scalar_prefetch=1, grid=(STEPS,), in_specs=in_specs, out_specs=out_specs
+                num_scalar_prefetch=1, grid=(steps,), in_specs=in_specs, out_specs=out_specs
             ),
             out_shape=out_shape,
             input_output_aliases=aliases,
-            cost_estimate=cost(micros),
+            compiler_params=PARAMS,
+        cost_estimate=cost(micros),
             name=name,
         )(self.place, *operands)
 
     def late_stats(self, swapped):
         return self.call(
+            STATS_STEPS,
             stats_kernel,
             "temporal_stats",
             5,
-            [self.own(1)] * 4 + [self.part(4, GROUP, 1)],
-            self.stats(),
+            [self.own(STATS_STEPS, 1)] * 4 + [self.part(STATS_STEPS, 4, GROUP, 1)],
+            self.stats(STATS_STEPS),
             self.stats_shape(),
             self.arrays + (swapped,),
         )
 
     def early_grads(self, swapped, same, other, far):
         return self.call(
+            EARLY_STEPS,
             early_kernel,
             "temporal_early",
             EARLY_COST,
-            [self.own(0)] * 4
-            + [self.part(4, GROUP)]
-            + [self.own(1)] * 2
-            + [self.part(4, GROUP, 1)]
-            + [self.part(2, GROUP)] * 2
-            + [self.stats()],
-            [self.part(3, GROUP)] * 2 + [self.part(2, GROUP)] * 4 + [self.stats()],
+            [self.own(EARLY_STEPS, 0)] * 4
+            + [self.part(EARLY_STEPS, 4, GROUP)]
+            + [self.own(EARLY_STEPS, 1)] * 2
+            + [self.part(EARLY_STEPS, 4, GROUP, 1)]
+            + [self.part(EARLY_STEPS, 2, GROUP)] * 2
+            + [self.stats(EARLY_STEPS)],
+            [self.part(EARLY_STEPS, 3, GROUP)] * 2 + [self.part(EARLY_STEPS, 2, GROUP)] * 4 + [self.stats(EARLY_STEPS)],
             [self.shape(3, GROUP)] * 2 + [self.shape(2, GROUP)] * 4 + [self.stats_shape()],
             self.arrays
             + (swapped, self.arrays[1], self.arrays[2], swapped, same, other, far),
@@ -448,35 +458,39 @@
 
     def late_grads(self, swapped, far, *parts):
         out = pl.BlockSpec(
-            (self.frames, self.positions, self.block), lambda j, p: (0, 0, p[0] * STEPS + j)
+            (self.frames, self.positions, self.half // LATE_STEPS), lambda j, p: (0, 0, (p[0] % 2) * LATE_STEPS + j)
         )
         out_shape = jax.ShapeDtypeStruct((self.frames, self.positions, self.width), jnp.bfloat16)
         return self.call(
+            LATE_STEPS,
             late_kernel,
             "temporal_late",
             LATE_COST,
-            [self.own(1)] * 4
-            + [self.part(4, GROUP, 1), self.stats()]
-            + [self.part(3, GROUP)] * 2
-            + [self.part(2, GROUP)] * 4,
-            [out] * 3 + [self.part(3, self.positions)],
+            [self.own(LATE_STEPS, 1)] * 4
+            + [self.part(LATE_STEPS, 4, GROUP, 1), self.stats(LATE_STEPS)]
+            + [self.part(LATE_STEPS, 3, GROUP)] * 2
+            + [self.part(LATE_STEPS, 2, GROUP)] * 4,
+            [out] * 3 + [self.part(LATE_STEPS, 3, self.positions)],
             [out_shape] * 3 + [self.shape(3, self.positions)],
             self.arrays + (swapped, far) + parts,
+            LATE_PARAMS,
         )
 
     def finish(self, outs, swapped):
         out = pl.BlockSpec(
-            (self.frames, self.positions, self.block),
-            lambda j, p: (0, 0, (1 - p[0]) * STEPS + j),
+            (self.frames, self.positions, self.half // FINISH_STEPS),
+            lambda j, p: (0, 0, (1 - p[0] % 2) * FINISH_STEPS + j),
         )
         return self.call(
+            FINISH_STEPS,
             finish_kernel,
             "temporal_finish",
             3,
-            [self.part(3, self.positions)] + [pl.BlockSpec(memory_space=pl.ANY)] * 3,
+            [self.part(FINISH_STEPS, 3, self.positions)] + [pl.BlockSpec(memory_space=pl.ANY)] * 3,
             [out] * 3,
             [jax.ShapeDtypeStruct(a.shape, a.dtype) for a in outs],
             (swapped,) + tuple(outs),
+            LATE_PARAMS,
             {2: 0, 3: 1, 4: 2},
         )
 
@@ -494,6 +508,9 @@
     def chips(array):
         return lax.ppermute(array, "tm", CHIPS)
 
+    def crossed(array):
+        return lax.ppermute(array, "tm", CROSSED)
+
     def cores(array):
         return lax.ppermute(array, "tm", CORES)
 
@@ -501,22 +518,16 @@
     arrays = tuple(map(flat, (time_query, time_key, time_value, time_grad)))
 
     ships, arrays, spatial = lax.optimization_barrier((ship_pack(*arrays), arrays, spatial))
-    same, other = map(chips, ships)
-    swapped = cores(swap_pack(*arrays))
+    same, other, swapped = chips(ships[0]), crossed(ships[1]), cores(ships[2])
     work = Temporal(arrays)
-    packed, far, other = lax.optimization_barrier(
-        (pack_heads(*spatial), work.late_stats(swapped), other)
-    )
+    packed, far = lax.optimization_barrier((pack_heads(*spatial), work.late_stats(swapped)))
     far = chips(far)
     packed = lax.all_to_all(packed, "space", 0, 0, tiled=True)
     early, early_other, near, near_other, back, back_other, far = work.early_grads(
-        swapped, same, cores(other), far
+        swapped, same, other, far
     )
     far, back_other, back = chips(far), chips(back_other), chips(back)
-    packed, far, back, back_other = lax.optimization_barrier(
-        (spatial_grads(packed), far, back, back_other)
-    )
-    packed = lax.all_to_all(packed, "space", 0, 0, tiled=True)
+    packed = lax.all_to_all(spatial_grads(packed), "space", 0, 0, tiled=True)
     *outs, theirs = work.late_grads(
         swapped, far, early, early_other, near, near_other, back, back_other
     )

time: 170 us -> 154 us (0.906)
  Pallas kernels: 61.7 us -> 50.9 us
  starting transfers between devices: 30.4 us -> 27.1 us
  local copies, waits for them, and re-layouts: 5.58 us -> 2.6 us
  waiting for transfers between devices: 69.8 us -> 72.1 us
    all_to_all x2 -> x1, waiting for transfers between devices: 64.7 us -> 37.8 us  [local(): packed = lax.all_to_all(packed, 'space', 0, 0, tiled=True)]
    all_to_all x0 -> x1, waiting for transfers between devices: none -> 25 us  [local(): packed = lax.all_to_all(spatial_grads(packed), 'space', 0, 0, tiled=True)]
    all_to_all x2 -> x1, starting transfers between devices: 23.1 us -> 10.6 us  [local(): packed = lax.all_to_all(packed, 'space', 0, 0, tiled=True)]
    all_to_all x0 -> x1, starting transfers between devices: none -> 8.95 us  [local(): packed = lax.all_to_all(spatial_grads(packed), 'space', 0, 0, tiled=True)]
    pallas_call x4 -> x3, Pallas kernels: 30.2 us -> 25 us  [the longest x1 18 us: spatial_grads(): pl.pallas_call(functools.partial(spatial_kernel, min(1024, parts * rows))...]
    pallas_call x4, Pallas kernels: 27.1 us -> 23.4 us  [call(): pl.pallas_call(kernel, grid_spec=pltpu.PrefetchScalarGridSpec(num_scalar_...]
    ppermute x0 -> x1, waiting for transfers between devices: none -> 3.44 us  [crossed(): return lax.ppermute(array, 'tm', CROSSED)]
    unnamed x18 -> x10, local copies, waits for them, and re-layouts: 5.58 us -> 2.6 us
  transfers between devices with their start and end apart: 11 -> 10, of which waited for: 4 -> 5; matrix products, arithmetic and copies ran while one was open for 0% -> 0% of each run, Pallas kernels for 31% -> 29%
where the time goes in v3:
time: 154 us; the launch traced here: 153 us
  waiting for transfers between devices  72.1 us (47%)
  Pallas kernels  50.9 us (33%)
  starting transfers between devices  27.1 us (18%)
  local copies, waits for them, and re-layouts  2.6 us (2%)
    all_to_all x1, waiting for transfers between devices, local(): packed = lax.all_to_all(packed, 'space', 0, 0, tiled=True)  37.8 us
    all_to_all x1, waiting for transfers between devices, local(): packed = lax.all_to_all(spatial_grads(packed), 'space', 0, 0, tiled=True)  25 us
    pallas_call x4, Pallas kernels, call(): pl.pallas_call(kernel, grid_spec=pltpu.PrefetchScalarGridSpec(num_scalar_...  23.4 us
    pallas_call x1, Pallas kernels, spatial_grads(): pl.pallas_call(functools.partial(spatial_kernel, min(1024, parts * rows))...  18 us
    all_to_all x1, starting transfers between devices, local(): packed = lax.all_to_all(packed, 'space', 0, 0, tiled=True)  10.6 us
    all_to_all x1, starting transfers between devices, local(): packed = lax.all_to_all(spatial_grads(packed), 'space', 0, 0, tiled=True)  8.95 us
    ppermute x5, starting transfers between devices, chips(): return lax.ppermute(array, 'tm', CHIPS)  7.19 us
    ppermute x2, waiting for transfers between devices, cores(): return lax.ppermute(array, 'tm', CORES)  3.74 us
  transfers between devices with their start and end apart: 10, of which 5 were waited for; matrix products, arithmetic and copies ran while one was open for 0% of the time, Pallas kernels for 29%

profile of v3, /device:TPU:0, one launch (start us, length us, event | category | flops | bytes accessed | tf_op | source)
XLA Modules:
  0.0 153.4 jit_solution(2352090200600572952)
XLA Ops:
  0.6 3.6 %ship_pack.1 = (bf16[2,4,16,2048]{3,2,1,0:T(8,128)(2,1)}, bf16[2,4,16,2048]{3,2,1,0:T(8,128)(2,1)}, bf16[4,4,32,2048]{3,2,1,0:T(8,128)(2,1)}) custom-call(bf16[4,32,4096]{2,1,0:T(8,128)(2,1)} %bitcast.19, bf16[4,32,4096]{2,1,0:T(8,128)(2,1)} %bitcast.23, bf16[4,32,4096]{2,1,0:T(8,128)(2,1)} %bitcast.28, bf16[4,32,4096]{2,1,0:T(8,128)(2,1)} %bitcast.33), custom_call_target="tpu_custom_call" | custom-call | flops 2000000000 | tf_op jit(solution)/shard_map/ship_pack/pallas_call | solution.py:189
  4.3 0.1 collective-permute-start
  4.4 1.7 %collective-permute-start.1 = (bf16[2,4,16,2048]{3,2,1,0:T(8,128)(2,1)}, bf16[2,4,16,2048]{3,2,1,0:T(8,128)(2,1)S(1)}, u32[]{:S(2)}, u32[]{:S(2)}) collective-permute-start(bf16[2,4,16,2048]{3,2,1,0:T(8,128)(2,1)} %get-tuple-element.55), channel_id=1, source_target_pairs={{0,64},{32,96},{64,0},{96,32},{1,65},{33,97},{65,1},{97,33},{2,66}... | collective-permute-start | bytes 1572872 | tf_op jit(solution)/shard_map/ppermute | solution.py:509
  6.1 0.1 collective-permute-start.2
  6.2 3.4 %pack_heads.1 = bf16[32,4,4,32,128]{4,3,2,1,0:T(8,128)(2,1)} custom-call(bf16[4,32,4096]{2,1,0:T(8,128)(2,1)} %bitcast.15, bf16[4,32,4096]{2,1,0:T(8,128)(2,1)} %bitcast.16, bf16[4,32,4096]{2,1,0:T(8,128)(2,1)} %bitcast.17, bf16[4,32,4096]{2,1,0:T(8,128)(2,1)} %bitcast.18), custom_call_target="tpu_custom_call" | custom-call | flops 5000000000 | tf_op jit(solution)/shard_map/pack_heads/pallas_call | solution.py:56
  9.7 0.0 collective-permute-done.swapped.late_swapped
  9.7 0.0 copy-start
  9.7 1.4 copy-done
  11.1 3.1 %temporal_stats.1 = f32[16,8,128]{2,1,0:T(8,128)} custom-call(s32[1]{0:T(128)} %bitcast.8.place, bf16[4,32,4096]{2,1,0:T(8,128)(2,1)} %bitcast.20, bf16[4,32,4096]{2,1,0:T(8,128)(2,1)} %bitcast.24, bf16[4,32,4096]{2,1,0:T(8,128)(2,1)} %bitcast.29, bf16[4,32,4096]{2,1,0:T(8,128)(2,1)} %bitcast.34, bf16[4,4,32,2048]{3,2,1,0:T(8,128)(2,1)} %copy-done), custom_call_target="tpu_custom_call" | custom-call | flops 5000000000 | tf_op jit(solution)/shard_map/temporal_stats/pallas_call | solution.py:417
  14.1 1.7 %collective-permute-start.3 = (f32[16,8,128]{2,1,0:T(8,128)}, f32[16,8,128]{2,1,0:T(8,128)S(1)}, u32[]{:S(2)}, u32[]{:S(2)}) collective-permute-start(f32[16,8,128]{2,1,0:T(8,128)} %temporal_stats.1), channel_id=1, source_target_pairs={{0,64},{32,96},{64,0},{96,32},{1,65},{33,97},{65,1},{97,33},{2,66}... | collective-permute-start | bytes 196616 | tf_op jit(solution)/shard_map/ppermute | solution.py:509
  15.8 10.6 %all-to-all-start = ((bf16[32,4,4,32,128]{4,3,2,1,0:T(8,128)(2,1)}), bf16[32,4,4,32,128]{4,3,2,1,0:T(8,128)(2,1)}, u32[]{:S(2)}, u32[]{:S(2)}) async-start(bf16[32,4,4,32,128]{4,3,2,1,0:T(8,128)(2,1)} %pack_heads.1), calls=%async_computation | async-start | bytes 8388608 | tf_op jit(solution)/shard_map/all_to_all | solution.py:525
  26.5 0.0 collective-permute-done.1.same
  26.5 0.0 copy-start.1
  26.5 3.4 %collective-permute-done.2.other = bf16[2,4,16,2048]{3,2,1,0:T(8,128)(2,1)S(1)} collective-permute-done((bf16[2,4,16,2048]{3,2,1,0:T(8,128)(2,1)}, bf16[2,4,16,2048]{3,2,1,0:T(8,128)(2,1)S(1)}, u32[]{:S(2)}, u32[]{:S(2)}) %collective-permute-start.2) | collective-permute-done | bytes 524320 | tf_op jit(solution)/shard_map/ppermute | solution.py:512
  29.9 0.0 copy-start.2
  29.9 2.1 %collective-permute-done.3.far = f32[16,8,128]{2,1,0:T(8,128)S(1)} collective-permute-done((f32[16,8,128]{2,1,0:T(8,128)}, f32[16,8,128]{2,1,0:T(8,128)S(1)}, u32[]{:S(2)}, u32[]{:S(2)}) %collective-permute-start.3) | collective-permute-done | bytes 65568 | tf_op jit(solution)/shard_map/ppermute | solution.py:509
  32.0 0.0 copy-done.1
  32.0 0.0 copy-done.2
  32.0 0.0 copy-start.4
  32.1 0.6 copy-done.4
  32.7 9.1 %temporal_early.1 = (bf16[3,4,16,2048]{3,2,1,0:T(8,128)(2,1)}, bf16[3,4,16,2048]{3,2,1,0:T(8,128)(2,1)}, bf16[2,4,16,2048]{3,2,1,0:T(8,128)(2,1)}, bf16[2,4,16,2...) custom-call(s32[1]{0:T(128)} %bitcast.8.place, ...), custom_call_target="tpu_custom_call" | custom-call | flops 99999997952 | tf_op jit(solution)/shard_map/temporal_early/pallas_call | solution.py:417
  41.8 1.7 %collective-permute-start.4 = (f32[16,8,128]{2,1,0:T(8,128)}, f32[16,8,128]{2,1,0:T(8,128)S(1)}, u32[]{:S(2)}, u32[]{:S(2)}) collective-permute-start(f32[16,8,128]{2,1,0:T(8,128)} %get-tuple-element.58), channel_id=1, source_target_pairs={{0,64},{32,96},{64,0},{96,32},{1,65},{33,97},{65,1},{97,33},{2,66}... | collective-permute-start | bytes 196616 | tf_op jit(solution)/shard_map/ppermute | solution.py:509
  43.5 0.4 collective-permute-start.5
  43.9 1.7 %collective-permute-start.6 = (bf16[2,4,16,2048]{3,2,1,0:T(8,128)(2,1)}, bf16[2,4,16,2048]{3,2,1,0:T(8,128)(2,1)}, u32[]{:S(2)}, u32[]{:S(2)}) collective-permute-start(bf16[2,4,16,2048]{3,2,1,0:T(8,128)(2,1)} %get-tuple-element.64), channel_id=1, source_target_pairs={{0,64},{32,96},{64,0},{96,32},{1,65},{33,97},{65,1},{97,33},{2,66}... | collective-permute-start | bytes 1572872 | tf_op jit(solution)/shard_map/ppermute | solution.py:509
  45.5 37.8 %all-to-all-done.ref = bf16[32,4,4,32,128]{4,3,2,1,0:T(8,128)(2,1)} async-done(((bf16[32,4,4,32,128]{4,3,2,1,0:T(8,128)(2,1)}), bf16[32,4,4,32,128]{4,3,2,1,0:T(8,128)(2,1)}, u32[]{:S(2)}, u32[]{:S(2)}) %all-to-all-start) | async-done | bytes 4194336 | tf_op jit(solution)/shard_map/all_to_all | solution.py:525
  83.3 18.0 %spatial_grads.1 = bf16[32,4,3,32,128]{4,3,2,1,0:T(8,128)(2,1)} custom-call(bf16[32,4,4,32,128]{4,3,2,1,0:T(8,128)(2,1)} %all-to-all-done.ref), custom_call_target="tpu_custom_call" | custom-call | flops 20000000000 | tf_op jit(solution)/shard_map/spatial_grads/pallas_call | solution.py:129
  101.3 8.9 %all-to-all-start.1 = ((bf16[32,4,3,32,128]{4,3,2,1,0:T(8,128)(2,1)}), bf16[32,4,3,32,128]{4,3,2,1,0:T(8,128)(2,1)S(1)}, u32[]{:S(2)}, u32[]{:S(2)}) async-start(bf16[32,4,3,32,128]{4,3,2,1,0:T(8,128)(2,1)} %spatial_grads.1), calls=%async_computation.1 | async-start | bytes 6291456 | tf_op jit(solution)/shard_map/all_to_all | solution.py:530
  110.2 0.0 collective-permute-done.4.far
  110.2 0.0 copy-start.3
  110.2 0.0 collective-permute-done.5.back
  110.2 0.0 collective-permute-done.6.back_other
  110.3 0.6 copy-done.3
  110.8 7.7 %temporal_late.1 = (bf16[4,32,4096]{2,1,0:T(8,128)(2,1)}, bf16[4,32,4096]{2,1,0:T(8,128)(2,1)}, bf16[4,32,4096]{2,1,0:T(8,128)(2,1)}, bf16[3,4,32,2048]{3,2,1,0:T(8,128)(2,1)}) custom-call(s32[1]{0:T(128)} %bitcast.8.place, bf16[4,32,4096]{2,1,0:T(8,128)(2,1)} %bitcast.22, bf16[4,32,4096]{2,1,0:T(8,128)(2,1)} %bitcast.27, bf16[4,32,4096]{2,1,0:T(8,128)(2,1)} %bitcast.32, ...), custom_call_target="tpu_custom_call" | custom-call | flops 99999997952 | tf_op jit(solution)/shard_map/temporal_late/pallas_call | solution.py:417
  118.5 0.1 collective-permute-start.7
  118.6 3.7 %collective-permute-done.7.swapped = bf16[3,4,32,2048]{3,2,1,0:T(8,128)(2,1)} collective-permute-done((bf16[3,4,32,2048]{3,2,1,0:T(8,128)(2,1)}, bf16[3,4,32,2048]{3,2,1,0:T(8,128)(2,1)}, u32[]{:S(2)}, u32[]{:S(2)}) %collective-permute-start.7) | collective-permute-done | bytes 1572896 | tf_op jit(solution)/shard_map/ppermute | solution.py:515
  122.4 3.6 %temporal_finish.1 = (bf16[4,32,4096]{2,1,0:T(8,128)(2,1)}, bf16[4,32,4096]{2,1,0:T(8,128)(2,1)}, bf16[4,32,4096]{2,1,0:T(8,128)(2,1)}) custom-call(s32[1]{0:T(128)} %bitcast.8.place, bf16[3,4,32,2048]{3,2,1,0:T(8,128)(2,1)} %collective-permute-done.7.swapped, ...), custom_call_target="tpu_custom_call", output_to_operand_aliasing={{0}: (2, {}), {1}: (3, {}), {2}: (4, {})} | custom-call | flops 3000000000 | tf_op jit(solution)/shard_map/temporal_finish/pallas_call | solution.py:417
  125.9 25.0 %all-to-all-done.1.ref = bf16[32,4,3,32,128]{4,3,2,1,0:T(8,128)(2,1)S(1)} async-done(((bf16[32,4,3,32,128]{4,3,2,1,0:T(8,128)(2,1)}), bf16[32,4,3,32,128]{4,3,2,1,0:T(8,128)(2,1)S(1)}, u32[]{:S(2)}, u32[]{:S(2)}) %all-to-all-start.1) | async-done | bytes 3145760 | tf_op jit(solution)/shard_map/all_to_all | solution.py:530
  150.9 2.5 %unpack_heads.1 = (bf16[4,32,4096]{2,1,0:T(8,128)(2,1)}, bf16[4,32,4096]{2,1,0:T(8,128)(2,1)}, bf16[4,32,4096]{2,1,0:T(8,128)(2,1)}) custom-call(bf16[32,4,3,32,128]{4,3,2,1,0:T(8,128)(2,1)S(1)} %all-to-all-done.1.ref), custom_call_target="tpu_custom_call" | custom-call | flops 4000000000 | tf_op jit(solution)/shard_map/unpack_heads/pallas_call | solution.py:83
Async XLA Ops:
  4.3 5.4 %collective-permute-start = (bf16[4,4,32,2048]{3,2,1,0:T(8,128)(2,1)}, bf16[4,4,32,2048]{3,2,1,0:T(8,128)(2,1)S(1)}, u32[]{:S(2)}, u32[]{:S(2)}) collective-permute-start(bf16[4,4,32,2048]{3,2,1,0:T(8,128)(2,1)} %get-tuple-element.50), channel_id=1, source_target_pairs={{0,32},{32,0},{64,96},{96,64},{1,33},{33,1},{65,97},{97,65},{2,34}... | collective-permute-start | bytes 6291464 | tf_op jit(solution)/shard_map/ppermute | solution.py:515
  4.4 22.1 %collective-permute-start.1 = (bf16[2,4,16,2048]{3,2,1,0:T(8,128)(2,1)}, bf16[2,4,16,2048]{3,2,1,0:T(8,128)(2,1)S(1)}, u32[]{:S(2)}, u32[]{:S(2)}) collective-permute-start(bf16[2,4,16,2048]{3,2,1,0:T(8,128)(2,1)} %get-tuple-element.55), channel_id=1, source_target_pairs={{0,64},{32,96},{64,0},{96,32},{1,65},{33,97},{65,1},{97,33},{2,66}... | collective-permute-start | bytes 1572872 | tf_op jit(solution)/shard_map/ppermute | solution.py:509
  6.1 23.8 %collective-permute-start.2 = (bf16[2,4,16,2048]{3,2,1,0:T(8,128)(2,1)}, bf16[2,4,16,2048]{3,2,1,0:T(8,128)(2,1)S(1)}, u32[]{:S(2)}, u32[]{:S(2)}) collective-permute-start(bf16[2,4,16,2048]{3,2,1,0:T(8,128)(2,1)} %get-tuple-element.56), channel_id=1, source_target_pairs={{0,96},{32,64},{64,32},{96,0},{1,97},{33,65},{65,33},{97,1},{2,98}... | collective-permute-start | bytes 1572872 | tf_op jit(solution)/shard_map/ppermute | solution.py:512
  9.7 1.4 copy-start
  14.1 17.9 %collective-permute-start.3 = (f32[16,8,128]{2,1,0:T(8,128)}, f32[16,8,128]{2,1,0:T(8,128)S(1)}, u32[]{:S(2)}, u32[]{:S(2)}) collective-permute-start(f32[16,8,128]{2,1,0:T(8,128)} %temporal_stats.1), channel_id=1, source_target_pairs={{0,64},{32,96},{64,0},{96,32},{1,65},{33,97},{65,1},{97,33},{2,66}... | collective-permute-start | bytes 196616 | tf_op jit(solution)/shard_map/ppermute | solution.py:509
  15.8 67.5 %all-to-all-start = ((bf16[32,4,4,32,128]{4,3,2,1,0:T(8,128)(2,1)}), bf16[32,4,4,32,128]{4,3,2,1,0:T(8,128)(2,1)}, u32[]{:S(2)}, u32[]{:S(2)}) async-start(bf16[32,4,4,32,128]{4,3,2,1,0:T(8,128)(2,1)} %pack_heads.1), calls=%async_computation | async-start | bytes 8388608 | tf_op jit(solution)/shard_map/all_to_all | solution.py:525
  26.5 5.6 %copy-start.1 = (bf16[2,4,16,2048]{3,2,1,0:T(8,128)(2,1)}, bf16[2,4,16,2048]{3,2,1,0:T(8,128)(2,1)S(1)}, u32[]{:S(2)}) copy-start(bf16[2,4,16,2048]{3,2,1,0:T(8,128)(2,1)S(1)} %collective-permute-done.1.same) | copy-start | bytes 1572868
  29.9 2.1 %copy-start.2 = (bf16[2,4,16,2048]{3,2,1,0:T(8,128)(2,1)}, bf16[2,4,16,2048]{3,2,1,0:T(8,128)(2,1)S(1)}, u32[]{:S(2)}) copy-start(bf16[2,4,16,2048]{3,2,1,0:T(8,128)(2,1)S(1)} %collective-permute-done.2.other) | copy-start | bytes 1572868
  32.0 0.6 copy-start.4
  41.8 68.4 %collective-permute-start.4 = (f32[16,8,128]{2,1,0:T(8,128)}, f32[16,8,128]{2,1,0:T(8,128)S(1)}, u32[]{:S(2)}, u32[]{:S(2)}) collective-permute-start(f32[16,8,128]{2,1,0:T(8,128)} %get-tuple-element.58), channel_id=1, source_target_pairs={{0,64},{32,96},{64,0},{96,32},{1,65},{33,97},{65,1},{97,33},{2,66}... | collective-permute-start | bytes 196616 | tf_op jit(solution)/shard_map/ppermute | solution.py:509
  43.5 66.7 %collective-permute-start.5 = (bf16[2,4,16,2048]{3,2,1,0:T(8,128)(2,1)}, bf16[2,4,16,2048]{3,2,1,0:T(8,128)(2,1)}, u32[]{:S(2)}, u32[]{:S(2)}) collective-permute-start(bf16[2,4,16,2048]{3,2,1,0:T(8,128)(2,1)} %get-tuple-element.63), channel_id=1, source_target_pairs={{0,64},{32,96},{64,0},{96,32},{1,65},{33,97},{65,1},{97,33},{2,66}... | collective-permute-start | bytes 1572872 | tf_op jit(solution)/shard_map/ppermute | solution.py:509
  43.9 66.4 %collective-permute-start.6 = (bf16[2,4,16,2048]{3,2,1,0:T(8,128)(2,1)}, bf16[2,4,16,2048]{3,2,1,0:T(8,128)(2,1)}, u32[]{:S(2)}, u32[]{:S(2)}) collective-permute-start(bf16[2,4,16,2048]{3,2,1,0:T(8,128)(2,1)} %get-tuple-element.64), channel_id=1, source_target_pairs={{0,64},{32,96},{64,0},{96,32},{1,65},{33,97},{65,1},{97,33},{2,66}... | collective-permute-start | bytes 1572872 | tf_op jit(solution)/shard_map/ppermute | solution.py:509
  101.3 49.7 %all-to-all-start.1 = ((bf16[32,4,3,32,128]{4,3,2,1,0:T(8,128)(2,1)}), bf16[32,4,3,32,128]{4,3,2,1,0:T(8,128)(2,1)S(1)}, u32[]{:S(2)}, u32[]{:S(2)}) async-start(bf16[32,4,3,32,128]{4,3,2,1,0:T(8,128)(2,1)} %spatial_grads.1), calls=%async_computation.1 | async-start | bytes 6291456 | tf_op jit(solution)/shard_map/all_to_all | solution.py:530
  110.2 0.6 copy-start.3
  118.5 3.8 %collective-permute-start.7 = (bf16[3,4,32,2048]{3,2,1,0:T(8,128)(2,1)}, bf16[3,4,32,2048]{3,2,1,0:T(8,128)(2,1)}, u32[]{:S(2)}, u32[]{:S(2)}) collective-permute-start(bf16[3,4,32,2048]{3,2,1,0:T(8,128)(2,1)} %get-tuple-element.65), channel_id=1, source_target_pairs={{0,32},{32,0},{64,96},{96,64},{1,33},{33,1},{65,97},{97,65},{2,34}... | collective-permute-start | bytes 4718600 | tf_op jit(solution)/shard_map/ppermute | solution.py:515

commit v4 on v3

--- a/solution.py
+++ b/solution.py
@@ -1,4 +1,3 @@
-import functools
 import math
 
 import jax
@@ -94,40 +93,30 @@
     )(array)
 
 
-def spatial_kernel(block, ref, out):
+def spatial_kernel(ref, out):
     parts, _, _, rows, _ = ref.shape
-    total = parts * rows
-    query, key, value, grad = (ref[:, 0, a].reshape(total, HEAD_DIM) for a in range(4))
-    key_t = key.T
-    dkey = dvalue = None
-    for start in range(0, total, block):
-        q = query[start : start + block]
-        g = grad[start : start + block]
-        scores = dot(key, q, ((1,), (1,)))
-        peak = jnp.max(scores, axis=0, keepdims=True)
-        e = jnp.exp2((scores - peak) * (SCALE * LOG2E))
-        pgrad = dot(value, g, ((1,), (1,)))
-        probs = e * (1.0 / jnp.sum(e, axis=0, keepdims=True))
-        weights = probs.astype(jnp.bfloat16)
-        term = probs * pgrad
-        delta = jnp.sum(term, axis=0, keepdims=True)
-        sgrad = (term - probs * delta).astype(jnp.bfloat16)
-        dq = dot(key_t, sgrad, ((1,), (0,))).T * SCALE
-        out[start // rows : (start + block) // rows, 0, 0] = dq.astype(out.dtype).reshape(
-            block // rows, rows, HEAD_DIM
-        )
-        dk = dot(sgrad, q, ((1,), (0,)))
-        dv = dot(weights, g, ((1,), (0,)))
-        dkey = dk if dkey is None else dkey + dk
-        dvalue = dv if dvalue is None else dvalue + dv
-    out[:, 0, 1] = (dkey * SCALE).astype(out.dtype).reshape(parts, rows, HEAD_DIM)
-    out[:, 0, 2] = dvalue.astype(out.dtype).reshape(parts, rows, HEAD_DIM)
+    query, key, value, grad = (ref[:, 0, a].reshape(parts * rows, HEAD_DIM) for a in range(4))
+    scores = dot(query, key, ((1,), (1,)))
+    peak = jnp.max(scores, axis=1, keepdims=True)
+    e = jnp.exp2((scores - peak) * (SCALE * LOG2E))
+    pgrad = dot(grad, value, ((1,), (1,)))
+    probs = e * (1.0 / jnp.sum(e, axis=1, keepdims=True))
+    term = probs * pgrad
+    delta = jnp.sum(term, axis=1, keepdims=True)
+    sgrad = (term - probs * delta).astype(jnp.bfloat16)
+    results = (
+        dot(sgrad, key, ((1,), (0,))) * SCALE,
+        dot(query.T, sgrad, ((1,), (0,))).T * SCALE,
+        dot(grad.T, probs.astype(jnp.bfloat16), ((1,), (0,))).T,
+    )
+    for a, result in enumerate(results):
+        out[:, 0, a] = result.astype(out.dtype).reshape(parts, rows, HEAD_DIM)
 
 
 def spatial_grads(array):
     parts, frames, _, rows, _ = array.shape
     return pl.pallas_call(
-        functools.partial(spatial_kernel, min(1024, parts * rows)),
+        spatial_kernel,
         grid=(frames,),
         in_specs=[pl.BlockSpec((parts, 1, 4, rows, HEAD_DIM), lambda f: (0, f, 0, 0, 0))],
         out_specs=pl.BlockSpec((parts, 1, 3, rows, HEAD_DIM), lambda f: (0, f, 0, 0, 0)),
@@ -141,11 +130,12 @@
 GROUP = 16
 CHIPS = [(t, t ^ 2) for t in range(4)]
 CORES = [(t, t ^ 1) for t in range(4)]
+RETURNS = [(2, 0), (3, 1)]
 CROSSED = [(t, t ^ 3) for t in range(4)]
 NEVER = -1e30
 
 
-def ship_kernel(query, key, value, grad, same, other, swap, sems):
+def ship_kernel(query, key, value, grad, same, other, swap, held, held_swap, sems, out_sems):
     member = lax.axis_index("tm")
     chip, core = member // 2, member % 2
     width = same.shape[-1]
@@ -154,23 +144,30 @@
 
     def copy_all(first, second, row):
         rows = pl.ds(row, GROUP)
-        pairs = [
-            (ref.at[:, rows, columns], out.at[a])
-            for columns, out in ((other_columns, other), (own_columns, same))
+        steps = [
+            (ref.at[:, rows, columns], held.at[i, a], out.at[a])
+            for i, (columns, out) in enumerate(((other_columns, other), (own_columns, same)))
             for a, ref in enumerate((first, second))
         ]
-        pairs += [
-            (ref.at[:, :, other_columns], swap.at[a])
+        steps += [
+            (ref.at[:, :, other_columns], held_swap.at[a], swap.at[a])
             for a, ref in enumerate((query, key, value, grad))
         ]
-        copies = [
-            pltpu.make_async_copy(source, target, sems.at[i])
-            for i, (source, target) in enumerate(pairs)
-        ]
-        for copy in copies:
-            copy.start()
-        for copy in copies:
-            copy.wait()
+        loads = [
+            pltpu.make_async_copy(source, middle, sems.at[i])
+            for i, (source, middle, _) in enumerate(steps)
+        ]
+        stores = [
+            pltpu.make_async_copy(middle, target, out_sems.at[i])
+            for i, (_, middle, target) in enumerate(steps)
+        ]
+        for load in loads:
+            load.start()
+        for load, store in zip(loads, stores):
+            load.wait()
+            store.start()
+        for store in stores:
+            store.wait()
 
     @pl.when(chip == 0)
     def _():
@@ -189,9 +186,14 @@
     return pl.pallas_call(
         ship_kernel,
         in_specs=[pl.BlockSpec(memory_space=pltpu.HBM)] * 4,
-        out_specs=[pl.BlockSpec(memory_space=pltpu.VMEM)] * 3,
+        out_specs=[pl.BlockSpec(memory_space=pltpu.HBM)] * 3,
         out_shape=[shape, shape, swap_shape],
-        scratch_shapes=[pltpu.SemaphoreType.DMA((8,))],
+        scratch_shapes=[
+            pltpu.VMEM((2,) + shape.shape, shape.dtype),
+            pltpu.VMEM(swap_shape.shape, shape.dtype),
+            pltpu.SemaphoreType.DMA((8,)),
+            pltpu.SemaphoreType.DMA((8,)),
+        ],
         compiler_params=PARAMS,
         cost_estimate=cost(2),
         name="ship_pack",
@@ -249,17 +251,23 @@
 
 def stats_kernel(place, query, key, value, grad, swapped, out):
     mask = frame_mask(place[0] % 2, 2 * query.shape[0], True)
-    for h in range(query.shape[-1] // HEAD_DIM):
+    heads = query.shape[-1] // HEAD_DIM
+    for h in range(heads):
         columns = pl.ds(h * HEAD_DIM, HEAD_DIM)
         rows = [
             gather_rows(ref, swapped.at[a], 0, columns)
             for a, ref in enumerate((query, key, value, grad))
         ]
-        out[h] = stats_rows(block_stats(mask, *rows)[1])
-
-
-def stats_rows(stats):
-    return jnp.concatenate(stats + (jnp.zeros((5, stats[0].shape[1]), jnp.float32),), axis=0)
+        write_stats(out, h, heads, block_stats(mask, *rows)[1])
+
+
+def write_stats(out, h, heads, stats):
+    for i, row in enumerate(stats):
+        out[i, pl.ds(pl.program_id(0) * heads + h, 1)] = row
+
+
+def read_stats(far, h, heads):
+    return tuple(far[i, pl.ds(pl.program_id(0) * heads + h, 1)] for i in range(3))
 
 
 def choose(first, when_first, when_second):
@@ -279,13 +287,14 @@
 
 def early_kernel(
     place, query, key, value, grad, swapped, late_key, late_value, late_swapped, same, other, far,
-    early, early_other, near, near_other, back, back_other, stats_out,
+    early, early_other, near, near_other, back, back_value, stats_out,
 ):
     core, first = place[0] % 2, place[0] < 2
     frames = query.shape[0]
     causal = frame_mask(core, 2 * frames, True)
     cross = frame_mask(core, 2 * frames, False)
-    for h in range(query.shape[-1] // HEAD_DIM):
+    heads = query.shape[-1] // HEAD_DIM
+    for h in range(heads):
         columns = pl.ds(h * HEAD_DIM, HEAD_DIM)
         rows = [
             gather_rows(ref, swapped.at[a], 0, columns)
@@ -302,10 +311,10 @@
             jnp.where(first, late[1], sent[1]),
             jnp.where(first, sent[1], rows[3]),
         ]
-        received = tuple(far[h, i : i + 1] for i in range(3))
+        received = read_stats(far, h, heads)
         products, stats = block_stats(causal, *rows)
         cross_products, cross_stats = block_stats(cross, *crossed)
-        stats_out[h] = stats_rows(cross_stats)
+        write_stats(stats_out, h, heads, cross_stats)
         none = no_stats(2 * frames * GROUP)
         out = block_grads(
             products, stats, choose(first, none, cross_stats), rows[0], rows[1], rows[3]
@@ -324,27 +333,27 @@
         place_rows(early, early_other, 2, columns, out[2])
         place_rows(near, near_other, 0, columns, cross_out[1])
         place_rows(near, near_other, 1, columns, cross_out[2])
-        place_rows(
-            back, back_other, 0, columns, jnp.where(first, cross_out[0], cross_out[1])
-        )
-        place_rows(back, back_other, 1, columns, jnp.where(first, zero, cross_out[2]))
+        mixed = jnp.where(first, cross_out[0], cross_out[1])
+        place_rows(back.at[0:1], back.at[1:2], 0, columns, mixed)
+        place_rows(back_value.at[0:1], back_value.at[1:2], 0, columns, cross_out[2])
 
 
 def late_kernel(
     place, query, key, value, grad, swapped, far, early, early_other, near, near_other, back,
-    back_other, dquery, dkey, dvalue, theirs,
+    back_value, dquery, dkey, dvalue, theirs,
 ):
     core, first = place[0] % 2, place[0] < 2
     frames = query.shape[0]
     causal = frame_mask(core, 2 * frames, True)
     early_rows, late_rows = pl.ds(0, GROUP), pl.ds(GROUP, GROUP)
-    for h in range(query.shape[-1] // HEAD_DIM):
+    heads = query.shape[-1] // HEAD_DIM
+    for h in range(heads):
         columns = pl.ds(h * HEAD_DIM, HEAD_DIM)
         rows = [
             gather_rows(ref, swapped.at[a], 0, columns)
             for a, ref in enumerate((query, key, value, grad))
         ]
-        received = tuple(far[h, i : i + 1] for i in range(3))
+        received = read_stats(far, h, heads)
         products, stats = block_stats(causal, *rows)
         none = no_stats(2 * frames * GROUP)
         late = [
@@ -354,15 +363,15 @@
             )
         ]
 
-        def write(outs, side, near, back, early):
+        def write(outs, side, near, early):
             zero = jnp.zeros((frames, GROUP, HEAD_DIM), jnp.float32)
-            back = [back[a, :, :, columns].astype(jnp.float32) for a in range(2)]
+            far_rows = [ref[side, :, :, columns].astype(jnp.float32) for ref in (back, back_value)]
             near = [near[a, :, :, columns].astype(jnp.float32) for a in range(2)]
             early = [early[a, :, :, columns].astype(jnp.float32) for a in range(3)]
-            early[1] += jnp.where(first, back[0], zero)
-            early[2] += jnp.where(first, back[1], zero)
+            early[1] += jnp.where(first, far_rows[0], zero)
+            early[2] += jnp.where(first, far_rows[1], zero)
             more = (
-                jnp.where(first, zero, back[0]),
+                jnp.where(first, zero, far_rows[0]),
                 jnp.where(first, near[0], zero),
                 jnp.where(first, near[1], zero),
             )
@@ -370,8 +379,8 @@
                 out[:, early_rows, columns] = early[a].astype(jnp.bfloat16)
                 out[:, late_rows, columns] = (late[a][side] + more[a]).astype(jnp.bfloat16)
 
-        write((dquery, dkey, dvalue), 0, near, back, early)
-        write([theirs.at[a] for a in range(3)], 1, near_other, back_other, early_other)
+        write((dquery, dkey, dvalue), 0, near, early)
+        write([theirs.at[a] for a in range(3)], 1, near_other, early_other)
 
 
 def finish_kernel(place, swapped, *refs):
@@ -402,13 +411,11 @@
             (count, self.frames, rows, self.half // steps), lambda j, p: (0, 0, row, j)
         )
 
-    def stats(self, steps):
-        return pl.BlockSpec(
-            (self.heads // steps, 8, 2 * self.frames * GROUP), lambda j, p: (j, 0, 0)
-        )
+    def stats(self):
+        return pl.BlockSpec(self.stats_shape().shape, lambda j, p: (0, 0, 0))
 
     def stats_shape(self):
-        return jax.ShapeDtypeStruct((self.heads, 8, 2 * self.frames * GROUP), jnp.float32)
+        return jax.ShapeDtypeStruct((3, self.heads, 2 * self.frames * GROUP), jnp.float32)
 
     def shape(self, count, rows):
         return jax.ShapeDtypeStruct((count, self.frames, rows, self.half), jnp.bfloat16)
@@ -433,7 +440,7 @@
             "temporal_stats",
             5,
             [self.own(STATS_STEPS, 1)] * 4 + [self.part(STATS_STEPS, 4, GROUP, 1)],
-            self.stats(STATS_STEPS),
+            self.stats(),
             self.stats_shape(),
             self.arrays + (swapped,),
         )
@@ -449,8 +456,8 @@
             + [self.own(EARLY_STEPS, 1)] * 2
             + [self.part(EARLY_STEPS, 4, GROUP, 1)]
             + [self.part(EARLY_STEPS, 2, GROUP)] * 2
-            + [self.stats(EARLY_STEPS)],
-            [self.part(EARLY_STEPS, 3, GROUP)] * 2 + [self.part(EARLY_STEPS, 2, GROUP)] * 4 + [self.stats(EARLY_STEPS)],
+            + [self.stats()],
+            [self.part(EARLY_STEPS, 3, GROUP)] * 2 + [self.part(EARLY_STEPS, 2, GROUP)] * 4 + [self.stats()],
             [self.shape(3, GROUP)] * 2 + [self.shape(2, GROUP)] * 4 + [self.stats_shape()],
             self.arrays
             + (swapped, self.arrays[1], self.arrays[2], swapped, same, other, far),
@@ -467,7 +474,7 @@
             "temporal_late",
             LATE_COST,
             [self.own(LATE_STEPS, 1)] * 4
-            + [self.part(LATE_STEPS, 4, GROUP, 1), self.stats(LATE_STEPS)]
+            + [self.part(LATE_STEPS, 4, GROUP, 1), self.stats()]
             + [self.part(LATE_STEPS, 3, GROUP)] * 2
             + [self.part(LATE_STEPS, 2, GROUP)] * 4,
             [out] * 3 + [self.part(LATE_STEPS, 3, self.positions)],
@@ -523,13 +530,13 @@
     packed, far = lax.optimization_barrier((pack_heads(*spatial), work.late_stats(swapped)))
     far = chips(far)
     packed = lax.all_to_all(packed, "space", 0, 0, tiled=True)
-    early, early_other, near, near_other, back, back_other, far = work.early_grads(
+    early, early_other, near, near_other, back, back_value, far = work.early_grads(
         swapped, same, other, far
     )
-    far, back_other, back = chips(far), chips(back_other), chips(back)
+    far, back, back_value = chips(far), chips(back), lax.ppermute(back_value, "tm", RETURNS)
     packed = lax.all_to_all(spatial_grads(packed), "space", 0, 0, tiled=True)
     *outs, theirs = work.late_grads(
-        swapped, far, early, early_other, near, near_other, back, back_other
+        swapped, far, early, early_other, near, near_other, back, back_value
     )
     outs = work.finish(outs, cores(theirs))
     outs = tuple(unpack_heads(packed)) + tuple(outs)

time: 154 us -> 150 us (0.974)
  Pallas kernels: 50.9 us -> 47.2 us
    pallas_call x1, Pallas kernels: 18 us -> 15 us  [spatial_grads(): pl.pallas_call(spatial_kernel, grid=(frames,), in_specs=[pl.BlockSpec((pa...]
    ppermute x5 -> x4, starting transfers between devices: 7.19 us -> 5.57 us  [chips(): return lax.ppermute(array, 'tm', CHIPS)]
  transfers between devices with their start and end apart: 10 -> 10, of which waited for: 5 -> 5; matrix products, arithmetic and copies ran while one was open for 0% -> 0% of each run, Pallas kernels for 29% -> 28%
where the time goes in v4:
time: 150 us; the launch traced here: 149 us
  waiting for transfers between devices  71.7 us (48%)
  Pallas kernels  47.2 us (31%)
  starting transfers between devices  26.9 us (18%)
  local copies, waits for them, and re-layouts  2.58 us (2%)
    all_to_all x1, waiting for transfers between devices, local(): packed = lax.all_to_all(packed, 'space', 0, 0, tiled=True)  38.2 us
    all_to_all x1, waiting for transfers between devices, local(): packed = lax.all_to_all(spatial_grads(packed), 'space', 0, 0, tiled=True)  25 us
    pallas_call x4, Pallas kernels, call(): pl.pallas_call(kernel, grid_spec=pltpu.PrefetchScalarGridSpec(num_scalar_...  23.4 us
    pallas_call x1, Pallas kernels, spatial_grads(): pl.pallas_call(spatial_kernel, grid=(frames,), in_specs=[pl.BlockSpec((pa...  15 us
    all_to_all x1, starting transfers between devices, local(): packed = lax.all_to_all(packed, 'space', 0, 0, tiled=True)  10.6 us
    all_to_all x1, starting transfers between devices, local(): packed = lax.all_to_all(spatial_grads(packed), 'space', 0, 0, tiled=True)  9.17 us
    ppermute x4, starting transfers between devices, chips(): return lax.ppermute(array, 'tm', CHIPS)  5.57 us
    ppermute x2, waiting for transfers between devices, cores(): return lax.ppermute(array, 'tm', CORES)  3.74 us
  transfers between devices with their start and end apart: 10, of which 5 were waited for; matrix products, arithmetic and copies ran while one was open for 0% of the time, Pallas kernels for 28%

profile of v4, /device:TPU:0, one launch (start us, length us, event | category | flops | bytes accessed | tf_op | source)
XLA Modules:
  0.0 149.1 jit_solution(10984225228014426385)
XLA Ops:
  0.6 2.9 %ship_pack.1 = (bf16[2,4,16,2048]{3,2,1,0:T(8,128)(2,1)}, bf16[2,4,16,2048]{3,2,1,0:T(8,128)(2,1)}, bf16[4,4,32,2048]{3,2,1,0:T(8,128)(2,1)}) custom-call(bf16[4,32,4096]{2,1,0:T(8,128)(2,1)} %bitcast.19, bf16[4,32,4096]{2,1,0:T(8,128)(2,1)} %bitcast.23, bf16[4,32,4096]{2,1,0:T(8,128)(2,1)} %bitcast.28, bf16[4,32,4096]{2,1,0:T(8,128)(2,1)} %bitcast.33), custom_call_target="tpu_custom_call" | custom-call | flops 2000000000 | tf_op jit(solution)/shard_map/ship_pack/pallas_call | solution.py:186
  3.5 0.1 collective-permute-start
  3.6 1.8 %collective-permute-start.1 = (bf16[2,4,16,2048]{3,2,1,0:T(8,128)(2,1)}, bf16[2,4,16,2048]{3,2,1,0:T(8,128)(2,1)S(1)}, u32[]{:S(2)}, u32[]{:S(2)}) collective-permute-start(bf16[2,4,16,2048]{3,2,1,0:T(8,128)(2,1)} %get-tuple-element.55), channel_id=1, source_target_pairs={{0,64},{32,96},{64,0},{96,32},{1,65},{33,97},{65,1},{97,33},{2,66}... | collective-permute-start | bytes 1572872 | tf_op jit(solution)/shard_map/ppermute | solution.py:516
  5.4 0.1 collective-permute-start.2
  5.5 3.4 %pack_heads.1 = bf16[32,4,4,32,128]{4,3,2,1,0:T(8,128)(2,1)} custom-call(bf16[4,32,4096]{2,1,0:T(8,128)(2,1)} %bitcast.15, bf16[4,32,4096]{2,1,0:T(8,128)(2,1)} %bitcast.16, bf16[4,32,4096]{2,1,0:T(8,128)(2,1)} %bitcast.17, bf16[4,32,4096]{2,1,0:T(8,128)(2,1)} %bitcast.18), custom_call_target="tpu_custom_call" | custom-call | flops 5000000000 | tf_op jit(solution)/shard_map/pack_heads/pallas_call | solution.py:55
  8.9 0.0 collective-permute-done.swapped.late_swapped
  8.9 0.0 copy-start
  8.9 1.4 copy-done
  10.3 3.0 %temporal_stats.1 = f32[3,16,128]{2,1,0:T(8,128)} custom-call(s32[1]{0:T(128)} %bitcast.8.place, bf16[4,32,4096]{2,1,0:T(8,128)(2,1)} %bitcast.20, bf16[4,32,4096]{2,1,0:T(8,128)(2,1)} %bitcast.24, bf16[4,32,4096]{2,1,0:T(8,128)(2,1)} %bitcast.29, bf16[4,32,4096]{2,1,0:T(8,128)(2,1)} %bitcast.34, bf16[4,4,32,2048]{3,2,1,0:T(8,128)(2,1)} %copy-done), custom_call_target="tpu_custom_call" | custom-call | flops 5000000000 | tf_op jit(solution)/shard_map/temporal_stats/pallas_call | solution.py:424
  13.4 1.7 %collective-permute-start.3 = (f32[3,16,128]{2,1,0:T(8,128)}, f32[3,16,128]{2,1,0:T(8,128)S(1)}, u32[]{:S(2)}, u32[]{:S(2)}) collective-permute-start(f32[3,16,128]{2,1,0:T(8,128)} %temporal_stats.1), channel_id=1, source_target_pairs={{0,64},{32,96},{64,0},{96,32},{1,65},{33,97},{65,1},{97,33},{2,66}... | collective-permute-start | bytes 73736 | tf_op jit(solution)/shard_map/ppermute | solution.py:516
  15.1 10.6 %all-to-all-start = ((bf16[32,4,4,32,128]{4,3,2,1,0:T(8,128)(2,1)}), bf16[32,4,4,32,128]{4,3,2,1,0:T(8,128)(2,1)}, u32[]{:S(2)}, u32[]{:S(2)}) async-start(bf16[32,4,4,32,128]{4,3,2,1,0:T(8,128)(2,1)} %pack_heads.1), calls=%async_computation | async-start | bytes 8388608 | tf_op jit(solution)/shard_map/all_to_all | solution.py:532
  25.7 0.0 collective-permute-done.1.same
  25.7 0.0 copy-start.1
  25.7 3.5 %collective-permute-done.2.other = bf16[2,4,16,2048]{3,2,1,0:T(8,128)(2,1)S(1)} collective-permute-done((bf16[2,4,16,2048]{3,2,1,0:T(8,128)(2,1)}, bf16[2,4,16,2048]{3,2,1,0:T(8,128)(2,1)S(1)}, u32[]{:S(2)}, u32[]{:S(2)}) %collective-permute-start.2) | collective-permute-done | bytes 524320 | tf_op jit(solution)/shard_map/ppermute | solution.py:519
  29.2 0.0 copy-start.2
  29.2 1.2 collective-permute-done.3.far
  30.4 0.0 copy-done.1
  30.4 0.0 copy-done.2
  30.4 0.0 copy-start.4
  30.4 0.6 copy-done.4
  31.0 9.1 %temporal_early.1 = (bf16[3,4,16,2048]{3,2,1,0:T(8,128)(2,1)}, bf16[3,4,16,2048]{3,2,1,0:T(8,128)(2,1)}, bf16[2,4,16,2048]{3,2,1,0:T(8,128)(2,1)}, bf16[2,4,16,2...) custom-call(s32[1]{0:T(128)} %bitcast.8.place, ...), custom_call_target="tpu_custom_call" | custom-call | flops 99999997952 | tf_op jit(solution)/shard_map/temporal_early/pallas_call | solution.py:424
  40.1 1.8 %collective-permute-start.4 = (f32[3,16,128]{2,1,0:T(8,128)}, f32[3,16,128]{2,1,0:T(8,128)S(1)}, u32[]{:S(2)}, u32[]{:S(2)}) collective-permute-start(f32[3,16,128]{2,1,0:T(8,128)} %get-tuple-element.58), channel_id=1, source_target_pairs={{0,64},{32,96},{64,0},{96,32},{1,65},{33,97},{65,1},{97,33},{2,66}... | collective-permute-start | bytes 73736 | tf_op jit(solution)/shard_map/ppermute | solution.py:516
  41.9 0.3 collective-permute-start.5
  42.2 1.3 collective-permute-start.6
  43.5 38.2 %all-to-all-done.ref = bf16[32,4,4,32,128]{4,3,2,1,0:T(8,128)(2,1)} async-done(((bf16[32,4,4,32,128]{4,3,2,1,0:T(8,128)(2,1)}), bf16[32,4,4,32,128]{4,3,2,1,0:T(8,128)(2,1)}, u32[]{:S(2)}, u32[]{:S(2)}) %all-to-all-start) | async-done | bytes 4194336 | tf_op jit(solution)/shard_map/all_to_all | solution.py:532
  81.7 15.0 %spatial_grads.1 = bf16[32,4,3,32,128]{4,3,2,1,0:T(8,128)(2,1)} custom-call(bf16[32,4,4,32,128]{4,3,2,1,0:T(8,128)(2,1)} %all-to-all-done.ref), custom_call_target="tpu_custom_call" | custom-call | flops 20000000000 | tf_op jit(solution)/shard_map/spatial_grads/pallas_call | solution.py:118
  96.8 9.2 %all-to-all-start.1 = ((bf16[32,4,3,32,128]{4,3,2,1,0:T(8,128)(2,1)}), bf16[32,4,3,32,128]{4,3,2,1,0:T(8,128)(2,1)S(1)}, u32[]{:S(2)}, u32[]{:S(2)}) async-start(bf16[32,4,3,32,128]{4,3,2,1,0:T(8,128)(2,1)} %spatial_grads.1), calls=%async_computation.1 | async-start | bytes 6291456 | tf_op jit(solution)/shard_map/all_to_all | solution.py:537
  105.9 0.0 collective-permute-done.4.far
  105.9 0.0 copy-start.3
  106.0 0.0 collective-permute-done.5.back
  106.0 0.0 collective-permute-done.6.back_value
  106.0 0.6 copy-done.3
  106.6 7.7 %temporal_late.1 = (bf16[4,32,4096]{2,1,0:T(8,128)(2,1)}, bf16[4,32,4096]{2,1,0:T(8,128)(2,1)}, bf16[4,32,4096]{2,1,0:T(8,128)(2,1)}, bf16[3,4,32,2048]{3,2,1,0:T(8,128)(2,1)}) custom-call(s32[1]{0:T(128)} %bitcast.8.place, bf16[4,32,4096]{2,1,0:T(8,128)(2,1)} %bitcast.22, bf16[4,32,4096]{2,1,0:T(8,128)(2,1)} %bitcast.27, bf16[4,32,4096]{2,1,0:T(8,128)(2,1)} %bitcast.32, ...), custom_call_target="tpu_custom_call" | custom-call | flops 99999997952 | tf_op jit(solution)/shard_map/temporal_late/pallas_call | solution.py:424
  114.2 0.1 collective-permute-start.7
  114.3 3.7 %collective-permute-done.7.swapped = bf16[3,4,32,2048]{3,2,1,0:T(8,128)(2,1)} collective-permute-done((bf16[3,4,32,2048]{3,2,1,0:T(8,128)(2,1)}, bf16[3,4,32,2048]{3,2,1,0:T(8,128)(2,1)}, u32[]{:S(2)}, u32[]{:S(2)}) %collective-permute-start.7) | collective-permute-done | bytes 1572896 | tf_op jit(solution)/shard_map/ppermute | solution.py:522
  118.1 3.6 %temporal_finish.1 = (bf16[4,32,4096]{2,1,0:T(8,128)(2,1)}, bf16[4,32,4096]{2,1,0:T(8,128)(2,1)}, bf16[4,32,4096]{2,1,0:T(8,128)(2,1)}) custom-call(s32[1]{0:T(128)} %bitcast.8.place, bf16[3,4,32,2048]{3,2,1,0:T(8,128)(2,1)} %collective-permute-done.7.swapped, ...), custom_call_target="tpu_custom_call", output_to_operand_aliasing={{0}: (2, {}), {1}: (3, {}), {2}: (4, {})} | custom-call | flops 3000000000 | tf_op jit(solution)/shard_map/temporal_finish/pallas_call | solution.py:424
  121.6 25.0 %all-to-all-done.1.ref = bf16[32,4,3,32,128]{4,3,2,1,0:T(8,128)(2,1)S(1)} async-done(((bf16[32,4,3,32,128]{4,3,2,1,0:T(8,128)(2,1)}), bf16[32,4,3,32,128]{4,3,2,1,0:T(8,128)(2,1)S(1)}, u32[]{:S(2)}, u32[]{:S(2)}) %all-to-all-start.1) | async-done | bytes 3145760 | tf_op jit(solution)/shard_map/all_to_all | solution.py:537
  146.7 2.5 %unpack_heads.1 = (bf16[4,32,4096]{2,1,0:T(8,128)(2,1)}, bf16[4,32,4096]{2,1,0:T(8,128)(2,1)}, bf16[4,32,4096]{2,1,0:T(8,128)(2,1)}) custom-call(bf16[32,4,3,32,128]{4,3,2,1,0:T(8,128)(2,1)S(1)} %all-to-all-done.1.ref), custom_call_target="tpu_custom_call" | custom-call | flops 4000000000 | tf_op jit(solution)/shard_map/unpack_heads/pallas_call | solution.py:82
Async XLA Ops:
  3.5 5.4 %collective-permute-start = (bf16[4,4,32,2048]{3,2,1,0:T(8,128)(2,1)}, bf16[4,4,32,2048]{3,2,1,0:T(8,128)(2,1)S(1)}, u32[]{:S(2)}, u32[]{:S(2)}) collective-permute-start(bf16[4,4,32,2048]{3,2,1,0:T(8,128)(2,1)} %get-tuple-element.50), channel_id=1, source_target_pairs={{0,32},{32,0},{64,96},{96,64},{1,33},{33,1},{65,97},{97,65},{2,34}... | collective-permute-start | bytes 6291464 | tf_op jit(solution)/shard_map/ppermute | solution.py:522
  3.6 22.1 %collective-permute-start.1 = (bf16[2,4,16,2048]{3,2,1,0:T(8,128)(2,1)}, bf16[2,4,16,2048]{3,2,1,0:T(8,128)(2,1)S(1)}, u32[]{:S(2)}, u32[]{:S(2)}) collective-permute-start(bf16[2,4,16,2048]{3,2,1,0:T(8,128)(2,1)} %get-tuple-element.55), channel_id=1, source_target_pairs={{0,64},{32,96},{64,0},{96,32},{1,65},{33,97},{65,1},{97,33},{2,66}... | collective-permute-start | bytes 1572872 | tf_op jit(solution)/shard_map/ppermute | solution.py:516
  5.4 23.8 %collective-permute-start.2 = (bf16[2,4,16,2048]{3,2,1,0:T(8,128)(2,1)}, bf16[2,4,16,2048]{3,2,1,0:T(8,128)(2,1)S(1)}, u32[]{:S(2)}, u32[]{:S(2)}) collective-permute-start(bf16[2,4,16,2048]{3,2,1,0:T(8,128)(2,1)} %get-tuple-element.56), channel_id=1, source_target_pairs={{0,96},{32,64},{64,32},{96,0},{1,97},{33,65},{65,33},{97,1},{2,98}... | collective-permute-start | bytes 1572872 | tf_op jit(solution)/shard_map/ppermute | solution.py:519
  8.9 1.4 copy-start
  13.4 17.0 %collective-permute-start.3 = (f32[3,16,128]{2,1,0:T(8,128)}, f32[3,16,128]{2,1,0:T(8,128)S(1)}, u32[]{:S(2)}, u32[]{:S(2)}) collective-permute-start(f32[3,16,128]{2,1,0:T(8,128)} %temporal_stats.1), channel_id=1, source_target_pairs={{0,64},{32,96},{64,0},{96,32},{1,65},{33,97},{65,1},{97,33},{2,66}... | collective-permute-start | bytes 73736 | tf_op jit(solution)/shard_map/ppermute | solution.py:516
  15.1 66.7 %all-to-all-start = ((bf16[32,4,4,32,128]{4,3,2,1,0:T(8,128)(2,1)}), bf16[32,4,4,32,128]{4,3,2,1,0:T(8,128)(2,1)}, u32[]{:S(2)}, u32[]{:S(2)}) async-start(bf16[32,4,4,32,128]{4,3,2,1,0:T(8,128)(2,1)} %pack_heads.1), calls=%async_computation | async-start | bytes 8388608 | tf_op jit(solution)/shard_map/all_to_all | solution.py:532
  25.7 4.7 %copy-start.1 = (bf16[2,4,16,2048]{3,2,1,0:T(8,128)(2,1)}, bf16[2,4,16,2048]{3,2,1,0:T(8,128)(2,1)S(1)}, u32[]{:S(2)}) copy-start(bf16[2,4,16,2048]{3,2,1,0:T(8,128)(2,1)S(1)} %collective-permute-done.1.same) | copy-start | bytes 1572868
  29.2 1.2 copy-start.2
  30.4 0.6 copy-start.4
  40.1 65.8 %collective-permute-start.4 = (f32[3,16,128]{2,1,0:T(8,128)}, f32[3,16,128]{2,1,0:T(8,128)S(1)}, u32[]{:S(2)}, u32[]{:S(2)}) collective-permute-start(f32[3,16,128]{2,1,0:T(8,128)} %get-tuple-element.58), channel_id=1, source_target_pairs={{0,64},{32,96},{64,0},{96,32},{1,65},{33,97},{65,1},{97,33},{2,66}... | collective-permute-start | bytes 73736 | tf_op jit(solution)/shard_map/ppermute | solution.py:516
  41.9 64.1 %collective-permute-start.5 = (bf16[2,4,16,2048]{3,2,1,0:T(8,128)(2,1)}, bf16[2,4,16,2048]{3,2,1,0:T(8,128)(2,1)}, u32[]{:S(2)}, u32[]{:S(2)}) collective-permute-start(bf16[2,4,16,2048]{3,2,1,0:T(8,128)(2,1)} %get-tuple-element.63), channel_id=1, source_target_pairs={{0,64},{32,96},{64,0},{96,32},{1,65},{33,97},{65,1},{97,33},{2,66}... | collective-permute-start | bytes 1572872 | tf_op jit(solution)/shard_map/ppermute | solution.py:516
  42.2 63.8 %collective-permute-start.6 = (bf16[2,4,16,2048]{3,2,1,0:T(8,128)(2,1)}, bf16[2,4,16,2048]{3,2,1,0:T(8,128)(2,1)}, u32[]{:S(2)}, u32[]{:S(2)}) collective-permute-start(bf16[2,4,16,2048]{3,2,1,0:T(8,128)(2,1)} %get-tuple-element.64), channel_id=1, source_target_pairs={{64,0},{96,32},{65,1},{97,33},{66,2},{98,34},{67,3},{99,35},{68,4}... | collective-permute-start | bytes 1572872 | tf_op jit(solution)/shard_map/ppermute | solution.py:536
  96.8 49.9 %all-to-all-start.1 = ((bf16[32,4,3,32,128]{4,3,2,1,0:T(8,128)(2,1)}), bf16[32,4,3,32,128]{4,3,2,1,0:T(8,128)(2,1)S(1)}, u32[]{:S(2)}, u32[]{:S(2)}) async-start(bf16[32,4,3,32,128]{4,3,2,1,0:T(8,128)(2,1)} %spatial_grads.1), calls=%async_computation.1 | async-start | bytes 6291456 | tf_op jit(solution)/shard_map/all_to_all | solution.py:537
  105.9 0.6 copy-start.3
  114.2 3.8 %collective-permute-start.7 = (bf16[3,4,32,2048]{3,2,1,0:T(8,128)(2,1)}, bf16[3,4,32,2048]{3,2,1,0:T(8,128)(2,1)}, u32[]{:S(2)}, u32[]{:S(2)}) collective-permute-start(bf16[3,4,32,2048]{3,2,1,0:T(8,128)(2,1)} %get-tuple-element.65), channel_id=1, source_target_pairs={{0,32},{32,0},{64,96},{96,64},{1,33},{33,1},{65,97},{97,65},{2,34}... | collective-permute-start | bytes 4718600 | tf_op jit(solution)/shard_map/ppermute | solution.py:522

commit v5 on v4

--- a/solution.py
+++ b/solution.py
@@ -130,44 +130,50 @@
 GROUP = 16
 CHIPS = [(t, t ^ 2) for t in range(4)]
 CORES = [(t, t ^ 1) for t in range(4)]
-RETURNS = [(2, 0), (3, 1)]
 CROSSED = [(t, t ^ 3) for t in range(4)]
 NEVER = -1e30
+
+
+def copy_through(steps, sems, out_sems):
+    loads = [
+        pltpu.make_async_copy(source, middle, sems.at[i])
+        for i, (source, middle, _) in enumerate(steps)
+    ]
+    stores = [
+        pltpu.make_async_copy(middle, target, out_sems.at[i])
+        for i, (_, middle, target) in enumerate(steps)
+    ]
+    for load in loads:
+        load.start()
+    for load, store in zip(loads, stores):
+        load.wait()
+        store.start()
+    for store in stores:
+        store.wait()
+
+
+def half_columns(core, width):
+    return pl.ds(pl.multiple_of(core * width, width), width)
 
 
 def ship_kernel(query, key, value, grad, same, other, swap, held, held_swap, sems, out_sems):
     member = lax.axis_index("tm")
     chip, core = member // 2, member % 2
     width = same.shape[-1]
-    own_columns = pl.ds(pl.multiple_of(core * width, width), width)
-    other_columns = pl.ds(pl.multiple_of((1 - core) * width, width), width)
+    own, others = half_columns(core, width), half_columns(1 - core, width)
 
     def copy_all(first, second, row):
         rows = pl.ds(row, GROUP)
         steps = [
             (ref.at[:, rows, columns], held.at[i, a], out.at[a])
-            for i, (columns, out) in enumerate(((other_columns, other), (own_columns, same)))
+            for i, (columns, out) in enumerate(((others, other), (own, same)))
             for a, ref in enumerate((first, second))
         ]
         steps += [
-            (ref.at[:, :, other_columns], held_swap.at[a], swap.at[a])
+            (ref.at[:, :, others], held_swap.at[a], swap.at[a])
             for a, ref in enumerate((query, key, value, grad))
         ]
-        loads = [
-            pltpu.make_async_copy(source, middle, sems.at[i])
-            for i, (source, middle, _) in enumerate(steps)
-        ]
-        stores = [
-            pltpu.make_async_copy(middle, target, out_sems.at[i])
-            for i, (_, middle, target) in enumerate(steps)
-        ]
-        for load in loads:
-            load.start()
-        for load, store in zip(loads, stores):
-            load.wait()
-            store.start()
-        for store in stores:
-            store.wait()
+        copy_through(steps, sems, out_sems)
 
     @pl.when(chip == 0)
     def _():
@@ -178,26 +184,27 @@
         copy_all(query, grad, GROUP)
 
 
-def ship_pack(query, key, value, grad):
-    frames, positions, width = query.shape
-    half = width // 2
-    shape = jax.ShapeDtypeStruct((2, frames, GROUP, half), query.dtype)
-    swap_shape = jax.ShapeDtypeStruct((4, frames, positions, half), query.dtype)
+def ship_pack(*arrays):
+    frames, positions, width = arrays[0].shape
+    dtype = arrays[0].dtype
+    shape = jax.ShapeDtypeStruct((2, frames, GROUP, width // 2), dtype)
+    swap_shape = jax.ShapeDtypeStruct((4, frames, positions, width // 2), dtype)
+    hbm = pl.BlockSpec(memory_space=pltpu.HBM)
     return pl.pallas_call(
         ship_kernel,
-        in_specs=[pl.BlockSpec(memory_space=pltpu.HBM)] * 4,
-        out_specs=[pl.BlockSpec(memory_space=pltpu.HBM)] * 3,
+        in_specs=[hbm] * 4,
+        out_specs=[hbm] * 3,
         out_shape=[shape, shape, swap_shape],
         scratch_shapes=[
-            pltpu.VMEM((2,) + shape.shape, shape.dtype),
-            pltpu.VMEM(swap_shape.shape, shape.dtype),
+            pltpu.VMEM((2,) + shape.shape, dtype),
+            pltpu.VMEM(swap_shape.shape, dtype),
             pltpu.SemaphoreType.DMA((8,)),
             pltpu.SemaphoreType.DMA((8,)),
         ],
         compiler_params=PARAMS,
         cost_estimate=cost(2),
         name="ship_pack",
-    )(query, key, value, grad)
+    )(*arrays)
 
 
 def frame_mask(core, chip_frames, causal):
@@ -234,33 +241,27 @@
     )
 
 
-def block_grads(products, stats, more, query, key, grad):
-    scores, pgrad = products
+def merged(stats, more):
     peak = jnp.maximum(stats[0], more[0])
     own_scale, more_scale = jnp.exp2(stats[0] - peak), jnp.exp2(more[0] - peak)
     inverse = 1.0 / (stats[1] * own_scale + more[1] * more_scale)
-    delta = (stats[2] * own_scale + more[2] * more_scale) * inverse
+    return peak, inverse, (stats[2] * own_scale + more[2] * more_scale) * inverse
+
+
+def block_weights(products, stats, more):
+    scores, pgrad = products
+    peak, inverse, delta = merged(stats, more)
     probs = jnp.exp2(scores - peak) * inverse
-    weights = probs.astype(jnp.bfloat16)
-    sgrad = (probs * (pgrad - delta)).astype(jnp.bfloat16)
+    return probs.astype(jnp.bfloat16), (probs * (pgrad - delta)).astype(jnp.bfloat16)
+
+
+def block_grads(weights, sgrad, query, key, grad):
     dquery = dot(sgrad, key, ((0,), (0,))) * SCALE
     dkey = dot(sgrad, query, ((1,), (0,))) * SCALE
     dvalue = dot(weights, grad, ((1,), (0,)))
     return dquery, dkey, dvalue
 
 
-def stats_kernel(place, query, key, value, grad, swapped, out):
-    mask = frame_mask(place[0] % 2, 2 * query.shape[0], True)
-    heads = query.shape[-1] // HEAD_DIM
-    for h in range(heads):
-        columns = pl.ds(h * HEAD_DIM, HEAD_DIM)
-        rows = [
-            gather_rows(ref, swapped.at[a], 0, columns)
-            for a, ref in enumerate((query, key, value, grad))
-        ]
-        write_stats(out, h, heads, block_stats(mask, *rows)[1])
-
-
 def write_stats(out, h, heads, stats):
     for i, row in enumerate(stats):
         out[i, pl.ds(pl.program_id(0) * heads + h, 1)] = row
@@ -285,102 +286,119 @@
     others[a, :, :, columns] = values[1]
 
 
+def load_rows(refs, swapped, columns):
+    return [gather_rows(ref, swapped.at[a], 0, columns) for a, ref in enumerate(refs)]
+
+
 def early_kernel(
-    place, query, key, value, grad, swapped, late_key, late_value, late_swapped, same, other, far,
-    early, early_other, near, near_other, back, back_value, stats_out,
+    place, query, key, value, grad, swapped, late_query, late_key, late_value, late_grad,
+    late_swapped, same, other, early, early_other, back, stats_out,
 ):
     core, first = place[0] % 2, place[0] < 2
     frames = query.shape[0]
     causal = frame_mask(core, 2 * frames, True)
     cross = frame_mask(core, 2 * frames, False)
+    none = no_stats(2 * frames * GROUP)
     heads = query.shape[-1] // HEAD_DIM
     for h in range(heads):
         columns = pl.ds(h * HEAD_DIM, HEAD_DIM)
-        rows = [
-            gather_rows(ref, swapped.at[a], 0, columns)
-            for a, ref in enumerate((query, key, value, grad))
-        ]
-        late = [
-            gather_rows(ref, late_swapped.at[a], 0, columns)
-            for a, ref in ((1, late_key), (2, late_value))
-        ]
+        rows = load_rows((query, key, value, grad), swapped, columns)
+        late = load_rows((late_query, late_key, late_value, late_grad), late_swapped, columns)
         sent = [gather_rows(same.at[a], other.at[a], 0, columns) for a in range(2)]
         crossed = [
             jnp.where(first, sent[0], rows[0]),
-            jnp.where(first, late[0], sent[0]),
-            jnp.where(first, late[1], sent[1]),
+            jnp.where(first, late[1], sent[0]),
+            jnp.where(first, late[2], sent[1]),
             jnp.where(first, sent[1], rows[3]),
         ]
-        received = read_stats(far, h, heads)
         products, stats = block_stats(causal, *rows)
         cross_products, cross_stats = block_stats(cross, *crossed)
-        write_stats(stats_out, h, heads, cross_stats)
-        none = no_stats(2 * frames * GROUP)
+        late_stats = block_stats(causal, *late)[1]
+        write_stats(stats_out, h, heads, choose(first, cross_stats, late_stats))
         out = block_grads(
-            products, stats, choose(first, none, cross_stats), rows[0], rows[1], rows[3]
-        )
-        cross_out = block_grads(
-            cross_products,
-            cross_stats,
-            choose(first, received, stats),
-            crossed[0],
-            crossed[1],
-            crossed[3],
-        )
-        zero = jnp.zeros_like(cross_out[0])
+            *block_weights(products, stats, choose(first, none, cross_stats)),
+            rows[0],
+            rows[1],
+            rows[3],
+        )
+        cross_weights, cross_sgrad = block_weights(
+            cross_products, cross_stats, choose(first, none, stats)
+        )
+        cross_out = block_grads(cross_weights, cross_sgrad, crossed[0], crossed[1], crossed[3])
+        mean_key = dot(cross_weights, crossed[1], ((0,), (0,))) * SCALE
+        zero = jnp.zeros_like(mean_key)
         place_rows(early, early_other, 0, columns, out[0] + jnp.where(first, zero, cross_out[0]))
         place_rows(early, early_other, 1, columns, out[1])
         place_rows(early, early_other, 2, columns, out[2])
-        place_rows(near, near_other, 0, columns, cross_out[1])
-        place_rows(near, near_other, 1, columns, cross_out[2])
-        mixed = jnp.where(first, cross_out[0], cross_out[1])
-        place_rows(back.at[0:1], back.at[1:2], 0, columns, mixed)
-        place_rows(back_value.at[0:1], back_value.at[1:2], 0, columns, cross_out[2])
+        returns = (
+            jnp.where(first, cross_out[0], cross_out[1]),
+            jnp.where(first, mean_key, cross_out[2]),
+        )
+        for a, values in enumerate(returns):
+            place_rows(back.at[0:2], back.at[2:4], a, columns, values)
 
 
 def late_kernel(
-    place, query, key, value, grad, swapped, far, early, early_other, near, near_other, back,
-    back_value, dquery, dkey, dvalue, theirs,
+    place, query, key, value, grad, swapped, same, other, far, early, early_other, back,
+    dquery, dkey, dvalue, theirs,
 ):
     core, first = place[0] % 2, place[0] < 2
     frames = query.shape[0]
     causal = frame_mask(core, 2 * frames, True)
+    cross = frame_mask(core, 2 * frames, False)
     early_rows, late_rows = pl.ds(0, GROUP), pl.ds(GROUP, GROUP)
+    none = no_stats(2 * frames * GROUP)
     heads = query.shape[-1] // HEAD_DIM
     for h in range(heads):
         columns = pl.ds(h * HEAD_DIM, HEAD_DIM)
-        rows = [
-            gather_rows(ref, swapped.at[a], 0, columns)
-            for a, ref in enumerate((query, key, value, grad))
-        ]
+        rows = load_rows((query, key, value, grad), swapped, columns)
+        sent = [gather_rows(same.at[a], other.at[a], 0, columns) for a in range(2)]
         received = read_stats(far, h, heads)
         products, stats = block_stats(causal, *rows)
-        none = no_stats(2 * frames * GROUP)
+        more = choose(first, none, received)
+        late = block_grads(*block_weights(products, stats, more), rows[0], rows[1], rows[3])
+
+        cross_products, cross_stats = block_stats(cross, sent[0], rows[1], rows[2], sent[1])
+        weights, sgrad = block_weights(cross_products, cross_stats, received)
+        near_key = dot(sgrad, sent[0], ((1,), (0,))) * SCALE
+        near_value = dot(weights, sent[1], ((1,), (0,)))
+
+        peak, inverse, delta = merged(stats, received)
+        share = received[1] * jnp.exp2(received[0] - peak) * inverse
+        shift = share * (delta - received[2] / received[1])
+        factors = jnp.concatenate(
+            [share, shift, jnp.zeros((6, share.shape[1]), jnp.float32)], axis=0
+        ).T
+        far_rows = [
+            jnp.concatenate(
+                [back[side * 2 + a, :, :, columns].reshape(-1, HEAD_DIM) for side in range(2)],
+                axis=0,
+            ).astype(jnp.float32)
+            for a in range(2)
+        ]
+        far_query = far_rows[0] * factors[:, 0:1] - far_rows[1] * factors[:, 1:2]
+        zero = jnp.zeros_like(far_query)
         late = [
-            values.reshape(2, frames, GROUP, HEAD_DIM)
-            for values in block_grads(
-                products, stats, choose(first, none, received), rows[0], rows[1], rows[3]
-            )
+            late[0] + jnp.where(first, zero, far_query),
+            late[1] + jnp.where(first, near_key, zero),
+            late[2] + jnp.where(first, near_value, zero),
         ]
-
-        def write(outs, side, near, early):
-            zero = jnp.zeros((frames, GROUP, HEAD_DIM), jnp.float32)
-            far_rows = [ref[side, :, :, columns].astype(jnp.float32) for ref in (back, back_value)]
-            near = [near[a, :, :, columns].astype(jnp.float32) for a in range(2)]
-            early = [early[a, :, :, columns].astype(jnp.float32) for a in range(3)]
-            early[1] += jnp.where(first, far_rows[0], zero)
-            early[2] += jnp.where(first, far_rows[1], zero)
-            more = (
-                jnp.where(first, zero, far_rows[0]),
-                jnp.where(first, near[0], zero),
-                jnp.where(first, near[1], zero),
-            )
+        late = [values.reshape(2, frames, GROUP, HEAD_DIM) for values in late]
+        far_rows = [
+            jnp.where(first, values, zero).reshape(2, frames, GROUP, HEAD_DIM)
+            for values in far_rows
+        ]
+
+        def write(outs, side, early):
             for a, out in enumerate(outs):
-                out[:, early_rows, columns] = early[a].astype(jnp.bfloat16)
-                out[:, late_rows, columns] = (late[a][side] + more[a]).astype(jnp.bfloat16)
-
-        write((dquery, dkey, dvalue), 0, near, early)
-        write([theirs.at[a] for a in range(3)], 1, near_other, early_other)
+                sums = early[a, :, :, columns].astype(jnp.float32)
+                if a > 0:
+                    sums += far_rows[a - 1][side]
+                out[:, early_rows, columns] = sums.astype(jnp.bfloat16)
+                out[:, late_rows, columns] = late[a][side].astype(jnp.bfloat16)
+
+        write((dquery, dkey, dvalue), 0, early)
+        write([theirs.at[a] for a in range(3)], 1, early_other)
 
 
 def finish_kernel(place, swapped, *refs):
@@ -388,7 +406,7 @@
         out[...] = swapped[a]
 
 
-STATS_STEPS, EARLY_STEPS, LATE_STEPS, FINISH_STEPS = 2, 4, 4, 4
+EARLY_STEPS, LATE_STEPS, FINISH_STEPS = 4, 4, 4
 
 
 class Temporal:
@@ -433,19 +451,7 @@
             name=name,
         )(self.place, *operands)
 
-    def late_stats(self, swapped):
-        return self.call(
-            STATS_STEPS,
-            stats_kernel,
-            "temporal_stats",
-            5,
-            [self.own(STATS_STEPS, 1)] * 4 + [self.part(STATS_STEPS, 4, GROUP, 1)],
-            self.stats(),
-            self.stats_shape(),
-            self.arrays + (swapped,),
-        )
-
-    def early_grads(self, swapped, same, other, far):
+    def early_grads(self, swapped, same, other):
         return self.call(
             EARLY_STEPS,
             early_kernel,
@@ -453,19 +459,19 @@
             EARLY_COST,
             [self.own(EARLY_STEPS, 0)] * 4
             + [self.part(EARLY_STEPS, 4, GROUP)]
-            + [self.own(EARLY_STEPS, 1)] * 2
+            + [self.own(EARLY_STEPS, 1)] * 4
             + [self.part(EARLY_STEPS, 4, GROUP, 1)]
-            + [self.part(EARLY_STEPS, 2, GROUP)] * 2
-            + [self.stats()],
-            [self.part(EARLY_STEPS, 3, GROUP)] * 2 + [self.part(EARLY_STEPS, 2, GROUP)] * 4 + [self.stats()],
-            [self.shape(3, GROUP)] * 2 + [self.shape(2, GROUP)] * 4 + [self.stats_shape()],
-            self.arrays
-            + (swapped, self.arrays[1], self.arrays[2], swapped, same, other, far),
-        )
-
-    def late_grads(self, swapped, far, *parts):
+            + [self.part(EARLY_STEPS, 2, GROUP)] * 2,
+            [self.part(EARLY_STEPS, 3, GROUP)] * 2
+            + [self.part(EARLY_STEPS, 4, GROUP), self.stats()],
+            [self.shape(3, GROUP)] * 2 + [self.shape(4, GROUP), self.stats_shape()],
+            self.arrays + (swapped,) + self.arrays + (swapped, same, other),
+        )
+
+    def late_grads(self, swapped, same, other, far, *parts):
         out = pl.BlockSpec(
-            (self.frames, self.positions, self.half // LATE_STEPS), lambda j, p: (0, 0, (p[0] % 2) * LATE_STEPS + j)
+            (self.frames, self.positions, self.half // LATE_STEPS),
+            lambda j, p: (0, 0, (p[0] % 2) * LATE_STEPS + j),
         )
         out_shape = jax.ShapeDtypeStruct((self.frames, self.positions, self.width), jnp.bfloat16)
         return self.call(
@@ -474,12 +480,14 @@
             "temporal_late",
             LATE_COST,
             [self.own(LATE_STEPS, 1)] * 4
-            + [self.part(LATE_STEPS, 4, GROUP, 1), self.stats()]
+            + [self.part(LATE_STEPS, 4, GROUP, 1)]
+            + [self.part(LATE_STEPS, 2, GROUP)] * 2
+            + [self.stats()]
             + [self.part(LATE_STEPS, 3, GROUP)] * 2
-            + [self.part(LATE_STEPS, 2, GROUP)] * 4,
+            + [self.part(LATE_STEPS, 4, GROUP)],
             [out] * 3 + [self.part(LATE_STEPS, 3, self.positions)],
             [out_shape] * 3 + [self.shape(3, self.positions)],
-            self.arrays + (swapped, far) + parts,
+            self.arrays + (swapped, same, other, far) + parts,
             LATE_PARAMS,
         )
 
@@ -526,18 +534,13 @@
 
     ships, arrays, spatial = lax.optimization_barrier((ship_pack(*arrays), arrays, spatial))
     same, other, swapped = chips(ships[0]), crossed(ships[1]), cores(ships[2])
+    packed, swapped = lax.optimization_barrier((pack_heads(*spatial), swapped))
+    packed = lax.all_to_all(packed, "space", 0, 0, tiled=True)
     work = Temporal(arrays)
-    packed, far = lax.optimization_barrier((pack_heads(*spatial), work.late_stats(swapped)))
-    far = chips(far)
-    packed = lax.all_to_all(packed, "space", 0, 0, tiled=True)
-    early, early_other, near, near_other, back, back_value, far = work.early_grads(
-        swapped, same, other, far
-    )
-    far, back, back_value = chips(far), chips(back), lax.ppermute(back_value, "tm", RETURNS)
+    early, early_other, back, far = work.early_grads(swapped, same, other)
+    far, back = chips(far), chips(back)
     packed = lax.all_to_all(spatial_grads(packed), "space", 0, 0, tiled=True)
-    *outs, theirs = work.late_grads(
-        swapped, far, early, early_other, near, near_other, back, back_value
-    )
+    *outs, theirs = work.late_grads(swapped, same, other, far, early, early_other, back)
     outs = work.finish(outs, cores(theirs))
     outs = tuple(unpack_heads(packed)) + tuple(outs)
     return tuple(out.reshape(space_query.shape) for out in outs)

time: 150 us -> 148 us (0.987)
  starting transfers between devices: 26.9 us -> 23.2 us
    ppermute x1, waiting for transfers between devices: 3.46 us -> 23.4 us  [crossed(): return lax.ppermute(array, 'tm', CROSSED)]
    all_to_all x1, waiting for transfers between devices: 38.2 us -> 24.3 us  [local(): packed = lax.all_to_all(packed, 'space', 0, 0, tiled=True)]
    all_to_all x1, waiting for transfers between devices: 25 us -> 21 us  [local(): packed = lax.all_to_all(spatial_grads(packed), 'space', 0, 0, tiled=True)]
    ppermute x4 -> x3, starting transfers between devices: 5.57 us -> 3.86 us  [chips(): return lax.ppermute(array, 'tm', CHIPS)]
    pallas_call x4 -> x3, Pallas kernels: 23.4 us -> 24.8 us  [call(): pl.pallas_call(kernel, grid_spec=pltpu.PrefetchScalarGridSpec(num_scalar_...]
  transfers between devices with their start and end apart: 10 -> 8, of which waited for: 5 -> 4; matrix products, arithmetic and copies ran while one was open for 0% -> 0% of each run, Pallas kernels for 28% -> 29%
where the time goes in v5:
time: 148 us
  waiting for transfers between devices  72.4 us (49%)
  Pallas kernels  48.5 us (33%)
  starting transfers between devices  23.2 us (16%)
  local copies, waits for them, and re-layouts  2.78 us (2%)
    pallas_call x3, Pallas kernels, call(): pl.pallas_call(kernel, grid_spec=pltpu.PrefetchScalarGridSpec(num_scalar_...  24.8 us
    all_to_all x1, waiting for transfers between devices, local(): packed = lax.all_to_all(packed, 'space', 0, 0, tiled=True)  24.3 us
    ppermute x1, waiting for transfers between devices, crossed(): return lax.ppermute(array, 'tm', CROSSED)  23.4 us
    all_to_all x1, waiting for transfers between devices, local(): packed = lax.all_to_all(spatial_grads(packed), 'space', 0, 0, tiled=True)  21 us
    pallas_call x1, Pallas kernels, spatial_grads(): pl.pallas_call(spatial_kernel, grid=(frames,), in_specs=[pl.BlockSpec((pa...  15 us
    all_to_all x1, starting transfers between devices, local(): packed = lax.all_to_all(packed, 'space', 0, 0, tiled=True)  11 us
    all_to_all x1, starting transfers between devices, local(): packed = lax.all_to_all(spatial_grads(packed), 'space', 0, 0, tiled=True)  8.07 us
    ppermute x3, starting transfers between devices, chips(): return lax.ppermute(array, 'tm', CHIPS)  3.86 us
  transfers between devices with their start and end apart: 8, of which 4 were waited for; matrix products, arithmetic and copies ran while one was open for 0% of the time, Pallas kernels for 29%

profile of v5, /device:TPU:0, one launch (start us, length us, event | category | flops | bytes accessed | tf_op | source)
XLA Modules:
  0.0 147.7 jit_solution(7337935581672183655)
XLA Ops:
  0.6 2.9 %ship_pack.1 = (bf16[2,4,16,2048]{3,2,1,0:T(8,128)(2,1)}, bf16[2,4,16,2048]{3,2,1,0:T(8,128)(2,1)}, bf16[4,4,32,2048]{3,2,1,0:T(8,128)(2,1)}) custom-call(bf16[4,32,4096]{2,1,0:T(8,128)(2,1)} %bitcast.19, bf16[4,32,4096]{2,1,0:T(8,128)(2,1)} %bitcast.23, bf16[4,32,4096]{2,1,0:T(8,128)(2,1)} %bitcast.27, bf16[4,32,4096]{2,1,0:T(8,128)(2,1)} %bitcast.31), custom_call_target="tpu_custom_call" | custom-call | flops 2000000000 | tf_op jit(solution)/shard_map/ship_pack/pallas_call | solution.py:193
  3.5 0.1 collective-permute-start
  3.6 1.8 %collective-permute-start.1 = (bf16[2,4,16,2048]{3,2,1,0:T(8,128)(2,1)}, bf16[2,4,16,2048]{3,2,1,0:T(8,128)(2,1)S(1)}, u32[]{:S(2)}, u32[]{:S(2)}) collective-permute-start(bf16[2,4,16,2048]{3,2,1,0:T(8,128)(2,1)} %get-tuple-element.53), channel_id=1, source_target_pairs={{0,64},{32,96},{64,0},{96,32},{1,65},{33,97},{65,1},{97,33},{2,66}... | collective-permute-start | bytes 1572872 | tf_op jit(solution)/shard_map/ppermute | solution.py:524
  5.4 0.1 collective-permute-start.2
  5.5 3.4 %pack_heads.1 = bf16[32,4,4,32,128]{4,3,2,1,0:T(8,128)(2,1)} custom-call(bf16[4,32,4096]{2,1,0:T(8,128)(2,1)} %bitcast.15, bf16[4,32,4096]{2,1,0:T(8,128)(2,1)} %bitcast.16, bf16[4,32,4096]{2,1,0:T(8,128)(2,1)} %bitcast.17, bf16[4,32,4096]{2,1,0:T(8,128)(2,1)} %bitcast.18), custom_call_target="tpu_custom_call" | custom-call | flops 5000000000 | tf_op jit(solution)/shard_map/pack_heads/pallas_call | solution.py:55
  8.9 0.0 collective-permute-done.swapped.late_swapped
  8.9 0.0 copy-start
  8.9 1.4 copy-done
  10.3 11.0 %all-to-all-start = ((bf16[32,4,4,32,128]{4,3,2,1,0:T(8,128)(2,1)}), bf16[32,4,4,32,128]{4,3,2,1,0:T(8,128)(2,1)}, u32[]{:S(2)}, u32[]{:S(2)}) async-start(bf16[32,4,4,32,128]{4,3,2,1,0:T(8,128)(2,1)} %pack_heads.1), calls=%async_computation | async-start | bytes 8388608 | tf_op jit(solution)/shard_map/all_to_all | solution.py:538
  21.3 0.0 collective-permute-done.1.same
  21.3 0.0 copy-start.1
  21.3 23.4 %collective-permute-done.2.other = bf16[2,4,16,2048]{3,2,1,0:T(8,128)(2,1)S(1)} collective-permute-done((bf16[2,4,16,2048]{3,2,1,0:T(8,128)(2,1)}, bf16[2,4,16,2048]{3,2,1,0:T(8,128)(2,1)S(1)}, u32[]{:S(2)}, u32[]{:S(2)}) %collective-permute-start.2) | collective-permute-done | bytes 524320 | tf_op jit(solution)/shard_map/ppermute | solution.py:527
  44.7 0.0 copy-start.2
  44.7 0.0 copy-done.1
  44.7 0.8 copy-done.2
  45.5 9.5 %temporal_early.1 = (bf16[3,4,16,2048]{3,2,1,0:T(8,128)(2,1)}, bf16[3,4,16,2048]{3,2,1,0:T(8,128)(2,1)}, bf16[4,4,16,2048]{3,2,1,0:T(8,128)(2,1)}, f32[3,16,128]{2,1,0:T(8,128)}) custom-call(s32[1]{0:T(128)} %bitcast.11.place, bf16[4,32,4096]{2,1,0:T(8,128)(2,1)} %bitcast.20, bf16[4,32,4096]{2,1,0:T(8,128)(2,1)} %bitcast.24, bf16[4,32,4096]{2,1,0:T(8,128)(2,1)} %bitcast.28, ...), custom_call_target="tpu_custom_call" | custom-call | flops 99999997952 | tf_op jit(solution)/shard_map/temporal_early/pallas_call | solution.py:442
  55.1 0.1 collective-permute-start.3
  55.2 2.0 %collective-permute-start.4 = (bf16[4,4,16,2048]{3,2,1,0:T(8,128)(2,1)}, bf16[4,4,16,2048]{3,2,1,0:T(8,128)(2,1)}, u32[]{:S(2)}, u32[]{:S(2)}) collective-permute-start(bf16[4,4,16,2048]{3,2,1,0:T(8,128)(2,1)} %get-tuple-element.58), channel_id=1, source_target_pairs={{0,64},{32,96},{64,0},{96,32},{1,65},{33,97},{65,1},{97,33},{2,66}... | collective-permute-start | bytes 3145736 | tf_op jit(solution)/shard_map/ppermute | solution.py:524
  57.2 24.3 %all-to-all-done.ref = bf16[32,4,4,32,128]{4,3,2,1,0:T(8,128)(2,1)} async-done(((bf16[32,4,4,32,128]{4,3,2,1,0:T(8,128)(2,1)}), bf16[32,4,4,32,128]{4,3,2,1,0:T(8,128)(2,1)}, u32[]{:S(2)}, u32[]{:S(2)}) %all-to-all-start) | async-done | bytes 4194336 | tf_op jit(solution)/shard_map/all_to_all | solution.py:538
  81.4 15.0 %spatial_grads.1 = bf16[32,4,3,32,128]{4,3,2,1,0:T(8,128)(2,1)} custom-call(bf16[32,4,4,32,128]{4,3,2,1,0:T(8,128)(2,1)} %all-to-all-done.ref), custom_call_target="tpu_custom_call" | custom-call | flops 20000000000 | tf_op jit(solution)/shard_map/spatial_grads/pallas_call | solution.py:118
  96.4 8.1 %all-to-all-start.1 = ((bf16[32,4,3,32,128]{4,3,2,1,0:T(8,128)(2,1)}), bf16[32,4,3,32,128]{4,3,2,1,0:T(8,128)(2,1)S(1)}, u32[]{:S(2)}, u32[]{:S(2)}) async-start(bf16[32,4,3,32,128]{4,3,2,1,0:T(8,128)(2,1)} %spatial_grads.1), calls=%async_computation.1 | async-start | bytes 6291456 | tf_op jit(solution)/shard_map/all_to_all | solution.py:542
  104.5 0.0 collective-permute-done.3.far
  104.5 0.0 copy-start.3
  104.5 0.0 collective-permute-done.4.back
  104.5 0.6 copy-done.3
  105.1 11.7 %temporal_late.1 = (bf16[4,32,4096]{2,1,0:T(8,128)(2,1)}, bf16[4,32,4096]{2,1,0:T(8,128)(2,1)}, bf16[4,32,4096]{2,1,0:T(8,128)(2,1)}, bf16[3,4,32,2048]{3,2,1,0:T(8,128)(2,1)}) custom-call(s32[1]{0:T(128)} %bitcast.11.place, bf16[4,32,4096]{2,1,0:T(8,128)(2,1)} %bitcast.22, bf16[4,32,4096]{2,1,0:T(8,128)(2,1)} %bitcast.26, bf16[4,32,4096]{2,1,0:T(8,128)(2,1)} %bitcast.30, ...), custom_call_target="tpu_custom_call" | custom-call | flops 99999997952 | tf_op jit(solution)/shard_map/temporal_late/pallas_call | solution.py:442
  116.8 0.1 collective-permute-start.5
  116.9 3.7 %collective-permute-done.5.swapped = bf16[3,4,32,2048]{3,2,1,0:T(8,128)(2,1)} collective-permute-done((bf16[3,4,32,2048]{3,2,1,0:T(8,128)(2,1)}, bf16[3,4,32,2048]{3,2,1,0:T(8,128)(2,1)}, u32[]{:S(2)}, u32[]{:S(2)}) %collective-permute-start.5) | collective-permute-done | bytes 1572896 | tf_op jit(solution)/shard_map/ppermute | solution.py:530
  120.7 3.6 %temporal_finish.1 = (bf16[4,32,4096]{2,1,0:T(8,128)(2,1)}, bf16[4,32,4096]{2,1,0:T(8,128)(2,1)}, bf16[4,32,4096]{2,1,0:T(8,128)(2,1)}) custom-call(s32[1]{0:T(128)} %bitcast.11.place, bf16[3,4,32,2048]{3,2,1,0:T(8,128)(2,1)} %collective-permute-done.5.swapped, ...), custom_call_target="tpu_custom_call", output_to_operand_aliasing={{0}: (2, {}), {1}: (3, {}), {2}: (4, {})} | custom-call | flops 3000000000 | tf_op jit(solution)/shard_map/temporal_finish/pallas_call | solution.py:442
  124.2 21.0 %all-to-all-done.1.ref = bf16[32,4,3,32,128]{4,3,2,1,0:T(8,128)(2,1)S(1)} async-done(((bf16[32,4,3,32,128]{4,3,2,1,0:T(8,128)(2,1)}), bf16[32,4,3,32,128]{4,3,2,1,0:T(8,128)(2,1)S(1)}, u32[]{:S(2)}, u32[]{:S(2)}) %all-to-all-start.1) | async-done | bytes 3145760 | tf_op jit(solution)/shard_map/all_to_all | solution.py:542
  145.2 2.5 %unpack_heads.1 = (bf16[4,32,4096]{2,1,0:T(8,128)(2,1)}, bf16[4,32,4096]{2,1,0:T(8,128)(2,1)}, bf16[4,32,4096]{2,1,0:T(8,128)(2,1)}) custom-call(bf16[32,4,3,32,128]{4,3,2,1,0:T(8,128)(2,1)S(1)} %all-to-all-done.1.ref), custom_call_target="tpu_custom_call" | custom-call | flops 4000000000 | tf_op jit(solution)/shard_map/unpack_heads/pallas_call | solution.py:82
Async XLA Ops:
  3.5 5.4 %collective-permute-start = (bf16[4,4,32,2048]{3,2,1,0:T(8,128)(2,1)}, bf16[4,4,32,2048]{3,2,1,0:T(8,128)(2,1)S(1)}, u32[]{:S(2)}, u32[]{:S(2)}) collective-permute-start(bf16[4,4,32,2048]{3,2,1,0:T(8,128)(2,1)} %get-tuple-element.43), channel_id=1, source_target_pairs={{0,32},{32,0},{64,96},{96,64},{1,33},{33,1},{65,97},{97,65},{2,34}... | collective-permute-start | bytes 6291464 | tf_op jit(solution)/shard_map/ppermute | solution.py:530
  3.6 17.7 %collective-permute-start.1 = (bf16[2,4,16,2048]{3,2,1,0:T(8,128)(2,1)}, bf16[2,4,16,2048]{3,2,1,0:T(8,128)(2,1)S(1)}, u32[]{:S(2)}, u32[]{:S(2)}) collective-permute-start(bf16[2,4,16,2048]{3,2,1,0:T(8,128)(2,1)} %get-tuple-element.53), channel_id=1, source_target_pairs={{0,64},{32,96},{64,0},{96,32},{1,65},{33,97},{65,1},{97,33},{2,66}... | collective-permute-start | bytes 1572872 | tf_op jit(solution)/shard_map/ppermute | solution.py:524
  5.4 39.3 %collective-permute-start.2 = (bf16[2,4,16,2048]{3,2,1,0:T(8,128)(2,1)}, bf16[2,4,16,2048]{3,2,1,0:T(8,128)(2,1)S(1)}, u32[]{:S(2)}, u32[]{:S(2)}) collective-permute-start(bf16[2,4,16,2048]{3,2,1,0:T(8,128)(2,1)} %get-tuple-element.54), channel_id=1, source_target_pairs={{0,96},{32,64},{64,32},{96,0},{1,97},{33,65},{65,33},{97,1},{2,98}... | collective-permute-start | bytes 1572872 | tf_op jit(solution)/shard_map/ppermute | solution.py:527
  8.9 1.4 copy-start
  10.3 71.2 %all-to-all-start = ((bf16[32,4,4,32,128]{4,3,2,1,0:T(8,128)(2,1)}), bf16[32,4,4,32,128]{4,3,2,1,0:T(8,128)(2,1)}, u32[]{:S(2)}, u32[]{:S(2)}) async-start(bf16[32,4,4,32,128]{4,3,2,1,0:T(8,128)(2,1)} %pack_heads.1), calls=%async_computation | async-start | bytes 8388608 | tf_op jit(solution)/shard_map/all_to_all | solution.py:538
  21.3 23.4 %copy-start.1 = (bf16[2,4,16,2048]{3,2,1,0:T(8,128)(2,1)}, bf16[2,4,16,2048]{3,2,1,0:T(8,128)(2,1)S(1)}, u32[]{:S(2)}) copy-start(bf16[2,4,16,2048]{3,2,1,0:T(8,128)(2,1)S(1)} %collective-permute-done.1.same) | copy-start | bytes 1572868
  44.7 0.8 copy-start.2
  55.1 49.5 %collective-permute-start.3 = (f32[3,16,128]{2,1,0:T(8,128)}, f32[3,16,128]{2,1,0:T(8,128)S(1)}, u32[]{:S(2)}, u32[]{:S(2)}) collective-permute-start(f32[3,16,128]{2,1,0:T(8,128)} %get-tuple-element.55), channel_id=1, source_target_pairs={{0,64},{32,96},{64,0},{96,32},{1,65},{33,97},{65,1},{97,33},{2,66}... | collective-permute-start | bytes 73736 | tf_op jit(solution)/shard_map/ppermute | solution.py:524
  55.2 49.4 %collective-permute-start.4 = (bf16[4,4,16,2048]{3,2,1,0:T(8,128)(2,1)}, bf16[4,4,16,2048]{3,2,1,0:T(8,128)(2,1)}, u32[]{:S(2)}, u32[]{:S(2)}) collective-permute-start(bf16[4,4,16,2048]{3,2,1,0:T(8,128)(2,1)} %get-tuple-element.58), channel_id=1, source_target_pairs={{0,64},{32,96},{64,0},{96,32},{1,65},{33,97},{65,1},{97,33},{2,66}... | collective-permute-start | bytes 3145736 | tf_op jit(solution)/shard_map/ppermute | solution.py:524
  96.4 48.8 %all-to-all-start.1 = ((bf16[32,4,3,32,128]{4,3,2,1,0:T(8,128)(2,1)}), bf16[32,4,3,32,128]{4,3,2,1,0:T(8,128)(2,1)S(1)}, u32[]{:S(2)}, u32[]{:S(2)}) async-start(bf16[32,4,3,32,128]{4,3,2,1,0:T(8,128)(2,1)} %spatial_grads.1), calls=%async_computation.1 | async-start | bytes 6291456 | tf_op jit(solution)/shard_map/all_to_all | solution.py:542
  104.5 0.6 copy-start.3
  116.8 3.8 %collective-permute-start.5 = (bf16[3,4,32,2048]{3,2,1,0:T(8,128)(2,1)}, bf16[3,4,32,2048]{3,2,1,0:T(8,128)(2,1)}, u32[]{:S(2)}, u32[]{:S(2)}) collective-permute-start(bf16[3,4,32,2048]{3,2,1,0:T(8,128)(2,1)} %get-tuple-element.59), channel_id=1, source_target_pairs={{0,32},{32,0},{64,96},{96,64},{1,33},{33,1},{65,97},{97,65},{2,34}... | collective-permute-start | bytes 4718600 | tf_op jit(solution)/shard_map/ppermute | solution.py:530

commit v6 on v5

--- a/solution.py
+++ b/solution.py
@@ -69,24 +69,32 @@
     )(*arrays)
 
 
-def unpack_kernel(ref, *outs):
-    heads = ref.shape[0]
-    for a, out in enumerate(outs):
-        for h in range(heads):
-            out[0, :, h * HEAD_DIM : (h + 1) * HEAD_DIM] = ref[h, 0, a]
+def unpack_kernel(ref, *refs):
+    *outs, rows, sems = refs
+    count, frames = rows.shape[:2]
+    copies = []
+    for f in range(frames):
+        for a in range(count):
+            for h in range(ref.shape[0]):
+                rows[a, f, :, h * HEAD_DIM : (h + 1) * HEAD_DIM] = ref[h, f, a]
+            copies.append(pltpu.make_async_copy(rows.at[a, f], outs[a].at[f], sems.at[f, a]))
+            copies[-1].start()
+    for copy in copies:
+        copy.wait()
 
 
 def unpack_heads(array):
     heads, frames, count, positions, _ = array.shape
-    width = heads * HEAD_DIM
+    shape = (frames, positions, heads * HEAD_DIM)
     return pl.pallas_call(
         unpack_kernel,
-        grid=(frames,),
-        in_specs=[
-            pl.BlockSpec((heads, 1, count, positions, HEAD_DIM), lambda f: (0, f, 0, 0, 0))
+        in_specs=[pl.BlockSpec(memory_space=pltpu.VMEM)],
+        out_specs=[pl.BlockSpec(memory_space=pltpu.HBM)] * count,
+        out_shape=[jax.ShapeDtypeStruct(shape, array.dtype)] * count,
+        scratch_shapes=[
+            pltpu.VMEM((count,) + shape, array.dtype),
+            pltpu.SemaphoreType.DMA((frames, count)),
         ],
-        out_specs=[pl.BlockSpec((1, positions, width), lambda f: (f, 0, 0))] * count,
-        out_shape=[jax.ShapeDtypeStruct((frames, positions, width), array.dtype)] * count,
         compiler_params=UNPACK_PARAMS,
         cost_estimate=cost(4),
         name="unpack_heads",

time: 148 us -> 147 us (level)
  no operation moved by 1% of the time
where the time goes in v6:
time: 147 us
  waiting for transfers between devices  72.4 us (49%)
  Pallas kernels  47.9 us (33%)
  starting transfers between devices  23.2 us (16%)
  local copies, waits for them, and re-layouts  2.78 us (2%)
    pallas_call x3, Pallas kernels, call(): pl.pallas_call(kernel, grid_spec=pltpu.PrefetchScalarGridSpec(num_scalar_...  24.8 us
    all_to_all x1, waiting for transfers between devices, local(): packed = lax.all_to_all(packed, 'space', 0, 0, tiled=True)  24.3 us
    ppermute x1, waiting for transfers between devices, crossed(): return lax.ppermute(array, 'tm', CROSSED)  23.4 us
    all_to_all x1, waiting for transfers between devices, local(): packed = lax.all_to_all(spatial_grads(packed), 'space', 0, 0, tiled=True)  21 us
    pallas_call x1, Pallas kernels, spatial_grads(): pl.pallas_call(spatial_kernel, grid=(frames,), in_specs=[pl.BlockSpec((pa...  15 us
    all_to_all x1, starting transfers between devices, local(): packed = lax.all_to_all(packed, 'space', 0, 0, tiled=True)  11 us
    all_to_all x1, starting transfers between devices, local(): packed = lax.all_to_all(spatial_grads(packed), 'space', 0, 0, tiled=True)  8.07 us
    ppermute x3, starting transfers between devices, chips(): return lax.ppermute(array, 'tm', CHIPS)  3.86 us
  transfers between devices with their start and end apart: 8, of which 4 were waited for; matrix products, arithmetic and copies ran while one was open for 0% of the time, Pallas kernels for 29%

profile of v6, /device:TPU:0, one launch (start us, length us, event | category | flops | bytes accessed | tf_op | source)
XLA Modules:
  0.0 147.0 jit_solution(11050529256062857093)
XLA Ops:
  0.6 2.9 %ship_pack.1 = (bf16[2,4,16,2048]{3,2,1,0:T(8,128)(2,1)}, bf16[2,4,16,2048]{3,2,1,0:T(8,128)(2,1)}, bf16[4,4,32,2048]{3,2,1,0:T(8,128)(2,1)}) custom-call(bf16[4,32,4096]{2,1,0:T(8,128)(2,1)} %bitcast.19, bf16[4,32,4096]{2,1,0:T(8,128)(2,1)} %bitcast.23, bf16[4,32,4096]{2,1,0:T(8,128)(2,1)} %bitcast.27, bf16[4,32,4096]{2,1,0:T(8,128)(2,1)} %bitcast.31), custom_call_target="tpu_custom_call" | custom-call | flops 2000000000 | tf_op jit(solution)/shard_map/ship_pack/pallas_call | solution.py:201
  3.5 0.1 collective-permute-start
  3.6 1.8 %collective-permute-start.1 = (bf16[2,4,16,2048]{3,2,1,0:T(8,128)(2,1)}, bf16[2,4,16,2048]{3,2,1,0:T(8,128)(2,1)S(1)}, u32[]{:S(2)}, u32[]{:S(2)}) collective-permute-start(bf16[2,4,16,2048]{3,2,1,0:T(8,128)(2,1)} %get-tuple-element.53), channel_id=1, source_target_pairs={{0,64},{32,96},{64,0},{96,32},{1,65},{33,97},{65,1},{97,33},{2,66}... | collective-permute-start | bytes 1572872 | tf_op jit(solution)/shard_map/ppermute | solution.py:532
  5.4 0.1 collective-permute-start.2
  5.5 3.4 %pack_heads.1 = bf16[32,4,4,32,128]{4,3,2,1,0:T(8,128)(2,1)} custom-call(bf16[4,32,4096]{2,1,0:T(8,128)(2,1)} %bitcast.15, bf16[4,32,4096]{2,1,0:T(8,128)(2,1)} %bitcast.16, bf16[4,32,4096]{2,1,0:T(8,128)(2,1)} %bitcast.17, bf16[4,32,4096]{2,1,0:T(8,128)(2,1)} %bitcast.18), custom_call_target="tpu_custom_call" | custom-call | flops 5000000000 | tf_op jit(solution)/shard_map/pack_heads/pallas_call | solution.py:55
  8.9 0.0 collective-permute-done.swapped.late_swapped
  8.9 0.0 copy-start
  8.9 1.4 copy-done
  10.3 11.0 %all-to-all-start = ((bf16[32,4,4,32,128]{4,3,2,1,0:T(8,128)(2,1)}), bf16[32,4,4,32,128]{4,3,2,1,0:T(8,128)(2,1)}, u32[]{:S(2)}, u32[]{:S(2)}) async-start(bf16[32,4,4,32,128]{4,3,2,1,0:T(8,128)(2,1)} %pack_heads.1), calls=%async_computation | async-start | bytes 8388608 | tf_op jit(solution)/shard_map/all_to_all | solution.py:546
  21.3 0.0 collective-permute-done.1.same
  21.3 0.0 copy-start.1
  21.3 23.4 %collective-permute-done.2.other = bf16[2,4,16,2048]{3,2,1,0:T(8,128)(2,1)S(1)} collective-permute-done((bf16[2,4,16,2048]{3,2,1,0:T(8,128)(2,1)}, bf16[2,4,16,2048]{3,2,1,0:T(8,128)(2,1)S(1)}, u32[]{:S(2)}, u32[]{:S(2)}) %collective-permute-start.2) | collective-permute-done | bytes 524320 | tf_op jit(solution)/shard_map/ppermute | solution.py:535
  44.7 0.0 copy-start.2
  44.7 0.0 copy-done.1
  44.7 0.8 copy-done.2
  45.5 9.5 %temporal_early.1 = (bf16[3,4,16,2048]{3,2,1,0:T(8,128)(2,1)}, bf16[3,4,16,2048]{3,2,1,0:T(8,128)(2,1)}, bf16[4,4,16,2048]{3,2,1,0:T(8,128)(2,1)}, f32[3,16,128]{2,1,0:T(8,128)}) custom-call(s32[1]{0:T(128)} %bitcast.11.place, bf16[4,32,4096]{2,1,0:T(8,128)(2,1)} %bitcast.20, bf16[4,32,4096]{2,1,0:T(8,128)(2,1)} %bitcast.24, bf16[4,32,4096]{2,1,0:T(8,128)(2,1)} %bitcast.28, ...), custom_call_target="tpu_custom_call" | custom-call | flops 99999997952 | tf_op jit(solution)/shard_map/temporal_early/pallas_call | solution.py:450
  55.1 0.1 collective-permute-start.3
  55.2 2.0 %collective-permute-start.4 = (bf16[4,4,16,2048]{3,2,1,0:T(8,128)(2,1)}, bf16[4,4,16,2048]{3,2,1,0:T(8,128)(2,1)}, u32[]{:S(2)}, u32[]{:S(2)}) collective-permute-start(bf16[4,4,16,2048]{3,2,1,0:T(8,128)(2,1)} %get-tuple-element.58), channel_id=1, source_target_pairs={{0,64},{32,96},{64,0},{96,32},{1,65},{33,97},{65,1},{97,33},{2,66}... | collective-permute-start | bytes 3145736 | tf_op jit(solution)/shard_map/ppermute | solution.py:532
  57.2 24.3 %all-to-all-done.ref = bf16[32,4,4,32,128]{4,3,2,1,0:T(8,128)(2,1)} async-done(((bf16[32,4,4,32,128]{4,3,2,1,0:T(8,128)(2,1)}), bf16[32,4,4,32,128]{4,3,2,1,0:T(8,128)(2,1)}, u32[]{:S(2)}, u32[]{:S(2)}) %all-to-all-start) | async-done | bytes 4194336 | tf_op jit(solution)/shard_map/all_to_all | solution.py:546
  81.4 15.0 %spatial_grads.1 = bf16[32,4,3,32,128]{4,3,2,1,0:T(8,128)(2,1)} custom-call(bf16[32,4,4,32,128]{4,3,2,1,0:T(8,128)(2,1)} %all-to-all-done.ref), custom_call_target="tpu_custom_call" | custom-call | flops 20000000000 | tf_op jit(solution)/shard_map/spatial_grads/pallas_call | solution.py:126
  96.4 8.1 %all-to-all-start.1 = ((bf16[32,4,3,32,128]{4,3,2,1,0:T(8,128)(2,1)}), bf16[32,4,3,32,128]{4,3,2,1,0:T(8,128)(2,1)S(1)}, u32[]{:S(2)}, u32[]{:S(2)}) async-start(bf16[32,4,3,32,128]{4,3,2,1,0:T(8,128)(2,1)} %spatial_grads.1), calls=%async_computation.1 | async-start | bytes 6291456 | tf_op jit(solution)/shard_map/all_to_all | solution.py:550
  104.5 0.0 collective-permute-done.3.far
  104.5 0.0 copy-start.3
  104.5 0.0 collective-permute-done.4.back
  104.5 0.6 copy-done.3
  105.1 11.7 %temporal_late.1 = (bf16[4,32,4096]{2,1,0:T(8,128)(2,1)}, bf16[4,32,4096]{2,1,0:T(8,128)(2,1)}, bf16[4,32,4096]{2,1,0:T(8,128)(2,1)}, bf16[3,4,32,2048]{3,2,1,0:T(8,128)(2,1)}) custom-call(s32[1]{0:T(128)} %bitcast.11.place, bf16[4,32,4096]{2,1,0:T(8,128)(2,1)} %bitcast.22, bf16[4,32,4096]{2,1,0:T(8,128)(2,1)} %bitcast.26, bf16[4,32,4096]{2,1,0:T(8,128)(2,1)} %bitcast.30, ...), custom_call_target="tpu_custom_call" | custom-call | flops 99999997952 | tf_op jit(solution)/shard_map/temporal_late/pallas_call | solution.py:450
  116.8 0.1 collective-permute-start.5
  116.9 3.7 %collective-permute-done.5.swapped = bf16[3,4,32,2048]{3,2,1,0:T(8,128)(2,1)} collective-permute-done((bf16[3,4,32,2048]{3,2,1,0:T(8,128)(2,1)}, bf16[3,4,32,2048]{3,2,1,0:T(8,128)(2,1)}, u32[]{:S(2)}, u32[]{:S(2)}) %collective-permute-start.5) | collective-permute-done | bytes 1572896 | tf_op jit(solution)/shard_map/ppermute | solution.py:538
  120.7 3.6 %temporal_finish.1 = (bf16[4,32,4096]{2,1,0:T(8,128)(2,1)}, bf16[4,32,4096]{2,1,0:T(8,128)(2,1)}, bf16[4,32,4096]{2,1,0:T(8,128)(2,1)}) custom-call(s32[1]{0:T(128)} %bitcast.11.place, bf16[3,4,32,2048]{3,2,1,0:T(8,128)(2,1)} %collective-permute-done.5.swapped, ...), custom_call_target="tpu_custom_call", output_to_operand_aliasing={{0}: (2, {}), {1}: (3, {}), {2}: (4, {})} | custom-call | flops 3000000000 | tf_op jit(solution)/shard_map/temporal_finish/pallas_call | solution.py:450
  124.2 21.0 %all-to-all-done.1.ref = bf16[32,4,3,32,128]{4,3,2,1,0:T(8,128)(2,1)S(1)} async-done(((bf16[32,4,3,32,128]{4,3,2,1,0:T(8,128)(2,1)}), bf16[32,4,3,32,128]{4,3,2,1,0:T(8,128)(2,1)S(1)}, u32[]{:S(2)}, u32[]{:S(2)}) %all-to-all-start.1) | async-done | bytes 3145760 | tf_op jit(solution)/shard_map/all_to_all | solution.py:550
  145.2 1.8 %unpack_heads.1 = (bf16[4,32,4096]{2,1,0:T(8,128)(2,1)}, bf16[4,32,4096]{2,1,0:T(8,128)(2,1)}, bf16[4,32,4096]{2,1,0:T(8,128)(2,1)}) custom-call(bf16[32,4,3,32,128]{4,3,2,1,0:T(8,128)(2,1)S(1)} %all-to-all-done.1.ref), custom_call_target="tpu_custom_call" | custom-call | flops 4000000000 | tf_op jit(solution)/shard_map/unpack_heads/pallas_call | solution.py:89
Async XLA Ops:
  3.5 5.4 %collective-permute-start = (bf16[4,4,32,2048]{3,2,1,0:T(8,128)(2,1)}, bf16[4,4,32,2048]{3,2,1,0:T(8,128)(2,1)S(1)}, u32[]{:S(2)}, u32[]{:S(2)}) collective-permute-start(bf16[4,4,32,2048]{3,2,1,0:T(8,128)(2,1)} %get-tuple-element.43), channel_id=1, source_target_pairs={{0,32},{32,0},{64,96},{96,64},{1,33},{33,1},{65,97},{97,65},{2,34}... | collective-permute-start | bytes 6291464 | tf_op jit(solution)/shard_map/ppermute | solution.py:538
  3.6 17.7 %collective-permute-start.1 = (bf16[2,4,16,2048]{3,2,1,0:T(8,128)(2,1)}, bf16[2,4,16,2048]{3,2,1,0:T(8,128)(2,1)S(1)}, u32[]{:S(2)}, u32[]{:S(2)}) collective-permute-start(bf16[2,4,16,2048]{3,2,1,0:T(8,128)(2,1)} %get-tuple-element.53), channel_id=1, source_target_pairs={{0,64},{32,96},{64,0},{96,32},{1,65},{33,97},{65,1},{97,33},{2,66}... | collective-permute-start | bytes 1572872 | tf_op jit(solution)/shard_map/ppermute | solution.py:532
  5.4 39.3 %collective-permute-start.2 = (bf16[2,4,16,2048]{3,2,1,0:T(8,128)(2,1)}, bf16[2,4,16,2048]{3,2,1,0:T(8,128)(2,1)S(1)}, u32[]{:S(2)}, u32[]{:S(2)}) collective-permute-start(bf16[2,4,16,2048]{3,2,1,0:T(8,128)(2,1)} %get-tuple-element.54), channel_id=1, source_target_pairs={{0,96},{32,64},{64,32},{96,0},{1,97},{33,65},{65,33},{97,1},{2,98}... | collective-permute-start | bytes 1572872 | tf_op jit(solution)/shard_map/ppermute | solution.py:535
  8.9 1.4 copy-start
  10.3 71.2 %all-to-all-start = ((bf16[32,4,4,32,128]{4,3,2,1,0:T(8,128)(2,1)}), bf16[32,4,4,32,128]{4,3,2,1,0:T(8,128)(2,1)}, u32[]{:S(2)}, u32[]{:S(2)}) async-start(bf16[32,4,4,32,128]{4,3,2,1,0:T(8,128)(2,1)} %pack_heads.1), calls=%async_computation | async-start | bytes 8388608 | tf_op jit(solution)/shard_map/all_to_all | solution.py:546
  21.3 23.4 %copy-start.1 = (bf16[2,4,16,2048]{3,2,1,0:T(8,128)(2,1)}, bf16[2,4,16,2048]{3,2,1,0:T(8,128)(2,1)S(1)}, u32[]{:S(2)}) copy-start(bf16[2,4,16,2048]{3,2,1,0:T(8,128)(2,1)S(1)} %collective-permute-done.1.same) | copy-start | bytes 1572868
  44.7 0.8 copy-start.2
  55.1 49.5 %collective-permute-start.3 = (f32[3,16,128]{2,1,0:T(8,128)}, f32[3,16,128]{2,1,0:T(8,128)S(1)}, u32[]{:S(2)}, u32[]{:S(2)}) collective-permute-start(f32[3,16,128]{2,1,0:T(8,128)} %get-tuple-element.55), channel_id=1, source_target_pairs={{0,64},{32,96},{64,0},{96,32},{1,65},{33,97},{65,1},{97,33},{2,66}... | collective-permute-start | bytes 73736 | tf_op jit(solution)/shard_map/ppermute | solution.py:532
  55.2 49.4 %collective-permute-start.4 = (bf16[4,4,16,2048]{3,2,1,0:T(8,128)(2,1)}, bf16[4,4,16,2048]{3,2,1,0:T(8,128)(2,1)}, u32[]{:S(2)}, u32[]{:S(2)}) collective-permute-start(bf16[4,4,16,2048]{3,2,1,0:T(8,128)(2,1)} %get-tuple-element.58), channel_id=1, source_target_pairs={{0,64},{32,96},{64,0},{96,32},{1,65},{33,97},{65,1},{97,33},{2,66}... | collective-permute-start | bytes 3145736 | tf_op jit(solution)/shard_map/ppermute | solution.py:532
  96.4 48.8 %all-to-all-start.1 = ((bf16[32,4,3,32,128]{4,3,2,1,0:T(8,128)(2,1)}), bf16[32,4,3,32,128]{4,3,2,1,0:T(8,128)(2,1)S(1)}, u32[]{:S(2)}, u32[]{:S(2)}) async-start(bf16[32,4,3,32,128]{4,3,2,1,0:T(8,128)(2,1)} %spatial_grads.1), calls=%async_computation.1 | async-start | bytes 6291456 | tf_op jit(solution)/shard_map/all_to_all | solution.py:550
  104.5 0.6 copy-start.3
  116.8 3.8 %collective-permute-start.5 = (bf16[3,4,32,2048]{3,2,1,0:T(8,128)(2,1)}, bf16[3,4,32,2048]{3,2,1,0:T(8,128)(2,1)}, u32[]{:S(2)}, u32[]{:S(2)}) collective-permute-start(bf16[3,4,32,2048]{3,2,1,0:T(8,128)(2,1)} %get-tuple-element.59), channel_id=1, source_target_pairs={{0,32},{32,0},{64,96},{96,64},{1,33},{33,1},{65,97},{97,65},{2,34}... | collective-permute-start | bytes 4718600 | tf_op jit(solution)/shard_map/ppermute | solution.py:538

commit v7 on v6

--- a/solution.py
+++ b/solution.py
@@ -522,6 +522,14 @@
 LATE_COST = 100
 
 
+def exchange(array):
+    members = lax.axis_size("space")
+    groups = [[t * members + (i ^ (31 * (t % 2))) for i in range(members)] for t in range(4)]
+    return lax.all_to_all(
+        array, ("tm", "space"), 0, 0, axis_index_groups=groups, tiled=True
+    )
+
+
 def local(
     space_query, space_key, space_value, space_grad, time_query, time_key, time_value, time_grad
 ):
@@ -543,11 +551,11 @@
     ships, arrays, spatial = lax.optimization_barrier((ship_pack(*arrays), arrays, spatial))
     same, other, swapped = chips(ships[0]), crossed(ships[1]), cores(ships[2])
     packed, swapped = lax.optimization_barrier((pack_heads(*spatial), swapped))
-    packed = lax.all_to_all(packed, "space", 0, 0, tiled=True)
+    packed = exchange(packed)
     work = Temporal(arrays)
     early, early_other, back, far = work.early_grads(swapped, same, other)
     far, back = chips(far), chips(back)
-    packed = lax.all_to_all(spatial_grads(packed), "space", 0, 0, tiled=True)
+    packed = exchange(spatial_grads(packed))
     *outs, theirs = work.late_grads(swapped, same, other, far, early, early_other, back)
     outs = work.finish(outs, cores(theirs))
     outs = tuple(unpack_heads(packed)) + tuple(outs)

time: 147 us -> 145 us (0.986); the launches traced: 147 us -> 143 us
  waiting for transfers between devices: 72.4 us -> 67 us
  starting transfers between devices: 23.2 us -> 24.7 us
    all_to_all x2, waiting for transfers between devices: 45.3 us -> 39.1 us  [exchange(): lax.all_to_all(array, ('tm', 'space'), 0, 0, axis_index_groups=groups, ti...]
  transfers between devices with their start and end apart: 8 -> 8, of which waited for: 4 -> 4; matrix products, arithmetic and copies ran while one was open for 0% -> 0% of each run, Pallas kernels for 29% -> 30%
where the time goes in v7:
time: 145 us; the launch traced here: 143 us
  waiting for transfers between devices  67 us (46%)
  Pallas kernels  47.8 us (33%)
  starting transfers between devices  24.7 us (17%)
  local copies, waits for them, and re-layouts  2.78 us (2%)
    all_to_all x2, waiting for transfers between devices, exchange(): lax.all_to_all(array, ('tm', 'space'), 0, 0, axis_index_groups=groups, ti...  39.1 us
    pallas_call x3, Pallas kernels, call(): pl.pallas_call(kernel, grid_spec=pltpu.PrefetchScalarGridSpec(num_scalar_...  24.8 us
    ppermute x1, waiting for transfers between devices, crossed(): return lax.ppermute(array, 'tm', CROSSED)  24.5 us
    all_to_all x2, starting transfers between devices, exchange(): lax.all_to_all(array, ('tm', 'space'), 0, 0, axis_index_groups=groups, ti...  19.7 us
    pallas_call x1, Pallas kernels, spatial_grads(): pl.pallas_call(spatial_kernel, grid=(frames,), in_specs=[pl.BlockSpec((pa...  15 us
    ppermute x3, starting transfers between devices, chips(): return lax.ppermute(array, 'tm', CHIPS)  3.86 us
    pallas_call x1, Pallas kernels, pack_heads(): pl.pallas_call(pack_kernel, in_specs=[pl.BlockSpec(memory_space=pltpu.HBM...  3.41 us
    ppermute x2, waiting for transfers between devices, cores(): return lax.ppermute(array, 'tm', CORES)  3.38 us
  transfers between devices with their start and end apart: 8, of which 4 were waited for; matrix products, arithmetic and copies ran while one was open for 0% of the time, Pallas kernels for 30%

profile of v7, /device:TPU:0, one launch (start us, length us, event | category | flops | bytes accessed | tf_op | source)
XLA Modules:
  0.0 143.1 jit_solution(12087664473532896686)
XLA Ops:
  0.6 2.9 %ship_pack.1 = (bf16[2,4,16,2048]{3,2,1,0:T(8,128)(2,1)}, bf16[2,4,16,2048]{3,2,1,0:T(8,128)(2,1)}, bf16[4,4,32,2048]{3,2,1,0:T(8,128)(2,1)}) custom-call(bf16[4,32,4096]{2,1,0:T(8,128)(2,1)} %bitcast.19, bf16[4,32,4096]{2,1,0:T(8,128)(2,1)} %bitcast.23, bf16[4,32,4096]{2,1,0:T(8,128)(2,1)} %bitcast.27, bf16[4,32,4096]{2,1,0:T(8,128)(2,1)} %bitcast.31), custom_call_target="tpu_custom_call" | custom-call | flops 2000000000 | tf_op jit(solution)/shard_map/ship_pack/pallas_call | solution.py:201
  3.5 0.1 collective-permute-start
  3.6 1.8 %collective-permute-start.1 = (bf16[2,4,16,2048]{3,2,1,0:T(8,128)(2,1)}, bf16[2,4,16,2048]{3,2,1,0:T(8,128)(2,1)S(1)}, u32[]{:S(2)}, u32[]{:S(2)}) collective-permute-start(bf16[2,4,16,2048]{3,2,1,0:T(8,128)(2,1)} %get-tuple-element.53), channel_id=1, source_target_pairs={{0,64},{32,96},{64,0},{96,32},{1,65},{33,97},{65,1},{97,33},{2,66}... | collective-permute-start | bytes 1572872 | tf_op jit(solution)/shard_map/ppermute | solution.py:540
  5.4 0.1 collective-permute-start.2
  5.5 3.4 %pack_heads.1 = bf16[32,4,4,32,128]{4,3,2,1,0:T(8,128)(2,1)} custom-call(bf16[4,32,4096]{2,1,0:T(8,128)(2,1)} %bitcast.15, bf16[4,32,4096]{2,1,0:T(8,128)(2,1)} %bitcast.16, bf16[4,32,4096]{2,1,0:T(8,128)(2,1)} %bitcast.17, bf16[4,32,4096]{2,1,0:T(8,128)(2,1)} %bitcast.18), custom_call_target="tpu_custom_call" | custom-call | flops 5000000000 | tf_op jit(solution)/shard_map/pack_heads/pallas_call | solution.py:55
  8.9 0.0 collective-permute-done.swapped.late_swapped
  8.9 0.0 copy-start
  8.9 1.4 copy-done
  10.3 11.0 %all-to-all-start = ((bf16[32,4,4,32,128]{4,3,2,1,0:T(8,128)(2,1)}), bf16[32,4,4,32,128]{4,3,2,1,0:T(8,128)(2,1)}, u32[]{:S(2)}, u32[]{:S(2)}) async-start(bf16[32,4,4,32,128]{4,3,2,1,0:T(8,128)(2,1)} %pack_heads.1), calls=%async_computation | async-start | bytes 8388608 | tf_op jit(solution)/shard_map/all_to_all | solution.py:528
  21.3 0.0 collective-permute-done.1.same
  21.3 0.0 copy-start.1
  21.3 24.5 %collective-permute-done.2.other = bf16[2,4,16,2048]{3,2,1,0:T(8,128)(2,1)S(1)} collective-permute-done((bf16[2,4,16,2048]{3,2,1,0:T(8,128)(2,1)}, bf16[2,4,16,2048]{3,2,1,0:T(8,128)(2,1)S(1)}, u32[]{:S(2)}, u32[]{:S(2)}) %collective-permute-start.2) | collective-permute-done | bytes 524320 | tf_op jit(solution)/shard_map/ppermute | solution.py:543
  45.9 0.0 copy-start.2
  45.9 0.0 copy-done.1
  45.9 0.8 copy-done.2
  46.7 9.5 %temporal_early.1 = (bf16[3,4,16,2048]{3,2,1,0:T(8,128)(2,1)}, bf16[3,4,16,2048]{3,2,1,0:T(8,128)(2,1)}, bf16[4,4,16,2048]{3,2,1,0:T(8,128)(2,1)}, f32[3,16,128]{2,1,0:T(8,128)}) custom-call(s32[1]{0:T(128)} %bitcast.11.place, bf16[4,32,4096]{2,1,0:T(8,128)(2,1)} %bitcast.20, bf16[4,32,4096]{2,1,0:T(8,128)(2,1)} %bitcast.24, bf16[4,32,4096]{2,1,0:T(8,128)(2,1)} %bitcast.28, ...), custom_call_target="tpu_custom_call" | custom-call | flops 99999997952 | tf_op jit(solution)/shard_map/temporal_early/pallas_call | solution.py:450
  56.2 0.1 collective-permute-start.3
  56.3 2.0 %collective-permute-start.4 = (bf16[4,4,16,2048]{3,2,1,0:T(8,128)(2,1)}, bf16[4,4,16,2048]{3,2,1,0:T(8,128)(2,1)}, u32[]{:S(2)}, u32[]{:S(2)}) collective-permute-start(bf16[4,4,16,2048]{3,2,1,0:T(8,128)(2,1)} %get-tuple-element.58), channel_id=1, source_target_pairs={{0,64},{32,96},{64,0},{96,32},{1,65},{33,97},{65,1},{97,33},{2,66}... | collective-permute-start | bytes 3145736 | tf_op jit(solution)/shard_map/ppermute | solution.py:540
  58.3 21.0 %all-to-all-done.ref = bf16[32,4,4,32,128]{4,3,2,1,0:T(8,128)(2,1)} async-done(((bf16[32,4,4,32,128]{4,3,2,1,0:T(8,128)(2,1)}), bf16[32,4,4,32,128]{4,3,2,1,0:T(8,128)(2,1)}, u32[]{:S(2)}, u32[]{:S(2)}) %all-to-all-start) | async-done | bytes 4194336 | tf_op jit(solution)/shard_map/all_to_all | solution.py:528
  79.3 15.0 %spatial_grads.1 = bf16[32,4,3,32,128]{4,3,2,1,0:T(8,128)(2,1)} custom-call(bf16[32,4,4,32,128]{4,3,2,1,0:T(8,128)(2,1)} %all-to-all-done.ref), custom_call_target="tpu_custom_call" | custom-call | flops 20000000000 | tf_op jit(solution)/shard_map/spatial_grads/pallas_call | solution.py:126
  94.3 8.7 %all-to-all-start.1 = ((bf16[32,4,3,32,128]{4,3,2,1,0:T(8,128)(2,1)}), bf16[32,4,3,32,128]{4,3,2,1,0:T(8,128)(2,1)S(1)}, u32[]{:S(2)}, u32[]{:S(2)}) async-start(bf16[32,4,3,32,128]{4,3,2,1,0:T(8,128)(2,1)} %spatial_grads.1), calls=%async_computation.1 | async-start | bytes 6291456 | tf_op jit(solution)/shard_map/all_to_all | solution.py:528
  103.0 0.0 collective-permute-done.3.far
  103.0 0.0 copy-start.3
  103.1 0.0 collective-permute-done.4.back
  103.1 0.6 copy-done.3
  103.7 11.7 %temporal_late.1 = (bf16[4,32,4096]{2,1,0:T(8,128)(2,1)}, bf16[4,32,4096]{2,1,0:T(8,128)(2,1)}, bf16[4,32,4096]{2,1,0:T(8,128)(2,1)}, bf16[3,4,32,2048]{3,2,1,0:T(8,128)(2,1)}) custom-call(s32[1]{0:T(128)} %bitcast.11.place, bf16[4,32,4096]{2,1,0:T(8,128)(2,1)} %bitcast.22, bf16[4,32,4096]{2,1,0:T(8,128)(2,1)} %bitcast.26, bf16[4,32,4096]{2,1,0:T(8,128)(2,1)} %bitcast.30, ...), custom_call_target="tpu_custom_call" | custom-call | flops 99999997952 | tf_op jit(solution)/shard_map/temporal_late/pallas_call | solution.py:450
  115.3 1.0 collective-permute-start.5
  116.3 3.4 %collective-permute-done.5.swapped = bf16[3,4,32,2048]{3,2,1,0:T(8,128)(2,1)} collective-permute-done((bf16[3,4,32,2048]{3,2,1,0:T(8,128)(2,1)}, bf16[3,4,32,2048]{3,2,1,0:T(8,128)(2,1)}, u32[]{:S(2)}, u32[]{:S(2)}) %collective-permute-start.5) | collective-permute-done | bytes 1572896 | tf_op jit(solution)/shard_map/ppermute | solution.py:546
  119.7 3.6 %temporal_finish.1 = (bf16[4,32,4096]{2,1,0:T(8,128)(2,1)}, bf16[4,32,4096]{2,1,0:T(8,128)(2,1)}, bf16[4,32,4096]{2,1,0:T(8,128)(2,1)}) custom-call(s32[1]{0:T(128)} %bitcast.11.place, bf16[3,4,32,2048]{3,2,1,0:T(8,128)(2,1)} %collective-permute-done.5.swapped, ...), custom_call_target="tpu_custom_call", output_to_operand_aliasing={{0}: (2, {}), {1}: (3, {}), {2}: (4, {})} | custom-call | flops 3000000000 | tf_op jit(solution)/shard_map/temporal_finish/pallas_call | solution.py:450
  123.2 18.1 %all-to-all-done.1.ref = bf16[32,4,3,32,128]{4,3,2,1,0:T(8,128)(2,1)S(1)} async-done(((bf16[32,4,3,32,128]{4,3,2,1,0:T(8,128)(2,1)}), bf16[32,4,3,32,128]{4,3,2,1,0:T(8,128)(2,1)S(1)}, u32[]{:S(2)}, u32[]{:S(2)}) %all-to-all-start.1) | async-done | bytes 3145760 | tf_op jit(solution)/shard_map/all_to_all | solution.py:528
  141.3 1.8 %unpack_heads.1 = (bf16[4,32,4096]{2,1,0:T(8,128)(2,1)}, bf16[4,32,4096]{2,1,0:T(8,128)(2,1)}, bf16[4,32,4096]{2,1,0:T(8,128)(2,1)}) custom-call(bf16[32,4,3,32,128]{4,3,2,1,0:T(8,128)(2,1)S(1)} %all-to-all-done.1.ref), custom_call_target="tpu_custom_call" | custom-call | flops 4000000000 | tf_op jit(solution)/shard_map/unpack_heads/pallas_call | solution.py:89
Async XLA Ops:
  3.5 5.4 %collective-permute-start = (bf16[4,4,32,2048]{3,2,1,0:T(8,128)(2,1)}, bf16[4,4,32,2048]{3,2,1,0:T(8,128)(2,1)S(1)}, u32[]{:S(2)}, u32[]{:S(2)}) collective-permute-start(bf16[4,4,32,2048]{3,2,1,0:T(8,128)(2,1)} %get-tuple-element.43), channel_id=1, source_target_pairs={{0,32},{32,0},{64,96},{96,64},{1,33},{33,1},{65,97},{97,65},{2,34}... | collective-permute-start | bytes 6291464 | tf_op jit(solution)/shard_map/ppermute | solution.py:546
  3.6 17.7 %collective-permute-start.1 = (bf16[2,4,16,2048]{3,2,1,0:T(8,128)(2,1)}, bf16[2,4,16,2048]{3,2,1,0:T(8,128)(2,1)S(1)}, u32[]{:S(2)}, u32[]{:S(2)}) collective-permute-start(bf16[2,4,16,2048]{3,2,1,0:T(8,128)(2,1)} %get-tuple-element.53), channel_id=1, source_target_pairs={{0,64},{32,96},{64,0},{96,32},{1,65},{33,97},{65,1},{97,33},{2,66}... | collective-permute-start | bytes 1572872 | tf_op jit(solution)/shard_map/ppermute | solution.py:540
  5.4 40.5 %collective-permute-start.2 = (bf16[2,4,16,2048]{3,2,1,0:T(8,128)(2,1)}, bf16[2,4,16,2048]{3,2,1,0:T(8,128)(2,1)S(1)}, u32[]{:S(2)}, u32[]{:S(2)}) collective-permute-start(bf16[2,4,16,2048]{3,2,1,0:T(8,128)(2,1)} %get-tuple-element.54), channel_id=1, source_target_pairs={{0,96},{32,64},{64,32},{96,0},{1,97},{33,65},{65,33},{97,1},{2,98}... | collective-permute-start | bytes 1572872 | tf_op jit(solution)/shard_map/ppermute | solution.py:543
  8.9 1.4 copy-start
  10.3 69.0 %all-to-all-start = ((bf16[32,4,4,32,128]{4,3,2,1,0:T(8,128)(2,1)}), bf16[32,4,4,32,128]{4,3,2,1,0:T(8,128)(2,1)}, u32[]{:S(2)}, u32[]{:S(2)}) async-start(bf16[32,4,4,32,128]{4,3,2,1,0:T(8,128)(2,1)} %pack_heads.1), calls=%async_computation | async-start | bytes 8388608 | tf_op jit(solution)/shard_map/all_to_all | solution.py:528
  21.3 24.6 %copy-start.1 = (bf16[2,4,16,2048]{3,2,1,0:T(8,128)(2,1)}, bf16[2,4,16,2048]{3,2,1,0:T(8,128)(2,1)S(1)}, u32[]{:S(2)}) copy-start(bf16[2,4,16,2048]{3,2,1,0:T(8,128)(2,1)S(1)} %collective-permute-done.1.same) | copy-start | bytes 1572868
  45.9 0.8 copy-start.2
  56.2 46.8 %collective-permute-start.3 = (f32[3,16,128]{2,1,0:T(8,128)}, f32[3,16,128]{2,1,0:T(8,128)S(1)}, u32[]{:S(2)}, u32[]{:S(2)}) collective-permute-start(f32[3,16,128]{2,1,0:T(8,128)} %get-tuple-element.55), channel_id=1, source_target_pairs={{0,64},{32,96},{64,0},{96,32},{1,65},{33,97},{65,1},{97,33},{2,66}... | collective-permute-start | bytes 73736 | tf_op jit(solution)/shard_map/ppermute | solution.py:540
  56.3 46.8 %collective-permute-start.4 = (bf16[4,4,16,2048]{3,2,1,0:T(8,128)(2,1)}, bf16[4,4,16,2048]{3,2,1,0:T(8,128)(2,1)}, u32[]{:S(2)}, u32[]{:S(2)}) collective-permute-start(bf16[4,4,16,2048]{3,2,1,0:T(8,128)(2,1)} %get-tuple-element.58), channel_id=1, source_target_pairs={{0,64},{32,96},{64,0},{96,32},{1,65},{33,97},{65,1},{97,33},{2,66}... | collective-permute-start | bytes 3145736 | tf_op jit(solution)/shard_map/ppermute | solution.py:540
  94.3 47.0 %all-to-all-start.1 = ((bf16[32,4,3,32,128]{4,3,2,1,0:T(8,128)(2,1)}), bf16[32,4,3,32,128]{4,3,2,1,0:T(8,128)(2,1)S(1)}, u32[]{:S(2)}, u32[]{:S(2)}) async-start(bf16[32,4,3,32,128]{4,3,2,1,0:T(8,128)(2,1)} %spatial_grads.1), calls=%async_computation.1 | async-start | bytes 6291456 | tf_op jit(solution)/shard_map/all_to_all | solution.py:528
  103.0 0.6 copy-start.3
  115.3 4.3 %collective-permute-start.5 = (bf16[3,4,32,2048]{3,2,1,0:T(8,128)(2,1)}, bf16[3,4,32,2048]{3,2,1,0:T(8,128)(2,1)}, u32[]{:S(2)}, u32[]{:S(2)}) collective-permute-start(bf16[3,4,32,2048]{3,2,1,0:T(8,128)(2,1)} %get-tuple-element.59), channel_id=1, source_target_pairs={{0,32},{32,0},{64,96},{96,64},{1,33},{33,1},{65,97},{97,65},{2,34}... | collective-permute-start | bytes 4718600 | tf_op jit(solution)/shard_map/ppermute | solution.py:546

commit v8 on v7

--- a/solution.py
+++ b/solution.py
@@ -524,7 +524,7 @@
 
 def exchange(array):
     members = lax.axis_size("space")
-    groups = [[t * members + (i ^ (31 * (t % 2))) for i in range(members)] for t in range(4)]
+    groups = [[t * members + (i ^ (31 * (t % 2)) ^ (16 * (t // 2))) for i in range(members)] for t in range(4)]
     return lax.all_to_all(
         array, ("tm", "space"), 0, 0, axis_index_groups=groups, tiled=True
     )

time: 145 us -> 145 us (level)
  no operation moved by 1% of the time
where the time goes in v8:
time: 145 us; the launch traced here: 143 us
  waiting for transfers between devices  67 us (46%)
  Pallas kernels  47.9 us (33%)
  starting transfers between devices  24.7 us (17%)
  local copies, waits for them, and re-layouts  2.78 us (2%)
    all_to_all x2, waiting for transfers between devices, exchange(): lax.all_to_all(array, ('tm', 'space'), 0, 0, axis_index_groups=groups, ti...  38.5 us
    ppermute x1, waiting for transfers between devices, crossed(): return lax.ppermute(array, 'tm', CROSSED)  25.1 us
    pallas_call x3, Pallas kernels, call(): pl.pallas_call(kernel, grid_spec=pltpu.PrefetchScalarGridSpec(num_scalar_...  24.8 us
    all_to_all x2, starting transfers between devices, exchange(): lax.all_to_all(array, ('tm', 'space'), 0, 0, axis_index_groups=groups, ti...  19.7 us
    pallas_call x1, Pallas kernels, spatial_grads(): pl.pallas_call(spatial_kernel, grid=(frames,), in_specs=[pl.BlockSpec((pa...  15 us
    ppermute x3, starting transfers between devices, chips(): return lax.ppermute(array, 'tm', CHIPS)  3.87 us
    pallas_call x1, Pallas kernels, pack_heads(): pl.pallas_call(pack_kernel, in_specs=[pl.BlockSpec(memory_space=pltpu.HBM...  3.41 us
    ppermute x2, waiting for transfers between devices, cores(): return lax.ppermute(array, 'tm', CORES)  3.38 us
  transfers between devices with their start and end apart: 8, of which 4 were waited for; matrix products, arithmetic and copies ran while one was open for 0% of the time, Pallas kernels for 30%

profile of v8, /device:TPU:0, one launch (start us, length us, event | category | flops | bytes accessed | tf_op | source)
XLA Modules:
  0.0 143.1 jit_solution(8110878879551623378)
XLA Ops:
  0.6 2.9 %ship_pack.1 = (bf16[2,4,16,2048]{3,2,1,0:T(8,128)(2,1)}, bf16[2,4,16,2048]{3,2,1,0:T(8,128)(2,1)}, bf16[4,4,32,2048]{3,2,1,0:T(8,128)(2,1)}) custom-call(bf16[4,32,4096]{2,1,0:T(8,128)(2,1)} %bitcast.19, bf16[4,32,4096]{2,1,0:T(8,128)(2,1)} %bitcast.23, bf16[4,32,4096]{2,1,0:T(8,128)(2,1)} %bitcast.27, bf16[4,32,4096]{2,1,0:T(8,128)(2,1)} %bitcast.31), custom_call_target="tpu_custom_call" | custom-call | flops 2000000000 | tf_op jit(solution)/shard_map/ship_pack/pallas_call | solution.py:201
  3.5 0.1 collective-permute-start
  3.6 1.8 %collective-permute-start.1 = (bf16[2,4,16,2048]{3,2,1,0:T(8,128)(2,1)}, bf16[2,4,16,2048]{3,2,1,0:T(8,128)(2,1)S(1)}, u32[]{:S(2)}, u32[]{:S(2)}) collective-permute-start(bf16[2,4,16,2048]{3,2,1,0:T(8,128)(2,1)} %get-tuple-element.53), channel_id=1, source_target_pairs={{0,64},{32,96},{64,0},{96,32},{1,65},{33,97},{65,1},{97,33},{2,66}... | collective-permute-start | bytes 1572872 | tf_op jit(solution)/shard_map/ppermute | solution.py:540
  5.4 0.1 collective-permute-start.2
  5.5 3.4 %pack_heads.1 = bf16[32,4,4,32,128]{4,3,2,1,0:T(8,128)(2,1)} custom-call(bf16[4,32,4096]{2,1,0:T(8,128)(2,1)} %bitcast.15, bf16[4,32,4096]{2,1,0:T(8,128)(2,1)} %bitcast.16, bf16[4,32,4096]{2,1,0:T(8,128)(2,1)} %bitcast.17, bf16[4,32,4096]{2,1,0:T(8,128)(2,1)} %bitcast.18), custom_call_target="tpu_custom_call" | custom-call | flops 5000000000 | tf_op jit(solution)/shard_map/pack_heads/pallas_call | solution.py:55
  8.9 0.0 collective-permute-done.swapped.late_swapped
  8.9 0.0 copy-start
  8.9 1.4 copy-done
  10.3 11.0 %all-to-all-start = ((bf16[32,4,4,32,128]{4,3,2,1,0:T(8,128)(2,1)}), bf16[32,4,4,32,128]{4,3,2,1,0:T(8,128)(2,1)}, u32[]{:S(2)}, u32[]{:S(2)}) async-start(bf16[32,4,4,32,128]{4,3,2,1,0:T(8,128)(2,1)} %pack_heads.1), calls=%async_computation | async-start | bytes 8388608 | tf_op jit(solution)/shard_map/all_to_all | solution.py:528
  21.3 0.0 collective-permute-done.1.same
  21.3 0.0 copy-start.1
  21.3 25.1 %collective-permute-done.2.other = bf16[2,4,16,2048]{3,2,1,0:T(8,128)(2,1)S(1)} collective-permute-done((bf16[2,4,16,2048]{3,2,1,0:T(8,128)(2,1)}, bf16[2,4,16,2048]{3,2,1,0:T(8,128)(2,1)S(1)}, u32[]{:S(2)}, u32[]{:S(2)}) %collective-permute-start.2) | collective-permute-done | bytes 524320 | tf_op jit(solution)/shard_map/ppermute | solution.py:543
  46.4 0.0 copy-start.2
  46.4 0.0 copy-done.1
  46.4 0.8 copy-done.2
  47.2 9.5 %temporal_early.1 = (bf16[3,4,16,2048]{3,2,1,0:T(8,128)(2,1)}, bf16[3,4,16,2048]{3,2,1,0:T(8,128)(2,1)}, bf16[4,4,16,2048]{3,2,1,0:T(8,128)(2,1)}, f32[3,16,128]{2,1,0:T(8,128)}) custom-call(s32[1]{0:T(128)} %bitcast.11.place, bf16[4,32,4096]{2,1,0:T(8,128)(2,1)} %bitcast.20, bf16[4,32,4096]{2,1,0:T(8,128)(2,1)} %bitcast.24, bf16[4,32,4096]{2,1,0:T(8,128)(2,1)} %bitcast.28, ...), custom_call_target="tpu_custom_call" | custom-call | flops 99999997952 | tf_op jit(solution)/shard_map/temporal_early/pallas_call | solution.py:450
  56.8 0.7 collective-permute-start.3
  57.5 1.4 collective-permute-start.4
  58.9 20.4 %all-to-all-done.ref = bf16[32,4,4,32,128]{4,3,2,1,0:T(8,128)(2,1)} async-done(((bf16[32,4,4,32,128]{4,3,2,1,0:T(8,128)(2,1)}), bf16[32,4,4,32,128]{4,3,2,1,0:T(8,128)(2,1)}, u32[]{:S(2)}, u32[]{:S(2)}) %all-to-all-start) | async-done | bytes 4194336 | tf_op jit(solution)/shard_map/all_to_all | solution.py:528
  79.3 15.0 %spatial_grads.1 = bf16[32,4,3,32,128]{4,3,2,1,0:T(8,128)(2,1)} custom-call(bf16[32,4,4,32,128]{4,3,2,1,0:T(8,128)(2,1)} %all-to-all-done.ref), custom_call_target="tpu_custom_call" | custom-call | flops 20000000000 | tf_op jit(solution)/shard_map/spatial_grads/pallas_call | solution.py:126
  94.3 8.7 %all-to-all-start.1 = ((bf16[32,4,3,32,128]{4,3,2,1,0:T(8,128)(2,1)}), bf16[32,4,3,32,128]{4,3,2,1,0:T(8,128)(2,1)S(1)}, u32[]{:S(2)}, u32[]{:S(2)}) async-start(bf16[32,4,3,32,128]{4,3,2,1,0:T(8,128)(2,1)} %spatial_grads.1), calls=%async_computation.1 | async-start | bytes 6291456 | tf_op jit(solution)/shard_map/all_to_all | solution.py:528
  103.0 0.0 collective-permute-done.3.far
  103.0 0.0 copy-start.3
  103.1 0.0 collective-permute-done.4.back
  103.1 0.6 copy-done.3
  103.7 11.7 %temporal_late.1 = (bf16[4,32,4096]{2,1,0:T(8,128)(2,1)}, bf16[4,32,4096]{2,1,0:T(8,128)(2,1)}, bf16[4,32,4096]{2,1,0:T(8,128)(2,1)}, bf16[3,4,32,2048]{3,2,1,0:T(8,128)(2,1)}) custom-call(s32[1]{0:T(128)} %bitcast.11.place, bf16[4,32,4096]{2,1,0:T(8,128)(2,1)} %bitcast.22, bf16[4,32,4096]{2,1,0:T(8,128)(2,1)} %bitcast.26, bf16[4,32,4096]{2,1,0:T(8,128)(2,1)} %bitcast.30, ...), custom_call_target="tpu_custom_call" | custom-call | flops 99999997952 | tf_op jit(solution)/shard_map/temporal_late/pallas_call | solution.py:450
  115.3 1.0 collective-permute-start.5
  116.3 3.4 %collective-permute-done.5.swapped = bf16[3,4,32,2048]{3,2,1,0:T(8,128)(2,1)} collective-permute-done((bf16[3,4,32,2048]{3,2,1,0:T(8,128)(2,1)}, bf16[3,4,32,2048]{3,2,1,0:T(8,128)(2,1)}, u32[]{:S(2)}, u32[]{:S(2)}) %collective-permute-start.5) | collective-permute-done | bytes 1572896 | tf_op jit(solution)/shard_map/ppermute | solution.py:546
  119.7 3.6 %temporal_finish.1 = (bf16[4,32,4096]{2,1,0:T(8,128)(2,1)}, bf16[4,32,4096]{2,1,0:T(8,128)(2,1)}, bf16[4,32,4096]{2,1,0:T(8,128)(2,1)}) custom-call(s32[1]{0:T(128)} %bitcast.11.place, bf16[3,4,32,2048]{3,2,1,0:T(8,128)(2,1)} %collective-permute-done.5.swapped, ...), custom_call_target="tpu_custom_call", output_to_operand_aliasing={{0}: (2, {}), {1}: (3, {}), {2}: (4, {})} | custom-call | flops 3000000000 | tf_op jit(solution)/shard_map/temporal_finish/pallas_call | solution.py:450
  123.2 18.1 %all-to-all-done.1.ref = bf16[32,4,3,32,128]{4,3,2,1,0:T(8,128)(2,1)S(1)} async-done(((bf16[32,4,3,32,128]{4,3,2,1,0:T(8,128)(2,1)}), bf16[32,4,3,32,128]{4,3,2,1,0:T(8,128)(2,1)S(1)}, u32[]{:S(2)}, u32[]{:S(2)}) %all-to-all-start.1) | async-done | bytes 3145760 | tf_op jit(solution)/shard_map/all_to_all | solution.py:528
  141.3 1.8 %unpack_heads.1 = (bf16[4,32,4096]{2,1,0:T(8,128)(2,1)}, bf16[4,32,4096]{2,1,0:T(8,128)(2,1)}, bf16[4,32,4096]{2,1,0:T(8,128)(2,1)}) custom-call(bf16[32,4,3,32,128]{4,3,2,1,0:T(8,128)(2,1)S(1)} %all-to-all-done.1.ref), custom_call_target="tpu_custom_call" | custom-call | flops 4000000000 | tf_op jit(solution)/shard_map/unpack_heads/pallas_call | solution.py:89
Async XLA Ops:
  3.5 5.4 %collective-permute-start = (bf16[4,4,32,2048]{3,2,1,0:T(8,128)(2,1)}, bf16[4,4,32,2048]{3,2,1,0:T(8,128)(2,1)S(1)}, u32[]{:S(2)}, u32[]{:S(2)}) collective-permute-start(bf16[4,4,32,2048]{3,2,1,0:T(8,128)(2,1)} %get-tuple-element.43), channel_id=1, source_target_pairs={{0,32},{32,0},{64,96},{96,64},{1,33},{33,1},{65,97},{97,65},{2,34}... | collective-permute-start | bytes 6291464 | tf_op jit(solution)/shard_map/ppermute | solution.py:546
  3.6 17.7 %collective-permute-start.1 = (bf16[2,4,16,2048]{3,2,1,0:T(8,128)(2,1)}, bf16[2,4,16,2048]{3,2,1,0:T(8,128)(2,1)S(1)}, u32[]{:S(2)}, u32[]{:S(2)}) collective-permute-start(bf16[2,4,16,2048]{3,2,1,0:T(8,128)(2,1)} %get-tuple-element.53), channel_id=1, source_target_pairs={{0,64},{32,96},{64,0},{96,32},{1,65},{33,97},{65,1},{97,33},{2,66}... | collective-permute-start | bytes 1572872 | tf_op jit(solution)/shard_map/ppermute | solution.py:540
  5.4 41.1 %collective-permute-start.2 = (bf16[2,4,16,2048]{3,2,1,0:T(8,128)(2,1)}, bf16[2,4,16,2048]{3,2,1,0:T(8,128)(2,1)S(1)}, u32[]{:S(2)}, u32[]{:S(2)}) collective-permute-start(bf16[2,4,16,2048]{3,2,1,0:T(8,128)(2,1)} %get-tuple-element.54), channel_id=1, source_target_pairs={{0,96},{32,64},{64,32},{96,0},{1,97},{33,65},{65,33},{97,1},{2,98}... | collective-permute-start | bytes 1572872 | tf_op jit(solution)/shard_map/ppermute | solution.py:543
  8.9 1.4 copy-start
  10.3 69.0 %all-to-all-start = ((bf16[32,4,4,32,128]{4,3,2,1,0:T(8,128)(2,1)}), bf16[32,4,4,32,128]{4,3,2,1,0:T(8,128)(2,1)}, u32[]{:S(2)}, u32[]{:S(2)}) async-start(bf16[32,4,4,32,128]{4,3,2,1,0:T(8,128)(2,1)} %pack_heads.1), calls=%async_computation | async-start | bytes 8388608 | tf_op jit(solution)/shard_map/all_to_all | solution.py:528
  21.3 25.1 %copy-start.1 = (bf16[2,4,16,2048]{3,2,1,0:T(8,128)(2,1)}, bf16[2,4,16,2048]{3,2,1,0:T(8,128)(2,1)S(1)}, u32[]{:S(2)}) copy-start(bf16[2,4,16,2048]{3,2,1,0:T(8,128)(2,1)S(1)} %collective-permute-done.1.same) | copy-start | bytes 1572868
  46.4 0.8 copy-start.2
  56.8 46.2 %collective-permute-start.3 = (f32[3,16,128]{2,1,0:T(8,128)}, f32[3,16,128]{2,1,0:T(8,128)S(1)}, u32[]{:S(2)}, u32[]{:S(2)}) collective-permute-start(f32[3,16,128]{2,1,0:T(8,128)} %get-tuple-element.55), channel_id=1, source_target_pairs={{0,64},{32,96},{64,0},{96,32},{1,65},{33,97},{65,1},{97,33},{2,66}... | collective-permute-start | bytes 73736 | tf_op jit(solution)/shard_map/ppermute | solution.py:540
  57.5 45.6 %collective-permute-start.4 = (bf16[4,4,16,2048]{3,2,1,0:T(8,128)(2,1)}, bf16[4,4,16,2048]{3,2,1,0:T(8,128)(2,1)}, u32[]{:S(2)}, u32[]{:S(2)}) collective-permute-start(bf16[4,4,16,2048]{3,2,1,0:T(8,128)(2,1)} %get-tuple-element.58), channel_id=1, source_target_pairs={{0,64},{32,96},{64,0},{96,32},{1,65},{33,97},{65,1},{97,33},{2,66}... | collective-permute-start | bytes 3145736 | tf_op jit(solution)/shard_map/ppermute | solution.py:540
  94.3 47.0 %all-to-all-start.1 = ((bf16[32,4,3,32,128]{4,3,2,1,0:T(8,128)(2,1)}), bf16[32,4,3,32,128]{4,3,2,1,0:T(8,128)(2,1)S(1)}, u32[]{:S(2)}, u32[]{:S(2)}) async-start(bf16[32,4,3,32,128]{4,3,2,1,0:T(8,128)(2,1)} %spatial_grads.1), calls=%async_computation.1 | async-start | bytes 6291456 | tf_op jit(solution)/shard_map/all_to_all | solution.py:528
  103.0 0.6 copy-start.3
  115.3 4.3 %collective-permute-start.5 = (bf16[3,4,32,2048]{3,2,1,0:T(8,128)(2,1)}, bf16[3,4,32,2048]{3,2,1,0:T(8,128)(2,1)}, u32[]{:S(2)}, u32[]{:S(2)}) collective-permute-start(bf16[3,4,32,2048]{3,2,1,0:T(8,128)(2,1)} %get-tuple-element.59), channel_id=1, source_target_pairs={{0,32},{32,0},{64,96},{96,64},{1,33},{33,1},{65,97},{97,65},{2,34}... | collective-permute-start | bytes 4718600 | tf_op jit(solution)/shard_map/ppermute | solution.py:546
